TPU v7x, 256 devices: a whole 4x4x8 slice. The times are simulated.
256 devices in a mesh: section: 4 (over z_lo), ty: 8 (over y, core), tx: 8 (over z_hi, x).
Axes of the slice: x: 4, y: 4, z: 8 (z_hi: 2, z_lo: 4; z = z_hi * 4 + z_lo), core: 2. Of those that a mesh axis runs over, the one named last changes fastest.
Arguments:
- acts: float32 [4, 1, 96, 64, 1024], P('section', None, None, 'ty', 'tx'), may hold values from -6 to 6
- top_grad: float32 [1, 96, 64, 1024], P(None, None, 'ty', 'tx'), may hold values from -6 to 6
- kernel: float32 [4, 49, 96], P('section'), may hold values from -0.875 to 0.875
- ln_gain: float32 [4, 96], P('section'), may hold values from 0.5 to 1.5
- ln_bias: float32 [4, 96], P('section'), may hold values from -3 to 3
- w_in: float32 [4, 96, 384], P('section'), may hold values from -0.625 to 0.625
- b_in: float32 [4, 384], P('section'), may hold values from -3 to 3
- w_out: float32 [4, 384, 96], P('section'), may hold values from -0.3125 to 0.3125
- layer_scale: float32 [4, 96], P('section'), may hold values from 0.3 to 1.5
Outputs:
- input_grad: float32 [4, 1, 96, 64, 1024], P('section', None, None, 'ty', 'tx')
- grad_kernel: float32 [4, 49, 96], P('section')
- grad_gain: float32 [4, 96], P('section')
- grad_bias: float32 [4, 96], P('section')
- grad_w_in: float32 [4, 96, 384], P('section')
- grad_b_in: float32 [4, 384], P('section')
- grad_w_out: float32 [4, 384, 96], P('section')
- grad_scale: float32 [4, 96], P('section')
All inputs are finite; a program needn't handle non-finite values.
Results may differ from a plain program's by a relative error of at most 0.0001.
Values sent between devices are 32-bit elements; how exact they have to be, the bound alone decides.
No kernel may reach another device: no remote copies, remote signals or barrier semaphores. Data moves between devices by JAX's collectives and lax.ppermute only.
A program may use at most 128 MiB of HBM per device.

v0:
```python
import jax
import jax.numpy as jnp
from jax import lax
from jax.sharding import PartitionSpec as P

KS = 7


HIGHEST = lax.Precision.HIGHEST
EPSILON = 1e-06


def with_halo(value, sides, width):
    for axis, dim in sides:
        size, length = (lax.axis_size(axis), value.shape[dim])
        up = [(i, (i + 1) % size) for i in range(size - 1)]
        down = [(j, i) for i, j in up]
        last = lax.slice_in_dim(value, length - width, length, axis=dim)
        initial = lax.slice_in_dim(value, 0, width, axis=dim)
        before = lax.ppermute(last, axis, up)
        after = lax.ppermute(initial, axis, down)
        value = jnp.concatenate([before, value, after], axis=dim)
    return value


def from_behind(block, axis, distance):
    devices = range(lax.axis_size(axis))
    route = [(i - distance, i) for i in devices if i - distance in devices]
    return lax.ppermute(block, axis, route)


def grouped_conv(padded, filters):
    channels = padded.shape[0]
    result = lax.conv_general_dilated(
        padded[None],
        filters,
        (1, 1),
        "VALID",
        dimension_numbers=("NCHW", "OIHW", "NCHW"),
        feature_group_count=channels,
        precision=HIGHEST,
    )
    return result[0]


def kernel_filters(kernel):
    channels = kernel.shape[1]
    return jnp.transpose(kernel).reshape(channels, 1, KS, KS)


def conv_forward(kernel, padded):
    return grouped_conv(padded, kernel_filters(kernel))


def conv_transpose(kernel, grad_padded):
    flipped = kernel_filters(kernel)[:, :, ::-1, ::-1]
    return grouped_conv(grad_padded, flipped)


def kernel_grad(grad_conv, padded):
    channels = grad_conv.shape[0]
    taps = grouped_conv(padded, grad_conv[:, None, :, :])
    return jnp.transpose(taps.reshape(channels, KS * KS))


def pointwise_backward(conv_field, cotan_field, weights, first_row, first_col, out_rows, out_cols):
    kernel, gain, shift_bias, weight_in, bias_in, weight_out, scale = weights
    channels = conv_field.shape[0]
    field_rows = conv_field.shape[1]
    field_cols = conv_field.shape[2]
    cells = field_rows * field_cols
    lanes = (cells + 127) // 128 * 128

    def flatten(field):
        return jnp.pad(field.reshape(channels, cells), ((0, 0), (0, lanes - cells)))

    position = jnp.arange(lanes, dtype=jnp.int32)
    row_of = position // field_cols
    col_of = position % field_cols
    inside = (
        (position < cells)
        & (row_of >= first_row)
        & (row_of < first_row + out_rows)
        & (col_of >= first_col)
        & (col_of < first_col + out_cols)
    )
    weight_mask = inside.astype(jnp.float32)[None, :]
    conv_out = flatten(conv_field)
    cotan = flatten(cotan_field)
    centre = jnp.mean(conv_out, axis=0)
    spread = jnp.mean((conv_out - centre) ** 2, axis=0)
    inv_std = lax.rsqrt(spread + EPSILON)
    normed = (conv_out - centre) * inv_std
    lifted = normed * gain[:, None] + shift_bias[:, None]
    pre_act = jnp.einsum("ch,cn->hn", weight_in, lifted, precision=HIGHEST) + bias_in[:, None]
    hidden = jax.nn.gelu(pre_act, approximate=False)
    slope = (
        0.5 * (1.0 + jax.scipy.special.erf(pre_act * 0.7071067811865476))
        + pre_act * jnp.exp(-0.5 * pre_act * pre_act) * 0.3989422804014327
    )
    branch = jnp.einsum("hc,hn->cn", weight_out, hidden, precision=HIGHEST)
    grad_branch = scale[:, None] * cotan
    grad_hidden = jnp.einsum("hc,cn->hn", weight_out, grad_branch, precision=HIGHEST)
    grad_pre = grad_hidden * slope
    grad_lifted = jnp.einsum("ch,hn->cn", weight_in, grad_pre, precision=HIGHEST)
    grad_normed = grad_lifted * gain[:, None]
    grad_conv = inv_std * (
        grad_normed
        - jnp.mean(grad_normed, axis=0)
        - normed * jnp.mean(grad_normed * normed, axis=0)
    )
    grad_pre_kept = grad_pre * weight_mask
    grad_lifted_kept = grad_lifted * weight_mask
    grad_scale = jnp.sum(cotan * branch * weight_mask, axis=1)
    grad_w_out = jnp.einsum("hn,cn->hc", hidden, grad_branch * weight_mask, precision=HIGHEST)
    grad_b_in = jnp.sum(grad_pre_kept, axis=1)
    grad_w_in = jnp.einsum("cn,hn->ch", lifted, grad_pre_kept, precision=HIGHEST)
    grad_gain = jnp.sum(grad_lifted_kept * normed, axis=1)
    grad_bias = jnp.sum(grad_lifted_kept, axis=1)
    grad_field = grad_conv[:, :cells].reshape(channels, field_rows, field_cols)
    return (grad_field, (grad_gain, grad_bias, grad_w_in, grad_b_in, grad_w_out, grad_scale))


def block_backward(field, cotan, weights):
    kernel = weights[0]
    out_rows = field.shape[1]
    out_cols = field.shape[2]
    reach = KS // 2
    padded = with_halo(field, (("ty", 1), ("tx", 2)), reach)
    conv_out = conv_forward(kernel, padded)
    grad_conv, others = pointwise_backward(conv_out, cotan, weights, 0, 0, out_rows, out_cols)
    grad_padded = with_halo(grad_conv, (("ty", 1), ("tx", 2)), reach)
    field_grad = cotan + conv_transpose(kernel, grad_padded)
    taps_grad = kernel_grad(grad_conv, padded)
    return (field_grad, (taps_grad,) + others)


def on_device(acts, top_grad, kernel, ln_gain, ln_bias, w_in, b_in, w_out, layer_scale):
    sections = lax.axis_size("section")
    section_id = lax.axis_index("section")
    weights = (kernel[0], ln_gain[0], ln_bias[0], w_in[0], b_in[0], w_out[0], layer_scale[0])
    micro_count = acts.shape[1]
    field_shape = acts.shape[2:]
    received = jnp.zeros(field_shape, jnp.float32)
    grads_out = jnp.zeros(acts.shape[1:], jnp.float32)
    totals = (jnp.zeros(kernel.shape[1:], jnp.float32),) + tuple(
        (
            jnp.zeros(array.shape[1:], jnp.float32)
            for array in (ln_gain, ln_bias, w_in, b_in, w_out, layer_scale)
        )
    )
    tick_count = micro_count + sections - 1
    for tick_index in range(tick_count):
        micro = tick_index - (sections - 1 - section_id)
        active = jnp.logical_and(micro >= 0, micro < micro_count)
        picked = jnp.clip(micro, 0, micro_count - 1)
        field = lax.dynamic_index_in_dim(acts[0], picked, 0, keepdims=False)
        top_now = lax.dynamic_index_in_dim(top_grad, picked, 0, keepdims=False)
        cotan = jnp.where(section_id == sections - 1, top_now, received)
        field_grad, param_grads = block_backward(field, cotan, weights)
        factor = active.astype(jnp.float32)
        totals = tuple((total + factor * term for total, term in zip(totals, param_grads)))
        updated = lax.dynamic_update_index_in_dim(grads_out, field_grad, picked, 0)
        grads_out = jnp.where(active, updated, grads_out)
        if tick_index + 1 < tick_count:
            received = from_behind(field_grad, "section", -1)
    totals = lax.psum(totals, ("ty", "tx"))
    return (grads_out[None],) + tuple((total[None] for total in totals))


def solution(mesh):
    placed = (
        P("section", None, None, "ty", "tx"),
        P(None, None, "ty", "tx"),
        P("section", None, None),
        P("section", None),
        P("section", None),
        P("section", None, None),
        P("section", None),
        P("section", None, None),
        P("section", None),
    )
    return jax.shard_map(
        on_device,
        mesh=mesh,
        in_specs=placed,
        out_specs=(
            P("section", None, None, "ty", "tx"),
            P("section", None, None),
            P("section", None),
            P("section", None),
            P("section", None, None),
            P("section", None),
            P("section", None, None),
            P("section", None),
        ),
        check_vma=False,
    )
```

profile of v0, /device:TPU:1, one launch (start us, length us, event | category | flops | bytes accessed | tf_op | source)
XLA Modules:
  0.0 993.3 jit_solution(3349379790452503798)
XLA Ops:
  8.6 4.6 collective-permute-start
  16.1 4.1 collective-permute-done.1
  24.7 3.2 collective-permute-done.3
  34.5 6.4 fusion.5
  48.8 3.2 collective-permute-start.4
  54.6 4.4 collective-permute-done.5
  59.0 3.1 collective-permute-start.6
  63.4 7.9 collective-permute-done.7
  80.2 9.4 collective-permute-done.8
  98.2 5.8 collective-permute-start.9
  106.6 4.4 collective-permute-done.10
  111.7 10.2 %collective-permute-start.11 = (f32[96,14,3]{0,2,1:T(4,128)}, f32[96,14,3]{0,2,1:T(4,128)}, u32[]{:S(2)}, u32[]{:S(2)}) collective-permute-start(f32[96,14,3]{0,2,1:T(4,128)} %get-tuple-element.81), channel_id=1, source_target_pairs={{0,1},{1,2},{2,3},{3,4},{4,5},{5,6},{6,7},{8,9},{9,10},{10,11},{11... | collective-permute-start | bytes 48392 | tf_op jit(solution)/shard_map/ppermute | solution.py:20
  137.4 5.3 convolution_multiply_fusion.6
  155.6 5.4 collective-permute-start.14
  168.0 7.4 collective-permute-start.16
  176.7 8.5 convolution_multiply_fusion.5
  199.0 4.5 collective-permute-done.18
  217.2 4.9 convolution_multiply_fusion.4
  222.1 8.0 fusion.99
  231.0 4.6 collective-permute-start.19
  237.6 3.5 fusion.80
  243.3 4.4 collective-permute-start.21
  249.0 380.7 %all-reduce = (f32[1,49,96]{2,0,1:T(1,128)}, f32[1,96]{1,0:T(1,128)}, f32[1,96]{1,0:T(1,128)}, f32[1,384]{1,0:T(1,128)}, f32[1,96]{1,0:T(1,128)}) all-reduce(f32[1,49,96]{2,0,1:T(1,128)S(1)} %broadcast_in_dim.43, f32[1,96]{1,0:T(1,128)S(1)} %add_bitcast_fusion.2, ...), channel_id=1, replica_groups=mesh['section'=4,'ty'=8,'tx'=8] {'ty','tx'}, use_global_device_ids=true, to_apply=%region_10.11 | all-reduce | flops 5376 | bytes 43008 | tf_op jit(solution)/shard_map/psum | solution.py:167
  636.1 346.7 %all-reduce.4.cloned.1.call-done = (f32[1,96,384]{2,1,0:T(8,128)}, f32[1,384,96]{1,2,0:T(8,128)}) async-done(((f32[1,96,384]{2,1,0:T(8,128)}, f32[1,384,96]{1,2,0:T(8,128)}), (f32[1,96,384]{2,1,0:T(8,128)}, f32[1,384,96]{1,2,0:T(8,128)})) %all-reduce.4.cloned.1.call-update) | async-done | bytes 294928 | tf_op jit(solution)/shard_map/psum | solution.py:167
  (319 shorter events, 126.6 us)
Async XLA Ops:
  7.2 975.6 %all-reduce.4.cloned.1.call-start = ((), (), s32[]{:S(2)}) async-start(), calls=%async_computation | async-start | bytes 589824 | tf_op jit(solution)/shard_map/psum | solution.py:167
  8.6 7.5 collective-permute-start
  13.2 7.0 collective-permute-start.1
  20.2 4.5 collective-permute-start.2
  23.3 4.6 collective-permute-start.3
  48.8 5.8 collective-permute-start.4
  52.0 7.0 collective-permute-start.5
  59.0 4.4 collective-permute-start.6
  62.1 9.2 collective-permute-start.7
  78.9 10.7 %collective-permute-start.8 = (f32[96,8,128]{2,1,0:T(8,128)S(1)}, f32[96,8,128]{2,1,0:T(8,128)S(1)}, u32[]{:S(2)}, u32[]{:S(2)}) collective-permute-start(f32[96,8,128]{2,1,0:T(8,128)S(1)} %bitcast_add_fusion.3), channel_id=1, source_target_pairs={{64,0},{128,64},{192,128},{65,1},{129,65},{193,129},{66,2},{130,66... | collective-permute-start | bytes 1179656 | tf_op jit(solution)/shard_map/ppermute | solution.py:29
  98.2 8.4 collective-permute-start.9
  104.0 7.0 collective-permute-start.10
  111.7 14.8 %collective-permute-start.11 = (f32[96,14,3]{0,2,1:T(4,128)}, f32[96,14,3]{0,2,1:T(4,128)}, u32[]{:S(2)}, u32[]{:S(2)}) collective-permute-start(f32[96,14,3]{0,2,1:T(4,128)} %get-tuple-element.81), channel_id=1, source_target_pairs={{0,1},{1,2},{2,3},{3,4},{4,5},{5,6},{6,7},{8,9},{9,10},{10,11},{11... | collective-permute-start | bytes 48392 | tf_op jit(solution)/shard_map/ppermute | solution.py:20
  122.0 4.9 collective-permute-start.12
  136.0 11.0 %collective-permute-start.13 = (f32[96,8,128]{2,1,0:T(8,128)S(1)}, f32[96,8,128]{2,1,0:T(8,128)S(1)}, u32[]{:S(2)}, u32[]{:S(2)}) collective-permute-start(f32[96,8,128]{2,1,0:T(8,128)S(1)} %bitcast_add_fusion.2), channel_id=1, source_target_pairs={{64,0},{128,64},{192,128},{65,1},{129,65},{193,129},{66,2},{130,66... | collective-permute-start | bytes 1179656 | tf_op jit(solution)/shard_map/ppermute | solution.py:29
  155.6 10.4 %collective-permute-start.14 = (f32[96,3,128]{0,2,1:T(8,128)S(1)}, f32[96,3,128]{0,2,1:T(8,128)S(1)}, u32[]{:S(2)}, u32[]{:S(2)}) collective-permute-start(f32[96,3,128]{0,2,1:T(8,128)S(1)} %get-tuple-element.89), channel_id=1, source_target_pairs={{0,8},{8,16},{16,24},{24,32},{32,40},{40,48},{48,56},{1,9},{9,17},... | collective-permute-start | bytes 442376 | tf_op jit(solution)/shard_map/ppermute | solution.py:20
  161.0 7.0 collective-permute-start.15
  168.0 17.2 %collective-permute-start.16 = (f32[96,14,3]{0,2,1:T(4,128)S(1)}, f32[96,14,3]{0,2,1:T(4,128)S(1)}, u32[]{:S(2)}, u32[]{:S(2)}) collective-permute-start(f32[96,14,3]{0,2,1:T(4,128)S(1)} %get-tuple-element.79), channel_id=1, source_target_pairs={{0,1},{1,2},{2,3},{3,4},{4,5},{5,6},{6,7},{8,9},{9,10},{10,11},{11... | collective-permute-start | bytes 48392 | tf_op jit(solution)/shard_map/ppermute | solution.py:20
  175.4 9.9 collective-permute-start.17
  193.6 9.8 collective-permute-start.18
  231.0 12.3 %collective-permute-start.19 = (f32[96,3,128]{0,2,1:T(8,128)}, f32[96,3,128]{0,2,1:T(8,128)S(1)}, u32[]{:S(2)}, u32[]{:S(2)}) collective-permute-start(f32[96,3,128]{0,2,1:T(8,128)} %get-tuple-element.87), channel_id=1, source_target_pairs={{0,8},{8,16},{16,24},{24,32},{32,40},{40,48},{48,56},{1,9},{9,17},... | collective-permute-start | bytes 442376 | tf_op jit(solution)/shard_map/ppermute | solution.py:20
  235.6 7.6 collective-permute-start.20
  243.3 386.5 %collective-permute-start.21 = (f32[96,14,3]{0,2,1:T(4,128)S(1)}, f32[96,14,3]{0,2,1:T(4,128)S(1)}, u32[]{:S(2)}, u32[]{:S(2)}) collective-permute-start(f32[96,14,3]{0,2,1:T(4,128)S(1)} %get-tuple-element.77), channel_id=1, source_target_pairs={{0,1},{1,2},{2,3},{3,4},{4,5},{5,6},{6,7},{8,9},{9,10},{10,11},{11... | collective-permute-start | bytes 48392 | tf_op jit(solution)/shard_map/ppermute | solution.py:20
  247.7 382.1 %collective-permute-start.22 = (f32[96,14,3]{0,2,1:T(4,128)S(1)}, f32[96,14,3]{0,2,1:T(4,128)S(1)}, u32[]{:S(2)}, u32[]{:S(2)}) collective-permute-start(f32[96,14,3]{0,2,1:T(4,128)S(1)} %get-tuple-element.78), channel_id=1, source_target_pairs={{1,0},{2,1},{3,2},{4,3},{5,4},{6,5},{7,6},{9,8},{10,9},{11,10},{12... | collective-permute-start | bytes 48392 | tf_op jit(solution)/shard_map/ppermute | solution.py:21
  (83 other events, 642.2 us)
Sparse Core Ops, SparseCore 0:
  243.2 739.5 all-reduce.3
where the time goes:
time: 1010 us; the launch traced here: 993 us
  waiting for transfers between devices  391 us (39%)
  blocking collectives  381 us (38%)
  matrix products  79 us (8%)
  starting transfers between devices  72.6 us (7%)
  local copies, waits for them, and re-layouts  37.5 us (4%)
  other arithmetic  16.7 us (2%)
  between operations  16.2 us (2%)
    psum x1, blocking collectives, on_device(): totals = lax.psum(totals, ('ty', 'tx'))  381 us
    psum x1, waiting for transfers between devices, on_device(): totals = lax.psum(totals, ('ty', 'tx'))  347 us
    ppermute x10, starting transfers between devices, with_halo(): before = lax.ppermute(last, axis, up)  51.8 us
    conv_general_dilated x9, matrix products, grouped_conv(): lax.conv_general_dilated(padded[None], filters, (1, 1), 'VALID', dimensio...  36.4 us
    ppermute x10, waiting for transfers between devices, with_halo(): after = lax.ppermute(initial, axis, down)  26.2 us
  transfers between devices with their start and end apart: 24, of which 13 were waited for; matrix products, arithmetic and copies ran while one was open for 4% of the time, Pallas kernels for 0%

commit v1 on v0

v1 whole, which is shorter than its diff:
```python
import jax
import jax.numpy as jnp
from jax import lax
from jax.experimental import pallas as pl
from jax.experimental.pallas import tpu as pltpu
from jax.sharding import PartitionSpec as P

KS = 7
TAPS = KS * KS
REACH = KS // 2
EPSILON = 1e-06
LANES = 128
GROUP = 8
ROWS = 8
C = 96
HID = 384
CELLS = ROWS * LANES
FOLD = 24
CHUNK = 256
PAYLOAD_ROWS = 1024
F32 = jnp.float32
BF16 = jnp.bfloat16
TILES = ("ty", "tx")


def call(kernel, outs, *operands, scratch=()):
    whole = pl.BlockSpec(memory_space=pltpu.VMEM)
    return pl.pallas_call(
        kernel,
        out_shape=[jax.ShapeDtypeStruct(shape, F32) for shape in outs],
        in_specs=[whole] * len(operands),
        out_specs=[whole] * len(outs),
        scratch_shapes=[pltpu.VMEM(shape, F32) for shape in scratch],
        compiler_params=pltpu.CompilerParams(vmem_limit_bytes=28 * 1024 * 1024),
    )(*operands)


def roll(value, shift):
    return pltpu.roll(value, shift % LANES, 1)


def lane_of(rows):
    return lax.broadcasted_iota(jnp.int32, (rows, LANES), 1)


def block(row):
    return pl.ds(row * LANES, LANES)


def split(value):
    high = value.astype(BF16)
    low = (value - high.astype(F32)).astype(BF16)
    return high, low


def product(left, right, dims):
    def part(one, two):
        return lax.dot_general(one, two, (dims, ((), ())), preferred_element_type=F32)

    return part(left[0], right[0]) + (part(left[0], right[1]) + part(left[1], right[0]))


ROW_COL = ((1,), (0,))
COL_COL = ((0,), (0,))
ROW_ROW = ((1,), (1,))


def pack_edges(field_ref, right_ref, left_ref):
    lane = lane_of(FOLD)
    for edge, out_ref in ((LANES - REACH, right_ref), (0, left_ref)):
        folded = jnp.zeros((FOLD, LANES), F32)
        for quarter in range(C // FOLD):
            part = pl.ds(quarter * FOLD, FOLD)
            for row in range(ROWS):
                at = 32 * quarter + REACH * row
                moved = roll(field_ref[part, block(row)], at - edge)
                folded = jnp.where((lane >= at) & (lane < at + REACH), moved, folded)
        out_ref[...] = folded


def unfold(folded_ref, wide_ref):
    for quarter in range(C // FOLD):
        wide_ref[pl.ds(quarter * FOLD, FOLD), :] = roll(folded_ref[...], -32 * quarter)


def shifted_row(row, left, right, lane, distance):
    if distance > 0:
        return roll(jnp.where(lane < distance, right, row), -distance)
    if distance < 0:
        return roll(jnp.where(lane >= LANES + distance, left, row), -distance)
    return row


def left_edge(wide, row):
    return roll(wide, LANES - REACH - REACH * row)


def right_edge(wide, row):
    return roll(wide, -REACH * row)


def tap_of(taps, tap):
    return jnp.broadcast_to(taps[:, tap : tap + 1], (GROUP, LANES))


def take_field(acts_ref, field_ref, right_ref, left_ref):
    for row in range(ROWS):
        field_ref[:, block(row)] = acts_ref[pl.ds(row, C, stride=ROWS), :]
    pack_edges(field_ref, right_ref, left_ref)


def padded_rows(group, field_ref, above_ref, below_ref, wides):
    lefts = [ref[pl.ds(group, GROUP), :] for ref in wides[0::2]]
    rights = [ref[pl.ds(group, GROUP), :] for ref in wides[1::2]]
    rows = []
    for index in range(REACH):
        value = above_ref[pl.ds(index * C + group, GROUP), :]
        rows.append((value, lefts[0], rights[0], ROWS - REACH + index))
    for index in range(ROWS):
        rows.append((field_ref[pl.ds(group, GROUP), block(index)], lefts[1], rights[1], index))
    for index in range(REACH):
        value = below_ref[pl.ds(index * C + group, GROUP), :]
        rows.append((value, lefts[2], rights[2], index))
    return [(value, left_edge(left, at), right_edge(right, at)) for value, left, right, at in rows]


EDGE_ROWS = REACH * C


def unfold_six(own_left, own_right, above_ref, below_ref, wides):
    folded = (
        above_ref.at[pl.ds(EDGE_ROWS, FOLD), :],
        above_ref.at[pl.ds(EDGE_ROWS + FOLD, FOLD), :],
        own_left,
        own_right,
        below_ref.at[pl.ds(EDGE_ROWS, FOLD), :],
        below_ref.at[pl.ds(EDGE_ROWS + FOLD, FOLD), :],
    )
    for source, wide in zip(folded, wides):
        unfold(source, wide)


def forward(
    field_ref, left_ref, right_ref, above_ref, below_ref, taps_ref,
    gain_ref, bias_ref, w_in_ref, b_in_ref,
    normed_ref, inv_ref, slope_ref, hidden_ref,
    *wides,
):
    unfold_six(left_ref, right_ref, above_ref, below_ref, wides)
    lane = lane_of(GROUP)

    def conv_group(index, carry):
        group = pl.multiple_of(index * GROUP, GROUP)
        taps = taps_ref[pl.ds(group, GROUP), :]
        rows = padded_rows(group, field_ref, above_ref, below_ref, wides)
        sums = [jnp.zeros((GROUP, LANES), F32)] * ROWS
        for b in range(KS):
            moved = [shifted_row(*row, lane, b - REACH) for row in rows]
            for a in range(KS):
                weight = tap_of(taps, a * KS + b)
                sums = [total + weight * moved[row + a] for row, total in enumerate(sums)]
        for row in range(ROWS):
            normed_ref[pl.ds(group, GROUP), block(row)] = sums[row]
        return carry

    lax.fori_loop(0, C // GROUP, conv_group, 0)
    w_in = split(w_in_ref[...])
    for start in range(0, CELLS, CHUNK):
        cells = pl.ds(start, CHUNK)
        conv_out = normed_ref[:, cells]
        centred = conv_out - jnp.mean(conv_out, axis=0, keepdims=True)
        inv = lax.rsqrt(jnp.mean(centred * centred, axis=0, keepdims=True) + EPSILON)
        normed = centred * inv
        normed_ref[:, cells] = normed
        inv_ref[:, cells] = inv
        lifted = normed * gain_ref[...] + bias_ref[...]
        pre_act = product(w_in, split(lifted), COL_COL) + b_in_ref[...]
        gate = 0.5 * (1.0 + lax.erf(pre_act * 0.7071067811865476))
        hidden_ref[:, cells] = pre_act * gate
        slope_ref[:, cells] = gate + pre_act * jnp.exp(-0.5 * pre_act * pre_act) * 0.3989422804014327


def pointwise(
    cotan_of, cotan_ref, grad_pre_ref, normed_ref, inv_ref, slope_ref,
    gain_ref, w_in_ref, w_out_ref, scale_ref, grad_ref,
):
    w_out = split(w_out_ref[...] * scale_ref[...])
    w_in = split(w_in_ref[...] * gain_ref[...])
    for start in range(0, CELLS, CHUNK):
        cells = pl.ds(start, CHUNK)
        cotan = jnp.concatenate(
            [cotan_of(row) for row in range(start // LANES, (start + CHUNK) // LANES)], axis=1
        )
        cotan_ref[:, cells] = cotan
        grad_pre = product(w_out, split(cotan), ROW_COL) * slope_ref[:, cells]
        if grad_pre_ref is not None:
            grad_pre_ref[:, cells] = grad_pre
        grad_normed = product(w_in, split(grad_pre), ROW_COL)
        normed = normed_ref[:, cells]
        mean = jnp.mean(grad_normed, axis=0, keepdims=True)
        along = jnp.mean(grad_normed * normed, axis=0, keepdims=True)
        grad_ref[:, cells] = inv_ref[:, cells] * (grad_normed - mean - normed * along)


def first_step(
    top_ref, active_ref, normed_ref, inv_ref, slope_ref, gain_ref, w_in_ref, w_out_ref, scale_ref,
    cotan_ref, grad_ref, to_right_ref, to_left_ref,
):
    def cotan_of(row):
        return top_ref[pl.ds(row, C, stride=ROWS), :] * active_ref[...]

    pointwise(
        cotan_of, cotan_ref, None, normed_ref, inv_ref, slope_ref,
        gain_ref, w_in_ref, w_out_ref, scale_ref, grad_ref,
    )
    pack_edges(grad_ref, to_right_ref, to_left_ref)


def row_sum(main_ref, above_ref, below_ref, row):
    value = main_ref[:, block(row)]
    if row < REACH:
        value = value + above_ref[:, block(row)]
    if row >= ROWS - REACH:
        value = value + below_ref[:, block(row - ROWS + REACH)]
    return value


def middle_step(
    main_ref, above_ref, below_ref, normed_ref, inv_ref, slope_ref,
    gain_ref, w_in_ref, w_out_ref, scale_ref,
    cotan_ref, grad_ref, to_right_ref, to_left_ref,
):
    def cotan_of(row):
        return row_sum(main_ref, above_ref, below_ref, row)

    pointwise(
        cotan_of, cotan_ref, None, normed_ref, inv_ref, slope_ref,
        gain_ref, w_in_ref, w_out_ref, scale_ref, grad_ref,
    )
    pack_edges(grad_ref, to_right_ref, to_left_ref)


def last_step(
    main_ref, above_ref, below_ref, cotan0_ref, cotan1_ref, cotan2_ref,
    normed_ref, inv_ref, slope_ref, gain_ref, w_in_ref, w_out_ref, scale_ref,
    cotan_ref, grad_ref, to_right_ref, to_left_ref, grad_pre_ref,
):
    def cotan_of(row):
        at = (slice(None), block(row))
        return row_sum(main_ref, above_ref, below_ref, row) + (cotan0_ref[at] + cotan1_ref[at] + cotan2_ref[at])

    pointwise(
        cotan_of, cotan_ref, grad_pre_ref, normed_ref, inv_ref, slope_ref,
        gain_ref, w_in_ref, w_out_ref, scale_ref, grad_ref,
    )
    pack_edges(grad_ref, to_right_ref, to_left_ref)


def spread(
    cotan_ref, grad_ref, left_ref, right_ref, taps_ref, main_ref, up_ref, down_ref, wide_left, wide_right
):
    unfold(left_ref, wide_left)
    unfold(right_ref, wide_right)
    lane = lane_of(GROUP)

    def conv_group(index, carry):
        group = pl.multiple_of(index * GROUP, GROUP)
        channels = pl.ds(group, GROUP)
        taps = taps_ref[channels, :]
        left, right = wide_left[channels, :], wide_right[channels, :]
        rows = [
            (grad_ref[channels, block(row)], left_edge(left, row), right_edge(right, row))
            for row in range(ROWS)
        ]
        sums = [None] * (ROWS + 2 * REACH)
        for row in range(ROWS):
            sums[row + REACH] = cotan_ref[channels, block(row)]
        for b in range(KS):
            moved = [shifted_row(*row, lane, REACH - b) for row in rows]
            for a in range(KS):
                weight = tap_of(taps, a * KS + b)
                for row in range(ROWS):
                    term = weight * moved[row]
                    old = sums[row + a]
                    sums[row + a] = term if old is None else old + term
        for row in range(REACH):
            up_ref[channels, block(row)] = sums[row]
            down_ref[channels, block(row)] = sums[ROWS + REACH + row]
        for row in range(ROWS):
            main_ref[channels, block(row)] = sums[REACH + row]
        return carry

    lax.fori_loop(0, C // GROUP, conv_group, 0)


def finish_field(main_ref, above_ref, below_ref, out_ref):
    for row in range(ROWS):
        out_ref[pl.ds(row, C, stride=ROWS), :] = row_sum(main_ref, above_ref, below_ref, row)


LIFT_ROWS = C + GROUP
OUT_AT = 0
IN_AT = OUT_AT + C * HID // LANES
TAPS_AT = IN_AT + LIFT_ROWS * HID // LANES
USED_ROWS = TAPS_AT + C


def parameter_terms(
    field_ref, left_ref, right_ref, above_ref, below_ref, grad_ref, cotan_ref, hidden_ref, normed_ref, grad_pre_ref,
    payload_ref,
    *wides,
):
    unfold_six(left_ref, right_ref, above_ref, below_ref, wides)
    lane = lane_of(GROUP)

    def taps_group(index, carry):
        group = pl.multiple_of(index * GROUP, GROUP)
        rows = padded_rows(group, field_ref, above_ref, below_ref, wides)
        grads = [grad_ref[pl.ds(group, GROUP), block(row)] for row in range(ROWS)]
        result = jnp.zeros((GROUP, LANES), F32)
        for b in range(KS):
            moved = [shifted_row(*row, lane, b - REACH) for row in rows]
            for a in range(KS):
                terms = [grads[row] * moved[row + a] for row in range(ROWS)]
                while len(terms) > 1:
                    terms = [one + two for one, two in zip(terms[0::2], terms[1::2])]
                total = jnp.sum(terms[0], axis=1, keepdims=True)
                result = jnp.where(lane == a * KS + b, total, result)
        payload_ref[pl.ds(TAPS_AT + group, GROUP), :] = result
        return carry

    lax.fori_loop(0, C // GROUP, taps_group, 0)
    grad_w_out = product(split(cotan_ref[...]), split(hidden_ref[...]), ROW_ROW)
    ones = jnp.where(lax.broadcasted_iota(jnp.int32, (GROUP, CELLS), 0) == 0, 1.0, 0.0)
    lifted = jnp.concatenate([normed_ref[...], ones], axis=0)
    grad_w_in = product(split(lifted), split(grad_pre_ref[...]), ROW_ROW)
    for part in range(HID // LANES):
        payload_ref[pl.ds(OUT_AT + part * C, C), :] = grad_w_out[:, part * LANES : (part + 1) * LANES]
        payload_ref[pl.ds(IN_AT + part * LIFT_ROWS, LIFT_ROWS), :] = grad_w_in[:, part * LANES : (part + 1) * LANES]
    payload_ref[pl.ds(USED_ROWS, PAYLOAD_ROWS - USED_ROWS), :] = jnp.zeros((PAYLOAD_ROWS - USED_ROWS, LANES), F32)


def sum_shares(shares_ref, out_ref):
    devices, rows = out_ref.shape[0], out_ref.shape[1]

    def add(device, total):
        return total + shares_ref[device]

    total = lax.fori_loop(1, devices, add, shares_ref[0], unroll=7)

    def put(device, carry):
        out_ref[device] = total
        return carry

    lax.fori_loop(0, devices, put, 0, unroll=8)


def parameter_grads(
    payload_ref, gain_ref, bias_ref, w_in_ref, w_out_ref, scale_ref,
    kernel_out, gain_out, bias_out, w_in_out, b_in_out, w_out_out, scale_out,
):
    kernel_out[...] = payload_ref[pl.ds(TAPS_AT, C), :].T[:TAPS, :]
    grad_gain = jnp.zeros((C, 1), F32)
    grad_bias = jnp.zeros((C, 1), F32)
    grad_scale = jnp.zeros((1, C), F32)
    for part in range(HID // LANES):
        hidden = pl.ds(part * LANES, LANES)
        grad_out = payload_ref[pl.ds(OUT_AT + part * C, C), :].T
        grad_scale = grad_scale + jnp.sum(grad_out * w_out_ref[hidden, :], axis=0, keepdims=True)
        w_out_out[hidden, :] = grad_out * scale_ref[...]
        at = IN_AT + part * LIFT_ROWS
        grad_in = payload_ref[pl.ds(at, C), :]
        grad_b = payload_ref[pl.ds(at + C, 1), :]
        b_in_out[:, hidden] = grad_b
        w_in_out[:, hidden] = grad_in * gain_ref[...] + bias_ref[...] * grad_b
        w_in = w_in_ref[:, hidden]
        grad_gain = grad_gain + jnp.sum(w_in * grad_in, axis=1, keepdims=True)
        grad_bias = grad_bias + jnp.sum(w_in * grad_b, axis=1, keepdims=True)
    gain_out[...] = grad_gain
    bias_out[...] = grad_bias
    scale_out[...] = grad_scale


def exchange(to_next, to_previous, axis):
    size = lax.axis_size(axis)
    up = [(i, i + 1) for i in range(size - 1)]
    down = [(i + 1, i) for i in range(size - 1)]
    return lax.ppermute(to_next, axis, up), lax.ppermute(to_previous, axis, down)


def to_previous_section(block_, step):
    sections, tiles = lax.axis_size("section"), lax.axis_size("ty")
    route = [
        (section * tiles + tile, (section - 1) * tiles + tile + step)
        for section in range(1, sections)
        for tile in range(tiles)
        if 0 <= tile + step < tiles
    ]
    return lax.ppermute(block_, ("section", "ty"), route)


def sum_over_tiles(payload):
    devices = lax.axis_size(TILES)
    rows = PAYLOAD_ROWS // devices
    shares = lax.all_to_all(payload.reshape(devices, rows, LANES), TILES, 0, 0)
    (copies,) = call(sum_shares, [(devices, rows, LANES)], shares)
    return lax.all_to_all(copies, TILES, 0, 0).reshape(PAYLOAD_ROWS, LANES)


def on_device(acts, top_grad, kernel, ln_gain, ln_bias, w_in, b_in, w_out, layer_scale):
    sections = lax.axis_size("section")
    is_last = (lax.axis_index("section") == sections - 1).astype(F32)
    active = jnp.full((1, LANES), is_last, F32)
    taps = kernel[0].T
    gain, shift_bias, scale = (ln_gain.reshape(C, 1), ln_bias.reshape(C, 1), layer_scale)
    weight_in, weight_out = (w_in[0], w_out[0])
    field_shape, edge, side, wide = ((C, CELLS), (C, REACH * LANES), (FOLD, LANES), (C, LANES))

    field, to_right, to_left = call(take_field, [field_shape, side, side], acts.reshape(C * ROWS, LANES))
    left, right = exchange(to_right, to_left, "tx")

    def edge_rows(first):
        rows = [field[:, row * LANES : (row + 1) * LANES] for row in range(first, first + REACH)]
        return jnp.concatenate(rows + [left, right], axis=0)

    above, below = exchange(edge_rows(ROWS - REACH), edge_rows(0), "ty")
    around = (field, left, right, above, below)
    normed, inv, slope, hidden = call(
        forward,
        [field_shape, (1, CELLS), (HID, CELLS), (HID, CELLS)],
        *around, taps, gain, shift_bias, weight_in, b_in.reshape(HID, 1),
        scratch=[wide] * 6,
    )
    saved = (normed, inv, slope, gain, weight_in, weight_out, scale)
    step_outs = [field_shape, field_shape, side, side]

    cotans = []
    cotan, grad, to_right, to_left = call(first_step, step_outs, top_grad.reshape(C * ROWS, LANES), active, *saved)
    for step in range(1, sections + 1):
        grad_left, grad_right = exchange(to_right, to_left, "tx")
        main, up, down = call(
            spread, [field_shape, edge, edge], cotan, grad, grad_left, grad_right, taps, scratch=[wide] * 2
        )
        if step == sections:
            break
        cotans.append(cotan)
        from_below = to_previous_section(up, -1)
        from_above = to_previous_section(down, 1)
        arrived = to_previous_section(main, 0)
        if step < sections - 1:
            cotan, grad, to_right, to_left = call(middle_step, step_outs, arrived, from_above, from_below, *saved)
        else:
            cotan, grad, to_right, to_left, grad_pre = call(
                last_step, step_outs + [(HID, CELLS)], arrived, from_above, from_below, *cotans, *saved
            )
            (payload,) = call(
                parameter_terms, [(PAYLOAD_ROWS, LANES)],
                *around, grad, cotan, hidden, normed, grad_pre, scratch=[wide] * 6,
            )
    grad_above, grad_below = exchange(down, up, "ty")
    (input_grad,) = call(finish_field, [(C * ROWS, LANES)], main, grad_above, grad_below)
    payload = sum_over_tiles(payload)
    grad_kernel, grad_gain, grad_bias, grad_w_in, grad_b_in, grad_w_out, grad_scale = call(
        parameter_grads,
        [(TAPS, C), (C, 1), (C, 1), (C, HID), (1, HID), (HID, C), (1, C)],
        payload, gain, shift_bias, weight_in, weight_out, scale,
    )
    return (
        input_grad.reshape(1, 1, C, ROWS, LANES),
        grad_kernel[None],
        grad_gain.reshape(1, C),
        grad_bias.reshape(1, C),
        grad_w_in[None],
        grad_b_in,
        grad_w_out[None],
        grad_scale,
    )


def solution(mesh):
    placed = (
        P("section", None, None, "ty", "tx"),
        P(None, None, "ty", "tx"),
        P("section", None, None),
        P("section", None),
        P("section", None),
        P("section", None, None),
        P("section", None),
        P("section", None, None),
        P("section", None),
    )
    return jax.shard_map(
        on_device,
        mesh=mesh,
        in_specs=placed,
        out_specs=(
            P("section", None, None, "ty", "tx"),
            P("section", None, None),
            P("section", None),
            P("section", None),
            P("section", None, None),
            P("section", None),
            P("section", None, None),
            P("section", None),
        ),
        check_vma=False,
    )
```

time: 1010 us -> 228 us (0.23)
  the two profiles are of different devices: /device:TPU:1 before, /device:TPU:39 now
where the time goes in v1:
time: 228 us; the launch traced here: 227 us
  waiting for transfers between devices  79.8 us (35%)
  starting transfers between devices  75.8 us (33%)
  Pallas kernels  37.7 us (17%)
  blocking collectives  24.4 us (11%)
  local copies, waits for them, and re-layouts  6.71 us (3%)
    ppermute x7, waiting for transfers between devices, exchange(): lax.ppermute(to_previous, axis, down)  42.9 us
    pallas_call x14, Pallas kernels, call(): pl.pallas_call(kernel, out_shape=[jax.ShapeDtypeStruct(shape, F32) for sh...  37.7 us
    ppermute x9, waiting for transfers between devices, to_previous_section(): return lax.ppermute(block_, ('section', 'ty'), route)  36.7 us
    ppermute x7, starting transfers between devices, exchange(): lax.ppermute(to_next, axis, up)  28.6 us
    all_to_all x1, blocking collectives, sum_over_tiles(): shares = lax.all_to_all(payload.reshape(devices, rows, LANES), TILES, 0, 0)  24.4 us
    ppermute x9, starting transfers between devices, to_previous_section(): return lax.ppermute(block_, ('section', 'ty'), route)  20.6 us
    ppermute x7, starting transfers between devices, exchange(): lax.ppermute(to_previous, axis, down)  19.8 us
    all_to_all x1, starting transfers between devices, sum_over_tiles(): return lax.all_to_all(copies, TILES, 0, 0).reshape(PAYLOAD_ROWS, LANES)  6.78 us
  transfers between devices with their start and end apart: 24, of which 13 were waited for; matrix products, arithmetic and copies ran while one was open for 2% of the time, Pallas kernels for 2%

profile of v1, /device:TPU:39, one launch (start us, length us, event | category | flops | bytes accessed | tf_op | source)
XLA Modules:
  0.0 226.7 jit_solution(13338105985371915749)
XLA Ops:
  2.0 7.8 %collective-permute-start = (f32[24,128]{1,0:T(8,128)S(1)}, f32[24,128]{1,0:T(8,128)S(1)}, u32[]{:S(2)}, u32[]{:S(2)}) collective-permute-start(f32[24,128]{1,0:T(8,128)S(1)} %get-tuple-element.52), channel_id=1, source_target_pairs={{0,1},{1,2},{2,3},{3,4},{4,5},{5,6},{6,7},{8,9},{9,10},{10,11},{11... | collective-permute-start | bytes 36872 | tf_op jit(solution)/shard_map/ppermute | solution.py:388
  11.8 8.5 %collective-permute-done.1.right_ref = f32[24,128]{1,0:T(8,128)S(1)} collective-permute-done((f32[24,128]{1,0:T(8,128)S(1)}, f32[24,128]{1,0:T(8,128)S(1)}, u32[]{:S(2)}, u32[]{:S(2)}) %collective-permute-start.1) | collective-permute-done | bytes 12320 | tf_op jit(solution)/shard_map/ppermute | solution.py:388
  20.3 4.0 %collective-permute-start.3 = (f32[336,128]{1,0:T(8,128)S(1)}, f32[336,128]{1,0:T(8,128)S(1)}, u32[]{:S(2)}, u32[]{:S(2)}) collective-permute-start(f32[336,128]{1,0:T(8,128)S(1)} %get-tuple-element.116), channel_id=1, source_target_pairs={{8,0},{16,8},{24,16},{32,24},{40,32},{48,40},{56,48},{9,1},{17,9},... | collective-permute-start | bytes 516104 | tf_op jit(solution)/shard_map/ppermute | solution.py:388
  31.7 5.1 %shard_map.153 = (f32[96,1024]{1,0:T(8,128)S(1)}, f32[1,1024]{1,0:T(1,128)S(1)}, f32[384,1024]{1,0:T(8,128)S(1)}, f32[384,1024]{1,0:T(8,128)S(1)}) custom-call(f32[96,1024]{1,0:T(8,128)S(1)} %get-tuple-element.51.field_ref, f32[24,128]{1,0:T(8,128)S(1)} %collective-permute-done.left_ref, f32[24,128]{1,0:T(8,128)S(1)} %collective-permute-done.1.right_ref, ...), custom_call_target="tpu_custom_call" | custom-call | tf_op jit(solution)/shard_map/pallas_call | solution.py:28
  41.3 3.4 %collective-permute-start.5 = (f32[24,128]{1,0:T(8,128)S(1)}, f32[24,128]{1,0:T(8,128)S(1)}, u32[]{:S(2)}, u32[]{:S(2)}) collective-permute-start(f32[24,128]{1,0:T(8,128)S(1)} %get-tuple-element.60), channel_id=1, source_target_pairs={{1,0},{2,1},{3,2},{4,3},{5,4},{6,5},{7,6},{9,8},{10,9},{11,10},{12... | collective-permute-start | bytes 36872 | tf_op jit(solution)/shard_map/ppermute | solution.py:388
  44.7 7.1 %collective-permute-done.5.right_ref = f32[24,128]{1,0:T(8,128)S(1)} collective-permute-done((f32[24,128]{1,0:T(8,128)S(1)}, f32[24,128]{1,0:T(8,128)S(1)}, u32[]{:S(2)}, u32[]{:S(2)}) %collective-permute-start.5) | collective-permute-done | bytes 12320 | tf_op jit(solution)/shard_map/ppermute | solution.py:388
  51.9 3.2 %shard_map.155 = (f32[96,1024]{1,0:T(8,128)S(1)}, f32[96,384]{1,0:T(8,128)S(1)}, f32[96,384]{1,0:T(8,128)S(1)}) custom-call(f32[96,1024]{1,0:T(8,128)S(1)} %get-tuple-element.57.cotan_ref.cotan0_ref, f32[96,1024]{1,0:T(8,128)S(1)} %get-tuple-element.58.grad_ref, f32[24,128]{1,0:T(8,128)S(1)} %collective-permute-done.4.left_ref, ...), custom_call_target="tpu_custom_call" | custom-call | tf_op jit(solution)/shard_map/pallas_call | solution.py:28
  62.3 9.9 %collective-permute-done.7.above_ref = f32[96,384]{1,0:T(8,128)S(1)} collective-permute-done((f32[96,384]{1,0:T(8,128)S(1)}, f32[96,384]{1,0:T(8,128)S(1)}, u32[]{:S(2)}, u32[]{:S(2)}) %collective-permute-start.7) | collective-permute-done | bytes 147488 | tf_op jit(solution)/shard_map/ppermute | solution.py:399
  79.7 3.4 %collective-permute-start.10 = (f32[24,128]{1,0:T(8,128)S(1)}, f32[24,128]{1,0:T(8,128)S(1)}, u32[]{:S(2)}, u32[]{:S(2)}) collective-permute-start(f32[24,128]{1,0:T(8,128)S(1)} %get-tuple-element.67), channel_id=1, source_target_pairs={{1,0},{2,1},{3,2},{4,3},{5,4},{6,5},{7,6},{9,8},{10,9},{11,10},{12... | collective-permute-start | bytes 36872 | tf_op jit(solution)/shard_map/ppermute | solution.py:388
  83.1 7.2 %collective-permute-done.10.right_ref = f32[24,128]{1,0:T(8,128)S(1)} collective-permute-done((f32[24,128]{1,0:T(8,128)S(1)}, f32[24,128]{1,0:T(8,128)S(1)}, u32[]{:S(2)}, u32[]{:S(2)}) %collective-permute-start.10) | collective-permute-done | bytes 12320 | tf_op jit(solution)/shard_map/ppermute | solution.py:388
  90.2 3.2 %shard_map.157 = (f32[96,1024]{1,0:T(8,128)S(1)}, f32[96,384]{1,0:T(8,128)S(1)}, f32[96,384]{1,0:T(8,128)S(1)}) custom-call(f32[96,1024]{1,0:T(8,128)S(1)} %get-tuple-element.64.cotan_ref.cotan1_ref, f32[96,1024]{1,0:T(8,128)S(1)} %get-tuple-element.65.grad_ref, f32[24,128]{1,0:T(8,128)S(1)} %collective-permute-done.9.left_ref, ...), custom_call_target="tpu_custom_call" | custom-call | tf_op jit(solution)/shard_map/pallas_call | solution.py:28
  100.1 8.6 %collective-permute-done.12.above_ref = f32[96,384]{1,0:T(8,128)S(1)} collective-permute-done((f32[96,384]{1,0:T(8,128)S(1)}, f32[96,384]{1,0:T(8,128)S(1)}, u32[]{:S(2)}, u32[]{:S(2)}) %collective-permute-start.12) | collective-permute-done | bytes 147488 | tf_op jit(solution)/shard_map/ppermute | solution.py:399
  108.7 4.4 %collective-permute-done.13.below_ref = f32[96,384]{1,0:T(8,128)S(1)} collective-permute-done((f32[96,384]{1,0:T(8,128)S(1)}, f32[96,384]{1,0:T(8,128)S(1)}, u32[]{:S(2)}, u32[]{:S(2)}) %collective-permute-start.13) | collective-permute-done | bytes 147488 | tf_op jit(solution)/shard_map/ppermute | solution.py:399
  117.6 3.4 %collective-permute-start.15 = (f32[24,128]{1,0:T(8,128)S(1)}, f32[24,128]{1,0:T(8,128)S(1)}, u32[]{:S(2)}, u32[]{:S(2)}) collective-permute-start(f32[24,128]{1,0:T(8,128)S(1)} %get-tuple-element.74), channel_id=1, source_target_pairs={{1,0},{2,1},{3,2},{4,3},{5,4},{6,5},{7,6},{9,8},{10,9},{11,10},{12... | collective-permute-start | bytes 36872 | tf_op jit(solution)/shard_map/ppermute | solution.py:388
  121.0 7.2 %collective-permute-done.15.right_ref = f32[24,128]{1,0:T(8,128)S(1)} collective-permute-done((f32[24,128]{1,0:T(8,128)S(1)}, f32[24,128]{1,0:T(8,128)S(1)}, u32[]{:S(2)}, u32[]{:S(2)}) %collective-permute-start.15) | collective-permute-done | bytes 12320 | tf_op jit(solution)/shard_map/ppermute | solution.py:388
  128.2 3.2 %shard_map.159 = (f32[96,1024]{1,0:T(8,128)S(1)}, f32[96,384]{1,0:T(8,128)S(1)}, f32[96,384]{1,0:T(8,128)S(1)}) custom-call(f32[96,1024]{1,0:T(8,128)S(1)} %get-tuple-element.71.cotan_ref.cotan2_ref, f32[96,1024]{1,0:T(8,128)S(1)} %get-tuple-element.72.grad_ref, f32[24,128]{1,0:T(8,128)S(1)} %collective-permute-done.14.left_ref, ...), custom_call_target="tpu_custom_call" | custom-call | tf_op jit(solution)/shard_map/pallas_call | solution.py:28
  138.1 8.6 %collective-permute-done.17.above_ref = f32[96,384]{1,0:T(8,128)S(1)} collective-permute-done((f32[96,384]{1,0:T(8,128)S(1)}, f32[96,384]{1,0:T(8,128)S(1)}, u32[]{:S(2)}, u32[]{:S(2)}) %collective-permute-start.17) | collective-permute-done | bytes 147488 | tf_op jit(solution)/shard_map/ppermute | solution.py:399
  151.6 6.6 %shard_map.163 = f32[1024,128]{1,0:T(8,128)S(1)} custom-call(f32[96,1024]{1,0:T(8,128)S(1)} %get-tuple-element.51.field_ref, f32[24,128]{1,0:T(8,128)S(1)} %collective-permute-done.left_ref, f32[24,128]{1,0:T(8,128)S(1)} %collective-permute-done.1.right_ref, f32[336,128]{1,0:T(8,128)S(1)} %collective-permute-done.2.above_ref, ...), custom_call_target="tpu_custom_call" | custom-call | tf_op jit(solution)/shard_map/pallas_call | solution.py:28
  158.1 24.4 %all_to_all.10.shares_ref = f32[64,16,128]{2,1,0:T(8,128)S(1)} all-to-all(f32[64,16,128]{2,1,0:T(8,128)S(1)} %bitcast.30), channel_id=1, replica_groups=mesh['section'=4,'ty'=8,'tx'=8] {'ty','tx'}, dimensions={0} | all-to-all | bytes 1048576 | tf_op jit(solution)/shard_map/all_to_all | solution.py:405
  183.4 6.8 %all-to-all-start.1 = ((f32[64,16,128]{2,1,0:T(8,128)}), f32[64,16,128]{2,1,0:T(8,128)S(1)}, u32[]{:S(2)}, u32[]{:S(2)}) async-start(f32[64,16,128]{2,1,0:T(8,128)} %shard_map.164), calls=%async_computation.1 | async-start | bytes 1048576 | tf_op jit(solution)/shard_map/all_to_all | solution.py:407
  190.2 7.0 %collective-permute-start.19 = (f32[24,128]{1,0:T(8,128)S(1)}, f32[24,128]{1,0:T(8,128)S(1)}, u32[]{:S(2)}, u32[]{:S(2)}) collective-permute-start(f32[24,128]{1,0:T(8,128)S(1)} %get-tuple-element.80), channel_id=1, source_target_pairs={{0,1},{1,2},{2,3},{3,4},{4,5},{5,6},{6,7},{8,9},{9,10},{10,11},{11... | collective-permute-start | bytes 36872 | tf_op jit(solution)/shard_map/ppermute | solution.py:388
  199.2 8.5 %collective-permute-done.20.right_ref = f32[24,128]{1,0:T(8,128)S(1)} collective-permute-done((f32[24,128]{1,0:T(8,128)S(1)}, f32[24,128]{1,0:T(8,128)S(1)}, u32[]{:S(2)}, u32[]{:S(2)}) %collective-permute-start.20) | collective-permute-done | bytes 12320 | tf_op jit(solution)/shard_map/ppermute | solution.py:388
  210.9 4.9 %collective-permute-start.21 = (f32[96,384]{1,0:T(8,128)S(1)}, f32[96,384]{1,0:T(8,128)S(1)}, u32[]{:S(2)}, u32[]{:S(2)}) collective-permute-start(f32[96,384]{1,0:T(8,128)S(1)} %get-tuple-element.83), channel_id=1, source_target_pairs={{0,8},{8,16},{16,24},{24,32},{32,40},{40,48},{48,56},{1,9},{9,17},... | collective-permute-start | bytes 442376 | tf_op jit(solution)/shard_map/ppermute | solution.py:388
  217.8 4.4 %collective-permute-done.22.below_ref = f32[96,384]{1,0:T(8,128)S(1)} collective-permute-done((f32[96,384]{1,0:T(8,128)S(1)}, f32[96,384]{1,0:T(8,128)S(1)}, u32[]{:S(2)}, u32[]{:S(2)}) %collective-permute-start.22) | collective-permute-done | bytes 147488 | tf_op jit(solution)/shard_map/ppermute | solution.py:388
  (62 shorter events, 65.0 us)
Async XLA Ops:
  2.0 9.8 %collective-permute-start = (f32[24,128]{1,0:T(8,128)S(1)}, f32[24,128]{1,0:T(8,128)S(1)}, u32[]{:S(2)}, u32[]{:S(2)}) collective-permute-start(f32[24,128]{1,0:T(8,128)S(1)} %get-tuple-element.52), channel_id=1, source_target_pairs={{0,1},{1,2},{2,3},{3,4},{4,5},{5,6},{6,7},{8,9},{9,10},{10,11},{11... | collective-permute-start | bytes 36872 | tf_op jit(solution)/shard_map/ppermute | solution.py:388
  9.8 10.5 %collective-permute-start.1 = (f32[24,128]{1,0:T(8,128)S(1)}, f32[24,128]{1,0:T(8,128)S(1)}, u32[]{:S(2)}, u32[]{:S(2)}) collective-permute-start(f32[24,128]{1,0:T(8,128)S(1)} %get-tuple-element.53), channel_id=1, source_target_pairs={{1,0},{2,1},{3,2},{4,3},{5,4},{6,5},{7,6},{9,8},{10,9},{11,10},{12... | collective-permute-start | bytes 36872 | tf_op jit(solution)/shard_map/ppermute | solution.py:388
  20.3 11.3 %collective-permute-start.3 = (f32[336,128]{1,0:T(8,128)S(1)}, f32[336,128]{1,0:T(8,128)S(1)}, u32[]{:S(2)}, u32[]{:S(2)}) collective-permute-start(f32[336,128]{1,0:T(8,128)S(1)} %get-tuple-element.116), channel_id=1, source_target_pairs={{8,0},{16,8},{24,16},{32,24},{40,32},{48,40},{56,48},{9,1},{17,9},... | collective-permute-start | bytes 516104 | tf_op jit(solution)/shard_map/ppermute | solution.py:388
  24.3 7.3 %collective-permute-start.2 = (f32[336,128]{1,0:T(8,128)S(1)}, f32[336,128]{1,0:T(8,128)S(1)}, u32[]{:S(2)}, u32[]{:S(2)}) collective-permute-start(f32[336,128]{1,0:T(8,128)S(1)} %get-tuple-element.117), channel_id=1, source_target_pairs={{0,8},{8,16},{16,24},{24,32},{32,40},{40,48},{48,56},{1,9},{9,17},... | collective-permute-start | bytes 516104 | tf_op jit(solution)/shard_map/ppermute | solution.py:388
  39.4 5.3 %collective-permute-start.4 = (f32[24,128]{1,0:T(8,128)S(1)}, f32[24,128]{1,0:T(8,128)S(1)}, u32[]{:S(2)}, u32[]{:S(2)}) collective-permute-start(f32[24,128]{1,0:T(8,128)S(1)} %get-tuple-element.59), channel_id=1, source_target_pairs={{0,1},{1,2},{2,3},{3,4},{4,5},{5,6},{6,7},{8,9},{9,10},{10,11},{11... | collective-permute-start | bytes 36872 | tf_op jit(solution)/shard_map/ppermute | solution.py:388
  41.3 10.5 %collective-permute-start.5 = (f32[24,128]{1,0:T(8,128)S(1)}, f32[24,128]{1,0:T(8,128)S(1)}, u32[]{:S(2)}, u32[]{:S(2)}) collective-permute-start(f32[24,128]{1,0:T(8,128)S(1)} %get-tuple-element.60), channel_id=1, source_target_pairs={{1,0},{2,1},{3,2},{4,3},{5,4},{6,5},{7,6},{9,8},{10,9},{11,10},{12... | collective-permute-start | bytes 36872 | tf_op jit(solution)/shard_map/ppermute | solution.py:388
  55.1 20.1 %collective-permute-start.6 = (f32[96,1024]{1,0:T(8,128)S(1)}, f32[96,1024]{1,0:T(8,128)S(1)}, u32[]{:S(2)}, u32[]{:S(2)}) collective-permute-start(f32[96,1024]{1,0:T(8,128)S(1)} %get-tuple-element.61), channel_id=1, source_target_pairs={{64,0},{72,8},{80,16},{88,24},{96,32},{104,40},{112,48},{120,56},{... | collective-permute-start | bytes 1179656 | tf_op jit(solution)/shard_map/ppermute | solution.py:399
  57.7 14.5 %collective-permute-start.7 = (f32[96,384]{1,0:T(8,128)S(1)}, f32[96,384]{1,0:T(8,128)S(1)}, u32[]{:S(2)}, u32[]{:S(2)}) collective-permute-start(f32[96,384]{1,0:T(8,128)S(1)} %get-tuple-element.62), channel_id=1, source_target_pairs={{64,8},{72,16},{80,24},{88,32},{96,40},{104,48},{112,56},{128,72},... | collective-permute-start | bytes 442376 | tf_op jit(solution)/shard_map/ppermute | solution.py:399
  60.4 14.8 %collective-permute-start.8 = (f32[96,384]{1,0:T(8,128)S(1)}, f32[96,384]{1,0:T(8,128)S(1)}, u32[]{:S(2)}, u32[]{:S(2)}) collective-permute-start(f32[96,384]{1,0:T(8,128)S(1)} %get-tuple-element.63), channel_id=1, source_target_pairs={{72,0},{80,8},{88,16},{96,24},{104,32},{112,40},{120,48},{136,64},... | collective-permute-start | bytes 442376 | tf_op jit(solution)/shard_map/ppermute | solution.py:399
  77.7 5.3 %collective-permute-start.9 = (f32[24,128]{1,0:T(8,128)S(1)}, f32[24,128]{1,0:T(8,128)S(1)}, u32[]{:S(2)}, u32[]{:S(2)}) collective-permute-start(f32[24,128]{1,0:T(8,128)S(1)} %get-tuple-element.66), channel_id=1, source_target_pairs={{0,1},{1,2},{2,3},{3,4},{4,5},{5,6},{6,7},{8,9},{9,10},{10,11},{11... | collective-permute-start | bytes 36872 | tf_op jit(solution)/shard_map/ppermute | solution.py:388
  79.7 10.6 %collective-permute-start.10 = (f32[24,128]{1,0:T(8,128)S(1)}, f32[24,128]{1,0:T(8,128)S(1)}, u32[]{:S(2)}, u32[]{:S(2)}) collective-permute-start(f32[24,128]{1,0:T(8,128)S(1)} %get-tuple-element.67), channel_id=1, source_target_pairs={{1,0},{2,1},{3,2},{4,3},{5,4},{6,5},{7,6},{9,8},{10,9},{11,10},{12... | collective-permute-start | bytes 36872 | tf_op jit(solution)/shard_map/ppermute | solution.py:388
  93.5 19.7 %collective-permute-start.11 = (f32[96,1024]{1,0:T(8,128)S(1)}, f32[96,1024]{1,0:T(8,128)S(1)}, u32[]{:S(2)}, u32[]{:S(2)}) collective-permute-start(f32[96,1024]{1,0:T(8,128)S(1)} %get-tuple-element.68), channel_id=1, source_target_pairs={{64,0},{72,8},{80,16},{88,24},{96,32},{104,40},{112,48},{120,56},{... | collective-permute-start | bytes 1179656 | tf_op jit(solution)/shard_map/ppermute | solution.py:399
  96.0 12.7 %collective-permute-start.12 = (f32[96,384]{1,0:T(8,128)S(1)}, f32[96,384]{1,0:T(8,128)S(1)}, u32[]{:S(2)}, u32[]{:S(2)}) collective-permute-start(f32[96,384]{1,0:T(8,128)S(1)} %get-tuple-element.69), channel_id=1, source_target_pairs={{64,8},{72,16},{80,24},{88,32},{96,40},{104,48},{112,56},{128,72},... | collective-permute-start | bytes 442376 | tf_op jit(solution)/shard_map/ppermute | solution.py:399
  98.2 14.9 %collective-permute-start.13 = (f32[96,384]{1,0:T(8,128)S(1)}, f32[96,384]{1,0:T(8,128)S(1)}, u32[]{:S(2)}, u32[]{:S(2)}) collective-permute-start(f32[96,384]{1,0:T(8,128)S(1)} %get-tuple-element.70), channel_id=1, source_target_pairs={{72,0},{80,8},{88,16},{96,24},{104,32},{112,40},{120,48},{136,64},... | collective-permute-start | bytes 442376 | tf_op jit(solution)/shard_map/ppermute | solution.py:399
  115.7 5.3 %collective-permute-start.14 = (f32[24,128]{1,0:T(8,128)S(1)}, f32[24,128]{1,0:T(8,128)S(1)}, u32[]{:S(2)}, u32[]{:S(2)}) collective-permute-start(f32[24,128]{1,0:T(8,128)S(1)} %get-tuple-element.73), channel_id=1, source_target_pairs={{0,1},{1,2},{2,3},{3,4},{4,5},{5,6},{6,7},{8,9},{9,10},{10,11},{11... | collective-permute-start | bytes 36872 | tf_op jit(solution)/shard_map/ppermute | solution.py:388
  117.6 10.6 %collective-permute-start.15 = (f32[24,128]{1,0:T(8,128)S(1)}, f32[24,128]{1,0:T(8,128)S(1)}, u32[]{:S(2)}, u32[]{:S(2)}) collective-permute-start(f32[24,128]{1,0:T(8,128)S(1)} %get-tuple-element.74), channel_id=1, source_target_pairs={{1,0},{2,1},{3,2},{4,3},{5,4},{6,5},{7,6},{9,8},{10,9},{11,10},{12... | collective-permute-start | bytes 36872 | tf_op jit(solution)/shard_map/ppermute | solution.py:388
  131.4 17.6 %collective-permute-start.16 = (f32[96,1024]{1,0:T(8,128)S(1)}, f32[96,1024]{1,0:T(8,128)S(1)}, u32[]{:S(2)}, u32[]{:S(2)}) collective-permute-start(f32[96,1024]{1,0:T(8,128)S(1)} %get-tuple-element.75), channel_id=1, source_target_pairs={{64,0},{72,8},{80,16},{88,24},{96,32},{104,40},{112,48},{120,56},{... | collective-permute-start | bytes 1179656 | tf_op jit(solution)/shard_map/ppermute | solution.py:399
  133.8 12.9 %collective-permute-start.17 = (f32[96,384]{1,0:T(8,128)S(1)}, f32[96,384]{1,0:T(8,128)S(1)}, u32[]{:S(2)}, u32[]{:S(2)}) collective-permute-start(f32[96,384]{1,0:T(8,128)S(1)} %get-tuple-element.76), channel_id=1, source_target_pairs={{64,8},{72,16},{80,24},{88,32},{96,40},{104,48},{112,56},{128,72},... | collective-permute-start | bytes 442376 | tf_op jit(solution)/shard_map/ppermute | solution.py:399
  136.2 12.8 %collective-permute-start.18 = (f32[96,384]{1,0:T(8,128)S(1)}, f32[96,384]{1,0:T(8,128)S(1)}, u32[]{:S(2)}, u32[]{:S(2)}) collective-permute-start(f32[96,384]{1,0:T(8,128)S(1)} %get-tuple-element.77), channel_id=1, source_target_pairs={{72,0},{80,8},{88,16},{96,24},{104,32},{112,40},{120,48},{136,64},... | collective-permute-start | bytes 442376 | tf_op jit(solution)/shard_map/ppermute | solution.py:399
  183.4 39.6 %all-to-all-start.1 = ((f32[64,16,128]{2,1,0:T(8,128)}), f32[64,16,128]{2,1,0:T(8,128)S(1)}, u32[]{:S(2)}, u32[]{:S(2)}) async-start(f32[64,16,128]{2,1,0:T(8,128)} %shard_map.164), calls=%async_computation.1 | async-start | bytes 1048576 | tf_op jit(solution)/shard_map/all_to_all | solution.py:407
  190.2 8.9 %collective-permute-start.19 = (f32[24,128]{1,0:T(8,128)S(1)}, f32[24,128]{1,0:T(8,128)S(1)}, u32[]{:S(2)}, u32[]{:S(2)}) collective-permute-start(f32[24,128]{1,0:T(8,128)S(1)} %get-tuple-element.80), channel_id=1, source_target_pairs={{0,1},{1,2},{2,3},{3,4},{4,5},{5,6},{6,7},{8,9},{9,10},{10,11},{11... | collective-permute-start | bytes 36872 | tf_op jit(solution)/shard_map/ppermute | solution.py:388
  197.2 10.5 %collective-permute-start.20 = (f32[24,128]{1,0:T(8,128)S(1)}, f32[24,128]{1,0:T(8,128)S(1)}, u32[]{:S(2)}, u32[]{:S(2)}) collective-permute-start(f32[24,128]{1,0:T(8,128)S(1)} %get-tuple-element.81), channel_id=1, source_target_pairs={{1,0},{2,1},{3,2},{4,3},{5,4},{6,5},{7,6},{9,8},{10,9},{11,10},{12... | collective-permute-start | bytes 36872 | tf_op jit(solution)/shard_map/ppermute | solution.py:388
  210.9 6.9 %collective-permute-start.21 = (f32[96,384]{1,0:T(8,128)S(1)}, f32[96,384]{1,0:T(8,128)S(1)}, u32[]{:S(2)}, u32[]{:S(2)}) collective-permute-start(f32[96,384]{1,0:T(8,128)S(1)} %get-tuple-element.83), channel_id=1, source_target_pairs={{0,8},{8,16},{16,24},{24,32},{32,40},{40,48},{48,56},{1,9},{9,17},... | collective-permute-start | bytes 442376 | tf_op jit(solution)/shard_map/ppermute | solution.py:388
  215.7 6.5 %collective-permute-start.22 = (f32[96,384]{1,0:T(8,128)S(1)}, f32[96,384]{1,0:T(8,128)S(1)}, u32[]{:S(2)}, u32[]{:S(2)}) collective-permute-start(f32[96,384]{1,0:T(8,128)S(1)} %get-tuple-element.84), channel_id=1, source_target_pairs={{8,0},{16,8},{24,16},{32,24},{40,32},{48,40},{56,48},{9,1},{17,9},... | collective-permute-start | bytes 442376 | tf_op jit(solution)/shard_map/ppermute | solution.py:388
  (4 other events, 103.4 us)

commit v2 on v1

v2 whole, which is shorter than its diff:
```python
import functools

import jax
import jax.numpy as jnp
from jax import lax
from jax.experimental import pallas as pl
from jax.experimental.pallas import tpu as pltpu
from jax.sharding import PartitionSpec as P

KS = 7
TAPS = KS * KS
REACH = KS // 2
EPSILON = 1e-06
LANES = 128
GROUP = 8
ROWS = 8
C = 96
HID = 384
CELLS = ROWS * LANES
FOLD = 24
CHUNK = 256
PAYLOAD_ROWS = 1024
F32 = jnp.float32
BF16 = jnp.bfloat16
CONV_FLOPS = 2 * TAPS * C * CELLS
TILES = ("ty", "tx")


def call(kernel, outs, *operands, scratch=(), flops=0):
    whole = pl.BlockSpec(memory_space=pltpu.VMEM)
    return pl.pallas_call(
        kernel,
        out_shape=[jax.ShapeDtypeStruct(shape, F32) for shape in outs],
        in_specs=[whole] * len(operands),
        out_specs=[whole] * len(outs),
        scratch_shapes=[pltpu.VMEM(shape, F32) for shape in scratch],
        compiler_params=pltpu.CompilerParams(vmem_limit_bytes=28 * 1024 * 1024),
        cost_estimate=pl.CostEstimate(flops=flops, bytes_accessed=0, transcendentals=0) if flops else None,
    )(*operands)


def roll(value, shift):
    return pltpu.roll(value, shift % LANES, 1)


def lane_of(rows):
    return lax.broadcasted_iota(jnp.int32, (rows, LANES), 1)


def block(row):
    return pl.ds(row * LANES, LANES)


def split(value):
    high = value.astype(BF16)
    low = (value - high.astype(F32)).astype(BF16)
    return high, low


def product(left, right, dims):
    def part(one, two):
        return lax.dot_general(one, two, (dims, ((), ())), preferred_element_type=F32)

    return part(left[0], right[0]) + (part(left[0], right[1]) + part(left[1], right[0]))


ROW_COL = ((1,), (0,))
COL_COL = ((0,), (0,))
ROW_ROW = ((1,), (1,))


def pack_edges(field_ref, right_ref, left_ref):
    lane = lane_of(FOLD)
    for edge, out_ref in ((LANES - REACH, right_ref), (0, left_ref)):
        folded = jnp.zeros((FOLD, LANES), F32)
        for quarter in range(C // FOLD):
            part = pl.ds(quarter * FOLD, FOLD)
            for row in range(ROWS):
                at = 32 * quarter + REACH * row
                moved = roll(field_ref[part, block(row)], at - edge)
                folded = jnp.where((lane >= at) & (lane < at + REACH), moved, folded)
        out_ref[...] = folded


def unfold(folded_ref, wide_ref):
    for quarter in range(C // FOLD):
        wide_ref[pl.ds(quarter * FOLD, FOLD), :] = roll(folded_ref[...], -32 * quarter)


def shifted_row(row, left, right, lane, distance):
    if distance > 0:
        return roll(jnp.where(lane < distance, right, row), -distance)
    if distance < 0:
        return roll(jnp.where(lane >= LANES + distance, left, row), -distance)
    return row


def left_edge(wide, row):
    return roll(wide, LANES - REACH - REACH * row)


def right_edge(wide, row):
    return roll(wide, -REACH * row)


def tap_of(taps, tap):
    return jnp.broadcast_to(taps[:, tap : tap + 1], (GROUP, LANES))


def take_field(acts_ref, field_ref, right_ref, left_ref):
    for row in range(ROWS):
        field_ref[:, block(row)] = acts_ref[pl.ds(row, C, stride=ROWS), :]
    pack_edges(field_ref, right_ref, left_ref)


def column(row):
    return jnp.broadcast_to(row, (GROUP, row.shape[1])).T[:, :1]


def prepare(
    top_ref, active_ref, kernel_ref, gain_row, bias_row, w_in_ref, b_in_row, w_out_ref, scale_row,
    cotan_ref, taps_ref, gain_ref, bias_ref, b_in_ref, w_in_gain_ref, w_out_scale_ref,
):
    for row in range(ROWS):
        cotan_ref[:, block(row)] = top_ref[pl.ds(row, C, stride=ROWS), :] * active_ref[...]
    taps_ref[:, :TAPS] = kernel_ref[:, 0, :].T
    gain_ref[...] = column(gain_row[...])
    bias_ref[...] = column(bias_row[...])
    b_in_ref[...] = column(b_in_row[...])
    w_in_gain_ref[...] = w_in_ref[...] * gain_ref[...]
    w_out_scale_ref[...] = (w_out_ref[...] * column(scale_row[...])).T


def padded_rows(group, field_ref, above_ref, below_ref, wides):
    lefts = [ref[pl.ds(group, GROUP), :] for ref in wides[0::2]]
    rights = [ref[pl.ds(group, GROUP), :] for ref in wides[1::2]]
    rows = []
    for index in range(REACH):
        value = above_ref[pl.ds(index * C + group, GROUP), :]
        rows.append((value, lefts[0], rights[0], ROWS - REACH + index))
    for index in range(ROWS):
        rows.append((field_ref[pl.ds(group, GROUP), block(index)], lefts[1], rights[1], index))
    for index in range(REACH):
        value = below_ref[pl.ds(index * C + group, GROUP), :]
        rows.append((value, lefts[2], rights[2], index))
    return [(value, left_edge(left, at), right_edge(right, at)) for value, left, right, at in rows]


EDGE_ROWS = REACH * C


def unfold_six(own_left, own_right, above_ref, below_ref, wides):
    folded = (
        above_ref.at[pl.ds(EDGE_ROWS, FOLD), :],
        above_ref.at[pl.ds(EDGE_ROWS + FOLD, FOLD), :],
        own_left,
        own_right,
        below_ref.at[pl.ds(EDGE_ROWS, FOLD), :],
        below_ref.at[pl.ds(EDGE_ROWS + FOLD, FOLD), :],
    )
    for source, wide in zip(folded, wides):
        unfold(source, wide)


def tap_index(a, b, flipped):
    tap = a * KS + b
    return TAPS - 1 - tap if flipped else tap


def conv_own(flipped, *refs):
    start_ref = refs[0] if flipped else None
    field_ref, left_ref, right_ref, taps_ref, out_ref, wide_left, wide_right = refs[-7:]
    unfold(left_ref, wide_left)
    unfold(right_ref, wide_right)
    lane = lane_of(GROUP)

    def conv_group(index, carry):
        channels = pl.ds(pl.multiple_of(index * GROUP, GROUP), GROUP)
        taps = taps_ref[channels, :]
        left, right = wide_left[channels, :], wide_right[channels, :]
        rows = [
            (field_ref[channels, block(row)], left_edge(left, row), right_edge(right, row))
            for row in range(ROWS)
        ]
        if flipped:
            sums = [start_ref[channels, block(row)] for row in range(ROWS)]
        else:
            sums = [jnp.zeros((GROUP, LANES), F32)] * ROWS
        for b in range(KS):
            moved = [shifted_row(*row, lane, b - REACH) for row in rows]
            for a in range(KS):
                weight = tap_of(taps, tap_index(a, b, flipped))
                for row in range(ROWS):
                    if 0 <= row + a - REACH < ROWS:
                        sums[row] = sums[row] + weight * moved[row + a - REACH]
        for row in range(ROWS):
            out_ref[channels, block(row)] = sums[row]
        return carry

    lax.fori_loop(0, C // GROUP, conv_group, 0)


def conv_edges(flipped, own_ref, above_ref, below_ref, taps_ref, wides, put):
    sources = (
        above_ref.at[pl.ds(EDGE_ROWS, FOLD), :],
        above_ref.at[pl.ds(EDGE_ROWS + FOLD, FOLD), :],
        below_ref.at[pl.ds(EDGE_ROWS, FOLD), :],
        below_ref.at[pl.ds(EDGE_ROWS + FOLD, FOLD), :],
    )
    for source, wide in zip(sources, wides):
        unfold(source, wide)
    lane = lane_of(GROUP)

    def conv_group(index, carry):
        group = pl.multiple_of(index * GROUP, GROUP)
        channels = pl.ds(group, GROUP)
        taps = taps_ref[channels, :]
        edges = [wide[channels, :] for wide in wides]
        rows = []
        for side, ref in enumerate((above_ref, below_ref)):
            for at in range(REACH):
                theirs = at if side else ROWS - REACH + at
                mine = ROWS + at if side else at - REACH
                left, right = edges[2 * side], edges[2 * side + 1]
                value = ref[pl.ds(at * C + group, GROUP), :]
                rows.append((mine, (value, left_edge(left, theirs), right_edge(right, theirs))))
        sums = [own_ref[channels, block(row)] for row in range(ROWS)]
        for b in range(KS):
            moved = {mine: shifted_row(*row, lane, b - REACH) for mine, row in rows}
            for a in range(KS):
                if a == REACH:
                    continue
                weight = tap_of(taps, tap_index(a, b, flipped))
                for row in range(ROWS):
                    if row + a - REACH in moved:
                        sums[row] = sums[row] + weight * moved[row + a - REACH]
        put(group, sums)
        return carry

    lax.fori_loop(0, C // GROUP, conv_group, 0)


def forward(
    own_ref, above_ref, below_ref, taps_ref, gain_ref, bias_ref, w_in_ref, b_in_ref,
    normed_ref, inv_ref, slope_ref, hidden_ref,
    *wides,
):
    def put(group, sums):
        for row in range(ROWS):
            normed_ref[pl.ds(group, GROUP), block(row)] = sums[row]

    conv_edges(False, own_ref, above_ref, below_ref, taps_ref, wides, put)
    w_in = split(w_in_ref[...])
    for start in range(0, CELLS, CHUNK):
        cells = pl.ds(start, CHUNK)
        conv_out = normed_ref[:, cells]
        centred = conv_out - jnp.mean(conv_out, axis=0, keepdims=True)
        inv = lax.rsqrt(jnp.mean(centred * centred, axis=0, keepdims=True) + EPSILON)
        normed = centred * inv
        normed_ref[:, cells] = normed
        inv_ref[:, cells] = inv
        lifted = normed * gain_ref[...] + bias_ref[...]
        pre_act = product(w_in, split(lifted), COL_COL) + b_in_ref[...]
        gate = 0.5 * (1.0 + lax.erf(pre_act * 0.7071067811865476))
        hidden_ref[:, cells] = pre_act * gate
        slope_ref[:, cells] = gate + pre_act * jnp.exp(-0.5 * pre_act * pre_act) * 0.3989422804014327


def step(
    cotan_refs, normed_ref, inv_ref, slope_ref, w_in_gain_ref, w_out_scale_ref,
    grad_ref, to_right_ref, to_left_ref, cotan_ref=None, grad_pre_ref=None,
):
    w_out = split(w_out_scale_ref[...])
    w_in = split(w_in_gain_ref[...])
    for start in range(0, CELLS, CHUNK):
        cells = pl.ds(start, CHUNK)
        cotan = sum(ref[:, cells] for ref in cotan_refs)
        grad_pre = product(w_out, split(cotan), ROW_COL) * slope_ref[:, cells]
        if grad_pre_ref is not None:
            cotan_ref[:, cells] = cotan
            grad_pre_ref[:, cells] = grad_pre
        grad_normed = product(w_in, split(grad_pre), ROW_COL)
        normed = normed_ref[:, cells]
        mean = jnp.mean(grad_normed, axis=0, keepdims=True)
        along = jnp.mean(grad_normed * normed, axis=0, keepdims=True)
        grad_ref[:, cells] = inv_ref[:, cells] * (grad_normed - mean - normed * along)
    pack_edges(grad_ref, to_right_ref, to_left_ref)


def middle_step(cotan_ref, *refs):
    step((cotan_ref,), *refs)


def last_step(count, *refs):
    step(refs[:count], *refs[count:])


def finish(own_ref, above_ref, below_ref, taps_ref, out_ref, *wides):
    def put(group, sums):
        for row in range(ROWS):
            out_ref[pl.ds(group, GROUP), block(row)] = sums[row]

    conv_edges(True, own_ref, above_ref, below_ref, taps_ref, wides, put)


def last_finish(own_ref, above_ref, below_ref, taps_ref, out_ref, *wides):
    def put(group, sums):
        for row in range(ROWS):
            out_ref[pl.ds(group * ROWS + row, GROUP, stride=ROWS), :] = sums[row]

    conv_edges(True, own_ref, above_ref, below_ref, taps_ref, wides, put)


LIFT_ROWS = C + GROUP
OUT_AT = 0
IN_AT = OUT_AT + C * HID // LANES
TAPS_AT = IN_AT + LIFT_ROWS * HID // LANES
USED_ROWS = TAPS_AT + C


def parameter_terms(
    field_ref, left_ref, right_ref, above_ref, below_ref, grad_ref, cotan_ref, hidden_ref, normed_ref, grad_pre_ref,
    payload_ref,
    *wides,
):
    unfold_six(left_ref, right_ref, above_ref, below_ref, wides)
    lane = lane_of(GROUP)

    def taps_group(index, carry):
        group = pl.multiple_of(index * GROUP, GROUP)
        rows = padded_rows(group, field_ref, above_ref, below_ref, wides)
        grads = [grad_ref[pl.ds(group, GROUP), block(row)] for row in range(ROWS)]
        result = jnp.zeros((GROUP, LANES), F32)
        for b in range(KS):
            moved = [shifted_row(*row, lane, b - REACH) for row in rows]
            for a in range(KS):
                terms = [grads[row] * moved[row + a] for row in range(ROWS)]
                while len(terms) > 1:
                    terms = [one + two for one, two in zip(terms[0::2], terms[1::2])]
                total = jnp.sum(terms[0], axis=1, keepdims=True)
                result = jnp.where(lane == a * KS + b, total, result)
        payload_ref[pl.ds(TAPS_AT + group, GROUP), :] = result
        return carry

    lax.fori_loop(0, C // GROUP, taps_group, 0)
    grad_w_out = product(split(cotan_ref[...]), split(hidden_ref[...]), ROW_ROW)
    ones = jnp.where(lax.broadcasted_iota(jnp.int32, (GROUP, CELLS), 0) == 0, 1.0, 0.0)
    lifted = jnp.concatenate([normed_ref[...], ones], axis=0)
    grad_w_in = product(split(lifted), split(grad_pre_ref[...]), ROW_ROW)
    for part in range(HID // LANES):
        payload_ref[pl.ds(OUT_AT + part * C, C), :] = grad_w_out[:, part * LANES : (part + 1) * LANES]
        payload_ref[pl.ds(IN_AT + part * LIFT_ROWS, LIFT_ROWS), :] = grad_w_in[:, part * LANES : (part + 1) * LANES]
    payload_ref[pl.ds(USED_ROWS, PAYLOAD_ROWS - USED_ROWS), :] = jnp.zeros((PAYLOAD_ROWS - USED_ROWS, LANES), F32)


def sum_shares(shares_ref, out_ref):
    devices, rows = out_ref.shape[0], out_ref.shape[1]

    def add(device, total):
        return total + shares_ref[device]

    total = lax.fori_loop(1, devices, add, shares_ref[0], unroll=7)

    def put(device, carry):
        out_ref[device] = total
        return carry

    lax.fori_loop(0, devices, put, 0, unroll=8)


def parameter_grads(
    payload_ref, gain_ref, bias_ref, w_in_ref, w_out_ref, scale_row,
    kernel_out, gain_out, bias_out, w_in_out, b_in_out, w_out_out, scale_out,
):
    kernel_out[:, 0, :] = payload_ref[pl.ds(TAPS_AT, C), :].T[:TAPS, :]
    scale = column(scale_row[...])
    sums = [jnp.zeros((C, 1), F32)] * 3
    for part in range(HID // LANES):
        hidden = pl.ds(part * LANES, LANES)
        grad_out = payload_ref[pl.ds(OUT_AT + part * C, C), :]
        w_out_out[:, hidden] = grad_out * scale
        at = IN_AT + part * LIFT_ROWS
        grad_in = payload_ref[pl.ds(at, C), :]
        grad_b = payload_ref[pl.ds(at + C, 1), :]
        b_in_out[:, hidden] = grad_b
        w_in_out[:, hidden] = grad_in * gain_ref[...] + bias_ref[...] * grad_b
        w_in = w_in_ref[:, hidden]
        terms = (w_in * grad_in, w_in * grad_b, w_out_ref[:, hidden] * grad_out)
        sums = [total + jnp.sum(term, axis=1, keepdims=True) for total, term in zip(sums, terms)]
    for total, out in zip(sums, (gain_out, bias_out, scale_out)):
        out[...] = jnp.broadcast_to(total, (C, LANES)).T[:1, :]


def exchange(to_next, to_previous, axis, section=None):
    size = lax.axis_size(axis)
    sections = range(lax.axis_size("section")) if section is None else (section,)
    up = [(s * size + i, s * size + i + 1) for s in sections for i in range(size - 1)]
    down = [(there, here) for here, there in up]
    axes = ("section", axis)
    return lax.ppermute(to_next, axes, up), lax.ppermute(to_previous, axes, down)


def sum_over_tiles(payload):
    devices = lax.axis_size(TILES)
    rows = PAYLOAD_ROWS // devices
    shares = lax.all_to_all(payload.reshape(devices, rows, LANES), TILES, 0, 0)
    (copies,) = call(sum_shares, [(devices, rows, LANES)], shares)
    return lax.all_to_all(copies, TILES, 0, 0).reshape(PAYLOAD_ROWS, LANES)


def edge_rows(field, left, right, first):
    rows = [field[:, row * LANES : (row + 1) * LANES] for row in range(first, first + REACH)]
    return jnp.concatenate(rows + [left, right], axis=0)


def exchange_rows(field, left, right, section=None):
    return exchange(edge_rows(field, left, right, ROWS - REACH), edge_rows(field, left, right, 0), "ty", section)


def on_device(acts, top_grad, kernel, ln_gain, ln_bias, w_in, b_in, w_out, layer_scale):
    sections = lax.axis_size("section")
    is_last = (lax.axis_index("section") == sections - 1).astype(F32)
    active = jnp.full((1, LANES), is_last, F32)
    field_shape, side, wide, hidden_shape = ((C, CELLS), (FOLD, LANES), (C, LANES), (HID, CELLS))
    weight_in, weight_out = (w_in[0], w_out[0].T)
    acts_rows, top_rows = (acts.reshape(C * ROWS, LANES), top_grad.reshape(C * ROWS, LANES))

    field, to_right, to_left = call(take_field, [field_shape, side, side], acts_rows)
    left, right = exchange(to_right, to_left, "tx")
    cotan, taps, gain, shift_bias, bias_in, w_in_gain, w_out_scale = call(
        prepare,
        [field_shape, wide, (C, 1), (C, 1), (HID, 1), (C, HID), (HID, C)],
        top_rows, active, jnp.transpose(kernel, (1, 0, 2)), ln_gain, ln_bias, weight_in, b_in, weight_out, layer_scale,
    )
    above, below = exchange_rows(field, left, right)
    (own,) = call(
        functools.partial(conv_own, False), [field_shape], field, left, right, taps, scratch=[wide] * 2, flops=CONV_FLOPS
    )
    normed, inv, slope, hidden = call(
        forward,
        [field_shape, (1, CELLS), hidden_shape, hidden_shape],
        own, above, below, taps, gain, shift_bias, weight_in, bias_in,
        scratch=[wide] * 4,
    )
    saved = (normed, inv, slope, w_in_gain, w_out_scale)
    step_outs = [field_shape, side, side]

    cotans = [cotan]
    for section in reversed(range(sections)):
        if section:
            only = section
            grad, to_right, to_left = call(middle_step, step_outs, cotan, *saved)
        else:
            only = None
            grad, to_right, to_left, cotan, grad_pre = call(
                functools.partial(last_step, len(cotans)), step_outs + [field_shape, hidden_shape], *cotans, *saved
            )
        grad_left, grad_right = exchange(to_right, to_left, "tx", only)
        if not section:
            (payload,) = call(
                parameter_terms, [(PAYLOAD_ROWS, LANES)],
                field, left, right, above, below, grad, cotan, hidden, normed, grad_pre, scratch=[wide] * 6,
                flops=4 * CONV_FLOPS,
            )
        grad_above, grad_below = exchange_rows(grad, grad_left, grad_right, only)
        (own,) = call(
            functools.partial(conv_own, True), [field_shape],
            cotan, grad, grad_left, grad_right, taps, scratch=[wide] * 2, flops=CONV_FLOPS,
        )
        edges = (own, grad_above, grad_below, taps)
        if section:
            (cotan,) = call(finish, [field_shape], *edges, scratch=[wide] * 4)
            cotan = lax.ppermute(cotan, "section", [(section, section - 1)])
            cotans.append(cotan)
    (input_grad,) = call(last_finish, [(C * ROWS, LANES)], *edges, scratch=[wide] * 4)
    payload = sum_over_tiles(payload)
    grad_kernel, grad_gain, grad_bias, grad_w_in, grad_b_in, grad_w_out, grad_scale = call(
        parameter_grads,
        [(TAPS, 1, C), (1, C), (1, C), (C, HID), (1, HID), (C, HID), (1, C)],
        payload, gain, shift_bias, weight_in, weight_out, layer_scale,
    )
    return (
        input_grad.reshape(1, 1, C, ROWS, LANES),
        jnp.transpose(grad_kernel, (1, 0, 2)),
        grad_gain,
        grad_bias,
        grad_w_in[None],
        grad_b_in,
        grad_w_out.T[None],
        grad_scale,
    )


def solution(mesh):
    placed = (
        P("section", None, None, "ty", "tx"),
        P(None, None, "ty", "tx"),
        P("section", None, None),
        P("section", None),
        P("section", None),
        P("section", None, None),
        P("section", None),
        P("section", None, None),
        P("section", None),
    )
    return jax.shard_map(
        on_device,
        mesh=mesh,
        in_specs=placed,
        out_specs=(
            P("section", None, None, "ty", "tx"),
            P("section", None, None),
            P("section", None),
            P("section", None),
            P("section", None, None),
            P("section", None),
            P("section", None, None),
            P("section", None),
        ),
        check_vma=False,
    )
```

time: 228 us -> 220 us (0.965)
  the two profiles are of different devices: /device:TPU:39 before, /device:TPU:1 now
where the time goes in v2:
time: 220 us; the launch traced here: 219 us
  waiting for transfers between devices  95.9 us (44%)
  starting transfers between devices  63.5 us (29%)
  Pallas kernels  51.3 us (23%)
  local copies, waits for them, and re-layouts  7.42 us (3%)
    ppermute x3, waiting for transfers between devices, on_device(): cotan = lax.ppermute(cotan, 'section', [(section, section - 1)])  77.1 us
    pallas_call x19, Pallas kernels, call(): pl.pallas_call(kernel, out_shape=[jax.ShapeDtypeStruct(shape, F32) for sh...  51.3 us
    all_to_all x1, starting transfers between devices, sum_over_tiles(): shares = lax.all_to_all(payload.reshape(devices, rows, LANES), TILES, 0, 0)  24.3 us
    ppermute x10, starting transfers between devices, exchange(): lax.ppermute(to_next, axes, up)  17.5 us
    ppermute x10, starting transfers between devices, exchange(): lax.ppermute(to_previous, axes, down)  12.9 us
    all_to_all x1, waiting for transfers between devices, sum_over_tiles(): shares = lax.all_to_all(payload.reshape(devices, rows, LANES), TILES, 0, 0)  11.7 us
    unnamed x44, local copies, waits for them, and re-layouts  7.4 us
    all_to_all x1, starting transfers between devices, sum_over_tiles(): return lax.all_to_all(copies, TILES, 0, 0).reshape(PAYLOAD_ROWS, LANES)  5.88 us
  transfers between devices with their start and end apart: 25, of which 4 were waited for; matrix products, arithmetic and copies ran while one was open for 0% of the time, Pallas kernels for 9%

profile of v2, /device:TPU:1, one launch (start us, length us, event | category | flops | bytes accessed | tf_op | source)
XLA Modules:
  0.0 219.5 jit_solution(6060699018543877080)
XLA Ops:
  2.0 3.9 %collective-permute-start = (f32[24,128]{1,0:T(8,128)S(1)}, f32[24,128]{1,0:T(8,128)S(1)}, u32[]{:S(2)}, u32[]{:S(2)}) collective-permute-start(f32[24,128]{1,0:T(8,128)S(1)} %get-tuple-element.45), channel_id=1, source_target_pairs={{0,1},{1,2},{2,3},{3,4},{4,5},{5,6},{6,7},{64,65},{65,66},{66,67},... | collective-permute-start | bytes 36872 | tf_op jit(solution)/shard_map/ppermute | solution.py:400
  7.3 3.1 %collective-permute-done.1.refs_2_.right_ref = f32[24,128]{1,0:T(8,128)S(1)} collective-permute-done((f32[24,128]{1,0:T(8,128)S(1)}, f32[24,128]{1,0:T(8,128)S(1)}, u32[]{:S(2)}, u32[]{:S(2)}) %collective-permute-start.1) | collective-permute-done | bytes 12320 | tf_op jit(solution)/shard_map/ppermute | solution.py:400
  10.4 4.0 %collective-permute-start.3 = (f32[336,128]{1,0:T(8,128)S(1)}, f32[336,128]{1,0:T(8,128)S(1)}, u32[]{:S(2)}, u32[]{:S(2)}) collective-permute-start(f32[336,128]{1,0:T(8,128)S(1)} %get-tuple-element.124), channel_id=1, source_target_pairs={{8,0},{16,8},{24,16},{32,24},{40,32},{48,40},{56,48},{72,64},{80,7... | collective-permute-start | bytes 516104 | tf_op jit(solution)/shard_map/ppermute | solution.py:400
  14.4 3.1 %collective-permute-start.2 = (f32[336,128]{1,0:T(8,128)S(1)}, f32[336,128]{1,0:T(8,128)S(1)}, u32[]{:S(2)}, u32[]{:S(2)}) collective-permute-start(f32[336,128]{1,0:T(8,128)S(1)} %get-tuple-element.125), channel_id=1, source_target_pairs={{0,8},{8,16},{16,24},{24,32},{32,40},{40,48},{48,56},{64,72},{72,8... | collective-permute-start | bytes 516104 | tf_op jit(solution)/shard_map/ppermute | solution.py:400
  24.2 3.1 %shard_map.154.own_ref = f32[96,1024]{1,0:T(8,128)S(1)} custom-call(f32[96,1024]{1,0:T(8,128)S(1)} %get-tuple-element.44.refs_0_.field_ref, f32[24,128]{1,0:T(8,128)S(1)} %collective-permute-done.refs_1_.left_ref, f32[24,128]{1,0:T(8,128)S(1)} %collective-permute-done.1.refs_2_.right_ref, f32[96,128]{1,0:T(8,128)S(1)} %get-tuple-element.47.refs_3_.taps_ref.refs_4_), custom_call_target="tpu_custom_call" | custom-call | flops 9633792 | tf_op jit(solution)/shard_map/pallas_call | solution.py:31
  27.3 3.8 %shard_map.155 = (f32[96,1024]{1,0:T(8,128)S(1)}, f32[1,1024]{1,0:T(1,128)S(1)}, f32[384,1024]{1,0:T(8,128)S(1)}, f32[384,1024]{1,0:T(8,128)S(1)}) custom-call(f32[96,1024]{1,0:T(8,128)S(1)} %shard_map.154.own_ref, f32[336,128]{1,0:T(8,128)S(1)} %collective-permute-done.2.above_ref, f32[336,128]{1,0:T(8,128)S(1)} %collective-permute-done.3.below_ref, ...), custom_call_target="tpu_custom_call" | custom-call | tf_op jit(solution)/shard_map/pallas_call | solution.py:31
  31.2 2.5 %shard_map.156 = (f32[96,1024]{1,0:T(8,128)S(1)}, f32[24,128]{1,0:T(8,128)S(1)}, f32[24,128]{1,0:T(8,128)S(1)}) custom-call(f32[96,1024]{1,0:T(8,128)S(1)} %get-tuple-element.43.cotan_ref.refs_0_, f32[96,1024]{1,0:T(8,128)S(1)} %get-tuple-element.51.refs_0_.refs_4_.normed_ref, f32[1,1024]{1,0:T(1,128)S(1)} %get-tuple-element.52.refs_1_.refs_5_, ...), custom_call_target="tpu_custom_call" | custom-call | tf_op jit(solution)/shard_map/pallas_call | solution.py:31
  36.5 3.2 %shard_map.157.own_ref = f32[96,1024]{1,0:T(8,128)S(1)} custom-call(f32[96,1024]{1,0:T(8,128)S(1)} %get-tuple-element.43.cotan_ref.refs_0_, f32[96,1024]{1,0:T(8,128)S(1)} %get-tuple-element.56.refs_1_, f32[24,128]{1,0:T(8,128)S(1)} %collective-permute-done.4.refs_2_, f32[24,128]{1,0:T(8,128)S(1)} %collective-permute-done.5.refs_3_, ...), custom_call_target="tpu_custom_call" | custom-call | flops 9633792 | tf_op jit(solution)/shard_map/pallas_call | solution.py:31
  39.7 2.7 %shard_map.158 = f32[96,1024]{1,0:T(8,128)S(1)} custom-call(f32[96,1024]{1,0:T(8,128)S(1)} %shard_map.157.own_ref, f32[336,128]{1,0:T(8,128)S(1)} %collective-permute-done.6.above_ref, f32[336,128]{1,0:T(8,128)S(1)} %collective-permute-done.7.below_ref, f32[96,128]{1,0:T(8,128)S(1)} %get-tuple-element.47.refs_3_.taps_ref.refs_4_), custom_call_target="tpu_custom_call" | custom-call | tf_op jit(solution)/shard_map/pallas_call | solution.py:31
  48.4 3.2 %shard_map.160.own_ref = f32[96,1024]{1,0:T(8,128)S(1)} custom-call(f32[96,1024]{1,0:T(8,128)S(1)} %collective-permute-done.8.cotan_ref.refs_0_.refs_1_, f32[96,1024]{1,0:T(8,128)S(1)} %get-tuple-element.59.refs_1_, f32[24,128]{1,0:T(8,128)S(1)} %collective-permute-done.9.refs_2_, f32[24,128]{1,0:T(8,128)S(1)} %collective-permute-done.10.refs_3_, ...), custom_call_target="tpu_custom_call" | custom-call | flops 9633792 | tf_op jit(solution)/shard_map/pallas_call | solution.py:31
  51.6 2.7 %shard_map.161 = f32[96,1024]{1,0:T(8,128)S(1)} custom-call(f32[96,1024]{1,0:T(8,128)S(1)} %shard_map.160.own_ref, f32[336,128]{1,0:T(8,128)S(1)} %collective-permute-done.11.above_ref, f32[336,128]{1,0:T(8,128)S(1)} %collective-permute-done.12.below_ref, f32[96,128]{1,0:T(8,128)S(1)} %get-tuple-element.47.refs_3_.taps_ref.refs_4_), custom_call_target="tpu_custom_call" | custom-call | tf_op jit(solution)/shard_map/pallas_call | solution.py:31
  60.3 3.2 %shard_map.163.own_ref = f32[96,1024]{1,0:T(8,128)S(1)} custom-call(f32[96,1024]{1,0:T(8,128)S(1)} %collective-permute-done.13.cotan_ref.refs_0_.refs_2_, f32[96,1024]{1,0:T(8,128)S(1)} %get-tuple-element.62.refs_1_, f32[24,128]{1,0:T(8,128)S(1)} %collective-permute-done.14.refs_2_, f32[24,128]{1,0:T(8,128)S(1)} %collective-permute-done.15.refs_3_, ...), custom_call_target="tpu_custom_call" | custom-call | flops 9633792 | tf_op jit(solution)/shard_map/pallas_call | solution.py:31
  63.5 2.7 %shard_map.164 = f32[96,1024]{1,0:T(8,128)S(1)} custom-call(f32[96,1024]{1,0:T(8,128)S(1)} %shard_map.163.own_ref, f32[336,128]{1,0:T(8,128)S(1)} %collective-permute-done.16.above_ref, f32[336,128]{1,0:T(8,128)S(1)} %collective-permute-done.17.below_ref, f32[96,128]{1,0:T(8,128)S(1)} %get-tuple-element.47.refs_3_.taps_ref.refs_4_), custom_call_target="tpu_custom_call" | custom-call | tf_op jit(solution)/shard_map/pallas_call | solution.py:31
  67.6 77.1 %collective-permute-done.18.refs_3_ = f32[96,1024]{1,0:T(8,128)S(1)} collective-permute-done((f32[96,1024]{1,0:T(8,128)S(1)}, f32[96,1024]{1,0:T(8,128)S(1)}, u32[]{:S(2)}, u32[]{:S(2)}) %collective-permute-start.18) | collective-permute-done | bytes 393248 | tf_op jit(solution)/shard_map/ppermute | solution.py:473
  144.7 2.6 %shard_map.165 = (f32[96,1024]{1,0:T(8,128)S(1)}, f32[24,128]{1,0:T(8,128)S(1)}, f32[24,128]{1,0:T(8,128)S(1)}, f32[96,1024]{1,0:T(8,128)S(1)}, f32[384,1024]{1,0:T(8,128)S(1)}) custom-call(f32[96,1024]{1,0:T(8,128)S(1)} %get-tuple-element.43.cotan_ref.refs_0_, f32[96,1024]{1,0:T(8,128)S(1)} %collective-permute-done.8.cotan_ref.refs_0_.refs_1_, ...), custom_call_target="tpu_custom_call" | custom-call | tf_op jit(solution)/shard_map/pallas_call | solution.py:31
  147.3 7.4 %shard_map.168 = f32[1024,128]{1,0:T(8,128)} custom-call(f32[96,1024]{1,0:T(8,128)S(1)} %get-tuple-element.44.refs_0_.field_ref, f32[24,128]{1,0:T(8,128)S(1)} %collective-permute-done.refs_1_.left_ref, f32[24,128]{1,0:T(8,128)S(1)} %collective-permute-done.1.refs_2_.right_ref, f32[336,128]{1,0:T(8,128)S(1)} %collective-permute-done.2.above_ref, ...), custom_call_target="tpu_custom_call" | custom-call | flops 38535168 | tf_op jit(solution)/shard_map/pallas_call | solution.py:31
  154.7 24.3 %all-to-all-start = ((f32[64,16,128]{2,1,0:T(8,128)}), f32[64,16,128]{2,1,0:T(8,128)S(1)}, u32[]{:S(2)}, u32[]{:S(2)}) async-start(f32[64,16,128]{2,1,0:T(8,128)} %bitcast.7), calls=%async_computation | async-start | bytes 1048576 | tf_op jit(solution)/shard_map/all_to_all | solution.py:406
  179.0 3.3 %collective-permute-start.19 = (f32[24,128]{1,0:T(8,128)S(1)}, f32[24,128]{1,0:T(8,128)S(1)}, u32[]{:S(2)}, u32[]{:S(2)}) collective-permute-start(f32[24,128]{1,0:T(8,128)S(1)} %get-tuple-element.67), channel_id=1, source_target_pairs={{0,1},{1,2},{2,3},{3,4},{4,5},{5,6},{6,7},{64,65},{65,66},{66,67},... | collective-permute-start | bytes 36872 | tf_op jit(solution)/shard_map/ppermute | solution.py:400
  183.6 11.7 %all-to-all-done.shares_ref = f32[64,16,128]{2,1,0:T(8,128)S(1)} async-done(((f32[64,16,128]{2,1,0:T(8,128)}), f32[64,16,128]{2,1,0:T(8,128)S(1)}, u32[]{:S(2)}, u32[]{:S(2)}) %all-to-all-start) | async-done | bytes 524320 | tf_op jit(solution)/shard_map/all_to_all | solution.py:406
  196.2 5.9 %all-to-all-start.1 = ((f32[64,16,128]{2,1,0:T(8,128)}), f32[64,16,128]{2,1,0:T(8,128)S(1)}, u32[]{:S(2)}, u32[]{:S(2)}) async-start(f32[64,16,128]{2,1,0:T(8,128)} %shard_map.169), calls=%async_computation.1 | async-start | bytes 1048576 | tf_op jit(solution)/shard_map/all_to_all | solution.py:408
  204.6 3.2 %collective-permute-start.21 = (f32[336,128]{1,0:T(8,128)S(1)}, f32[336,128]{1,0:T(8,128)S(1)}, u32[]{:S(2)}, u32[]{:S(2)}) collective-permute-start(f32[336,128]{1,0:T(8,128)S(1)} %get-tuple-element.109), channel_id=1, source_target_pairs={{0,8},{8,16},{16,24},{24,32},{32,40},{40,48},{48,56},{64,72},{72,8... | collective-permute-start | bytes 516104 | tf_op jit(solution)/shard_map/ppermute | solution.py:400
  207.8 3.2 %shard_map.166.own_ref = f32[96,1024]{1,0:T(8,128)S(1)} custom-call(f32[96,1024]{1,0:T(8,128)S(1)} %get-tuple-element.65.refs_0_.cotan_ref, f32[96,1024]{1,0:T(8,128)S(1)} %get-tuple-element.66.refs_1_.grad_ref, f32[24,128]{1,0:T(8,128)S(1)} %collective-permute-done.19.refs_2_, f32[24,128]{1,0:T(8,128)S(1)} %collective-permute-done.20.refs_3_, ...), custom_call_target="tpu_custom_call" | custom-call | flops 9633792 | tf_op jit(solution)/shard_map/pallas_call | solution.py:31
  211.0 3.4 %shard_map.167 = f32[768,128]{1,0:T(8,128)} custom-call(f32[96,1024]{1,0:T(8,128)S(1)} %shard_map.166.own_ref, f32[336,128]{1,0:T(8,128)S(1)} %collective-permute-done.21.above_ref, f32[336,128]{1,0:T(8,128)S(1)} %collective-permute-done.22.below_ref, f32[96,128]{1,0:T(8,128)S(1)} %get-tuple-element.47.refs_3_.taps_ref.refs_4_), custom_call_target="tpu_custom_call" | custom-call | tf_op jit(solution)/shard_map/pallas_call | solution.py:31
  214.4 4.0 %all-to-all-done.1 = f32[64,16,128]{2,1,0:T(8,128)S(1)} async-done(((f32[64,16,128]{2,1,0:T(8,128)}), f32[64,16,128]{2,1,0:T(8,128)S(1)}, u32[]{:S(2)}, u32[]{:S(2)}) %all-to-all-start.1) | async-done | bytes 524320 | tf_op jit(solution)/shard_map/all_to_all | solution.py:408
  (95 shorter events, 31.1 us)
Async XLA Ops:
  2.0 5.3 %collective-permute-start = (f32[24,128]{1,0:T(8,128)S(1)}, f32[24,128]{1,0:T(8,128)S(1)}, u32[]{:S(2)}, u32[]{:S(2)}) collective-permute-start(f32[24,128]{1,0:T(8,128)S(1)} %get-tuple-element.45), channel_id=1, source_target_pairs={{0,1},{1,2},{2,3},{3,4},{4,5},{5,6},{6,7},{64,65},{65,66},{66,67},... | collective-permute-start | bytes 36872 | tf_op jit(solution)/shard_map/ppermute | solution.py:400
  5.9 4.4 %collective-permute-start.1 = (f32[24,128]{1,0:T(8,128)S(1)}, f32[24,128]{1,0:T(8,128)S(1)}, u32[]{:S(2)}, u32[]{:S(2)}) collective-permute-start(f32[24,128]{1,0:T(8,128)S(1)} %get-tuple-element.46), channel_id=1, source_target_pairs={{1,0},{2,1},{3,2},{4,3},{5,4},{6,5},{7,6},{65,64},{66,65},{67,66},... | collective-permute-start | bytes 36872 | tf_op jit(solution)/shard_map/ppermute | solution.py:400
  10.4 16.9 %collective-permute-start.3 = (f32[336,128]{1,0:T(8,128)S(1)}, f32[336,128]{1,0:T(8,128)S(1)}, u32[]{:S(2)}, u32[]{:S(2)}) collective-permute-start(f32[336,128]{1,0:T(8,128)S(1)} %get-tuple-element.124), channel_id=1, source_target_pairs={{8,0},{16,8},{24,16},{32,24},{40,32},{48,40},{56,48},{72,64},{80,7... | collective-permute-start | bytes 516104 | tf_op jit(solution)/shard_map/ppermute | solution.py:400
  14.4 12.9 %collective-permute-start.2 = (f32[336,128]{1,0:T(8,128)S(1)}, f32[336,128]{1,0:T(8,128)S(1)}, u32[]{:S(2)}, u32[]{:S(2)}) collective-permute-start(f32[336,128]{1,0:T(8,128)S(1)} %get-tuple-element.125), channel_id=1, source_target_pairs={{0,8},{8,16},{16,24},{24,32},{32,40},{40,48},{48,56},{64,72},{72,8... | collective-permute-start | bytes 516104 | tf_op jit(solution)/shard_map/ppermute | solution.py:400
  33.7 1.4 collective-permute-start.4
  34.4 0.7 collective-permute-start.5
  35.1 4.5 %collective-permute-start.7 = (f32[336,128]{1,0:T(8,128)S(1)}, f32[336,128]{1,0:T(8,128)S(1)}, u32[]{:S(2)}, u32[]{:S(2)}) collective-permute-start(f32[336,128]{1,0:T(8,128)S(1)} %get-tuple-element.120), channel_id=1, source_target_pairs={{200,192},{208,200},{216,208},{224,216},{232,224},{240,232},{248,2... | collective-permute-start | bytes 516104 | tf_op jit(solution)/shard_map/ppermute | solution.py:400
  35.8 3.9 %collective-permute-start.6 = (f32[336,128]{1,0:T(8,128)S(1)}, f32[336,128]{1,0:T(8,128)S(1)}, u32[]{:S(2)}, u32[]{:S(2)}) collective-permute-start(f32[336,128]{1,0:T(8,128)S(1)} %get-tuple-element.121), channel_id=1, source_target_pairs={{192,200},{200,208},{208,216},{216,224},{224,232},{232,240},{240,2... | collective-permute-start | bytes 516104 | tf_op jit(solution)/shard_map/ppermute | solution.py:400
  42.3 0.7 collective-permute-start.8
  45.6 1.4 collective-permute-start.9
  46.3 0.7 collective-permute-start.10
  47.0 4.5 %collective-permute-start.12 = (f32[336,128]{1,0:T(8,128)S(1)}, f32[336,128]{1,0:T(8,128)S(1)}, u32[]{:S(2)}, u32[]{:S(2)}) collective-permute-start(f32[336,128]{1,0:T(8,128)S(1)} %get-tuple-element.116), channel_id=1, source_target_pairs={{136,128},{144,136},{152,144},{160,152},{168,160},{176,168},{184,1... | collective-permute-start | bytes 516104 | tf_op jit(solution)/shard_map/ppermute | solution.py:400
  47.7 3.9 %collective-permute-start.11 = (f32[336,128]{1,0:T(8,128)S(1)}, f32[336,128]{1,0:T(8,128)S(1)}, u32[]{:S(2)}, u32[]{:S(2)}) collective-permute-start(f32[336,128]{1,0:T(8,128)S(1)} %get-tuple-element.117), channel_id=1, source_target_pairs={{128,136},{136,144},{144,152},{152,160},{160,168},{168,176},{176,1... | collective-permute-start | bytes 516104 | tf_op jit(solution)/shard_map/ppermute | solution.py:400
  57.5 1.4 collective-permute-start.14
  58.2 0.7 collective-permute-start.15
  58.9 4.5 %collective-permute-start.17 = (f32[336,128]{1,0:T(8,128)S(1)}, f32[336,128]{1,0:T(8,128)S(1)}, u32[]{:S(2)}, u32[]{:S(2)}) collective-permute-start(f32[336,128]{1,0:T(8,128)S(1)} %get-tuple-element.112), channel_id=1, source_target_pairs={{72,64},{80,72},{88,80},{96,88},{104,96},{112,104},{120,112},{73,6... | collective-permute-start | bytes 516104 | tf_op jit(solution)/shard_map/ppermute | solution.py:400
  59.6 3.9 %collective-permute-start.16 = (f32[336,128]{1,0:T(8,128)S(1)}, f32[336,128]{1,0:T(8,128)S(1)}, u32[]{:S(2)}, u32[]{:S(2)}) collective-permute-start(f32[336,128]{1,0:T(8,128)S(1)} %get-tuple-element.113), channel_id=1, source_target_pairs={{64,72},{72,80},{80,88},{88,96},{96,104},{104,112},{112,120},{65,7... | collective-permute-start | bytes 516104 | tf_op jit(solution)/shard_map/ppermute | solution.py:400
  66.1 78.5 %collective-permute-start.18 = (f32[96,1024]{1,0:T(8,128)S(1)}, f32[96,1024]{1,0:T(8,128)S(1)}, u32[]{:S(2)}, u32[]{:S(2)}) collective-permute-start(f32[96,1024]{1,0:T(8,128)S(1)} %shard_map.164), channel_id=1, source_target_pairs={{64,0},{65,1},{66,2},{67,3},{68,4},{69,5},{70,6},{71,7},{72,8},{73... | collective-permute-start | bytes 1179656 | tf_op jit(solution)/shard_map/ppermute | solution.py:473
  154.7 40.6 %all-to-all-start = ((f32[64,16,128]{2,1,0:T(8,128)}), f32[64,16,128]{2,1,0:T(8,128)S(1)}, u32[]{:S(2)}, u32[]{:S(2)}) async-start(f32[64,16,128]{2,1,0:T(8,128)} %bitcast.7), calls=%async_computation | async-start | bytes 1048576 | tf_op jit(solution)/shard_map/all_to_all | solution.py:406
  179.0 23.2 %collective-permute-start.19 = (f32[24,128]{1,0:T(8,128)S(1)}, f32[24,128]{1,0:T(8,128)S(1)}, u32[]{:S(2)}, u32[]{:S(2)}) collective-permute-start(f32[24,128]{1,0:T(8,128)S(1)} %get-tuple-element.67), channel_id=1, source_target_pairs={{0,1},{1,2},{2,3},{3,4},{4,5},{5,6},{6,7},{64,65},{65,66},{66,67},... | collective-permute-start | bytes 36872 | tf_op jit(solution)/shard_map/ppermute | solution.py:400
  182.3 19.9 %collective-permute-start.20 = (f32[24,128]{1,0:T(8,128)S(1)}, f32[24,128]{1,0:T(8,128)S(1)}, u32[]{:S(2)}, u32[]{:S(2)}) collective-permute-start(f32[24,128]{1,0:T(8,128)S(1)} %get-tuple-element.68), channel_id=1, source_target_pairs={{1,0},{2,1},{3,2},{4,3},{5,4},{6,5},{7,6},{65,64},{66,65},{67,66},... | collective-permute-start | bytes 36872 | tf_op jit(solution)/shard_map/ppermute | solution.py:400
  196.2 22.2 %all-to-all-start.1 = ((f32[64,16,128]{2,1,0:T(8,128)}), f32[64,16,128]{2,1,0:T(8,128)S(1)}, u32[]{:S(2)}, u32[]{:S(2)}) async-start(f32[64,16,128]{2,1,0:T(8,128)} %shard_map.169), calls=%async_computation.1 | async-start | bytes 1048576 | tf_op jit(solution)/shard_map/all_to_all | solution.py:408
  202.2 8.7 %collective-permute-start.22 = (f32[336,128]{1,0:T(8,128)S(1)}, f32[336,128]{1,0:T(8,128)S(1)}, u32[]{:S(2)}, u32[]{:S(2)}) collective-permute-start(f32[336,128]{1,0:T(8,128)S(1)} %get-tuple-element.108), channel_id=1, source_target_pairs={{8,0},{16,8},{24,16},{32,24},{40,32},{48,40},{56,48},{72,64},{80,7... | collective-permute-start | bytes 516104 | tf_op jit(solution)/shard_map/ppermute | solution.py:400
  204.6 6.4 %collective-permute-start.21 = (f32[336,128]{1,0:T(8,128)S(1)}, f32[336,128]{1,0:T(8,128)S(1)}, u32[]{:S(2)}, u32[]{:S(2)}) collective-permute-start(f32[336,128]{1,0:T(8,128)S(1)} %get-tuple-element.109), channel_id=1, source_target_pairs={{0,8},{8,16},{16,24},{24,32},{32,40},{40,48},{48,56},{64,72},{72,8... | collective-permute-start | bytes 516104 | tf_op jit(solution)/shard_map/ppermute | solution.py:400
  (13 other events, 67.2 us)

commit v3 on v2

v3 whole, which is shorter than its diff:
```python
import functools

import jax
import jax.numpy as jnp
from jax import lax
from jax.experimental import pallas as pl
from jax.experimental.pallas import tpu as pltpu
from jax.sharding import PartitionSpec as P

KS = 7
TAPS = KS * KS
REACH = KS // 2
EPSILON = 1e-06
LANES = 128
GROUP = 8
ROWS = 8
C = 96
HID = 384
CELLS = ROWS * LANES
FOLD = 24
CHUNK = 256
PAYLOAD_ROWS = 1024
F32 = jnp.float32
BF16 = jnp.bfloat16
CONV_FLOPS = 2 * TAPS * C * CELLS
TILES = ("ty", "tx")


def call(kernel, outs, *operands, scratch=(), flops=0, copied=False):
    whole = pl.BlockSpec(memory_space=pltpu.VMEM)
    specs = [
        pl.BlockSpec(memory_space=pltpu.SMEM if operand.dtype == jnp.int32 else pltpu.HBM if copied else pltpu.VMEM)
        for operand in operands
    ]
    spaces = [pltpu.VMEM(shape, F32) if isinstance(shape, tuple) else shape for shape in scratch]
    return pl.pallas_call(
        kernel,
        out_shape=[jax.ShapeDtypeStruct(shape, F32) for shape in outs],
        in_specs=specs,
        out_specs=[whole] * len(outs),
        scratch_shapes=spaces,
        compiler_params=pltpu.CompilerParams(vmem_limit_bytes=28 * 1024 * 1024),
        cost_estimate=pl.CostEstimate(flops=flops, bytes_accessed=0, transcendentals=0) if flops else None,
    )(*operands)


def roll(value, shift):
    return pltpu.roll(value, shift % LANES, 1)


def lane_of(rows):
    return lax.broadcasted_iota(jnp.int32, (rows, LANES), 1)


def block(row):
    return pl.ds(row * LANES, LANES)


def split(value):
    high = value.astype(BF16)
    low = (value - high.astype(F32)).astype(BF16)
    return high, low


def product(left, right, dims):
    def part(one, two):
        return lax.dot_general(one, two, (dims, ((), ())), preferred_element_type=F32)

    return part(left[0], right[0]) + (part(left[0], right[1]) + part(left[1], right[0]))


ROW_COL = ((1,), (0,))
COL_COL = ((0,), (0,))
ROW_ROW = ((1,), (1,))


def pack_edges(field_ref, right_ref, left_ref):
    lane = lane_of(FOLD)
    for edge, out_ref in ((LANES - REACH, right_ref), (0, left_ref)):
        folded = jnp.zeros((FOLD, LANES), F32)
        for quarter in range(C // FOLD):
            part = pl.ds(quarter * FOLD, FOLD)
            for row in range(ROWS):
                at = 32 * quarter + REACH * row
                moved = roll(field_ref[part, block(row)], at - edge)
                folded = jnp.where((lane >= at) & (lane < at + REACH), moved, folded)
        out_ref[...] = folded


SIDE = 32


def unfold(left, right, quarters, rows):
    lane = lane_of(rows)
    parts = []
    for quarter in range(quarters):
        theirs = roll(left, -32 * quarter)
        parts.append(jnp.where(lane < SIDE, theirs, jnp.where(lane < 2 * SIDE, roll(right, SIDE - 32 * quarter), 0.0)))
    return jnp.concatenate(parts, axis=0)


def shifted_row(row, left, right, lane, distance):
    if distance > 0:
        return roll(jnp.where(lane < distance, right, row), -distance)
    if distance < 0:
        return roll(jnp.where(lane >= LANES + distance, left, row), -distance)
    return row


def with_edges(value, strip, row):
    return value, roll(strip, LANES - REACH - REACH * row), roll(strip, -SIDE - REACH * row)


def tap_of(taps, tap):
    return jnp.broadcast_to(taps[:, tap : tap + 1], (GROUP, LANES))


def take_field(acts_ref, field_ref, right_ref, left_ref):
    for row in range(ROWS):
        field_ref[:, block(row)] = acts_ref[pl.ds(row, C, stride=ROWS), :]
    pack_edges(field_ref, right_ref, left_ref)


def column(row):
    return jnp.broadcast_to(row, (GROUP, row.shape[1])).T[:, :1]


def prepare(*refs):
    count = 8
    sources, outs, held = refs[: count], refs[count : -count - 1], refs[-count - 1 : -1]
    sems = refs[-1]
    copies = [pltpu.make_async_copy(source, target, sems.at[i]) for i, (source, target) in enumerate(zip(sources, held))]
    for copy in copies:
        copy.start()
    for copy in copies:
        copy.wait()
    top_ref, kernel_ref, gain_row, bias_row, w_in_ref, b_in_row, w_out_ref, scale_row = held
    cotan_ref, taps_ref, gain_ref, bias_ref, scale_ref, b_in_ref, w_in_out, w_out_out, w_in_gain_ref, w_out_scale_ref = outs
    for row in range(ROWS):
        cotan_ref[:, block(row)] = top_ref[pl.ds(row, C, stride=ROWS), :]
    taps_ref[:, :TAPS] = kernel_ref[:, 0, :].T
    gain_ref[...] = column(gain_row[...])
    bias_ref[...] = column(bias_row[...])
    scale_ref[...] = column(scale_row[...])
    b_in_ref[...] = column(b_in_row[...])
    w_in_out[...] = w_in_ref[...]
    w_out_out[...] = w_out_ref[...]
    w_in_gain_ref[...] = w_in_ref[...] * gain_ref[...]
    w_out_scale_ref[...] = (w_out_ref[...] * scale_ref[...]).T


STRIP_AT = REACH * C
MESSAGE = (STRIP_AT + C, LANES)


def write_messages(field_ref, strip_ref, odd_ref, a_ref, b_ref):
    odd = odd_ref[0]
    for first, out_ref in (((1 - odd) * (ROWS - REACH), a_ref), (odd * (ROWS - REACH), b_ref)):
        for index in range(REACH):
            lanes = pl.ds(pl.multiple_of((first + index) * LANES, LANES), LANES)
            out_ref[pl.ds(index * C, C), :] = field_ref[:, lanes]
        out_ref[pl.ds(STRIP_AT, C), :] = strip_ref[...]


def outer_rows(group, a_ref, b_ref, odd):
    rows = {}
    for index in range(REACH + 1):
        at = pl.ds(index * C + group, GROUP)
        from_a, from_b = a_ref[at, :], b_ref[at, :]
        rows[index] = (jnp.where(odd, from_a, from_b), jnp.where(odd, from_b, from_a))
    above, below = rows.pop(REACH)
    found = {}
    for index in range(REACH):
        found[index - REACH] = with_edges(rows[index][0], above, ROWS - REACH + index)
        found[ROWS + index] = with_edges(rows[index][1], below, index)
    return found


def own_rows(channels, field_ref, strip_ref):
    strip = strip_ref[channels, :]
    return {row: with_edges(field_ref[channels, block(row)], strip, row) for row in range(ROWS)}


def edges(field_ref, left_ref, right_ref, odd_ref, strip_ref, a_ref, b_ref):
    strip_ref[...] = unfold(left_ref[...], right_ref[...], C // FOLD, FOLD)
    write_messages(field_ref, strip_ref, odd_ref, a_ref, b_ref)


def tap_index(a, b, flipped):
    tap = a * KS + b
    return TAPS - 1 - tap if flipped else tap


def conv_own(flipped, *refs):
    start_ref = refs[0] if flipped else None
    field_ref, strip_ref, taps_ref, out_ref = refs[-4:]
    lane = lane_of(GROUP)

    def conv_group(index, carry):
        channels = pl.ds(pl.multiple_of(index * GROUP, GROUP), GROUP)
        taps = taps_ref[channels, :]
        rows = own_rows(channels, field_ref, strip_ref)
        if flipped:
            sums = [start_ref[channels, block(row)] for row in range(ROWS)]
        else:
            sums = [jnp.zeros((GROUP, LANES), F32)] * ROWS
        for b in range(KS):
            moved = [shifted_row(*rows[row], lane, b - REACH) for row in range(ROWS)]
            for a in range(KS):
                weight = tap_of(taps, tap_index(a, b, flipped))
                for row in range(ROWS):
                    if 0 <= row + a - REACH < ROWS:
                        sums[row] = sums[row] + weight * moved[row + a - REACH]
        for row in range(ROWS):
            out_ref[channels, block(row)] = sums[row]
        return carry

    lax.fori_loop(0, C // GROUP, conv_group, 0)


def conv_edges(flipped, own_ref, a_ref, b_ref, odd_ref, taps_ref, put):
    odd = odd_ref[0] == 1
    lane = lane_of(GROUP)

    def conv_group(index, carry):
        group = pl.multiple_of(index * GROUP, GROUP)
        channels = pl.ds(group, GROUP)
        taps = taps_ref[channels, :]
        rows = outer_rows(group, a_ref, b_ref, odd)
        sums = [own_ref[channels, block(row)] for row in range(ROWS)]
        for b in range(KS):
            moved = {at: shifted_row(*row, lane, b - REACH) for at, row in rows.items()}
            for a in range(KS):
                if a == REACH:
                    continue
                weight = tap_of(taps, tap_index(a, b, flipped))
                for row in range(ROWS):
                    if row + a - REACH in moved:
                        sums[row] = sums[row] + weight * moved[row + a - REACH]
        put(group, sums)
        return carry

    lax.fori_loop(0, C // GROUP, conv_group, 0)


def forward(
    own_ref, a_ref, b_ref, odd_ref, taps_ref, gain_ref, bias_ref, w_in_ref, b_in_ref,
    normed_ref, inv_ref, slope_ref, hidden_ref,
):
    def put(group, sums):
        for row in range(ROWS):
            normed_ref[pl.ds(group, GROUP), block(row)] = sums[row]

    conv_edges(False, own_ref, a_ref, b_ref, odd_ref, taps_ref, put)
    w_in = split(w_in_ref[...])
    for start in range(0, CELLS, CHUNK):
        cells = pl.ds(start, CHUNK)
        conv_out = normed_ref[:, cells]
        centred = conv_out - jnp.mean(conv_out, axis=0, keepdims=True)
        inv = lax.rsqrt(jnp.mean(centred * centred, axis=0, keepdims=True) + EPSILON)
        normed = centred * inv
        normed_ref[:, cells] = normed
        inv_ref[:, cells] = inv
        lifted = normed * gain_ref[...] + bias_ref[...]
        pre_act = product(w_in, split(lifted), COL_COL) + b_in_ref[...]
        gate = 0.5 * (1.0 + lax.erf(pre_act * 0.7071067811865476))
        hidden_ref[:, cells] = pre_act * gate
        slope_ref[:, cells] = gate + pre_act * jnp.exp(-0.5 * pre_act * pre_act) * 0.3989422804014327


SAVED_SIDE = (HID // 4 + FOLD + GROUP, LANES)


def pack_saved(normed_ref, inv_ref, slope_ref, right_ref, left_ref):
    for edge, out_ref in ((LANES - REACH, right_ref), (0, left_ref)):
        at = 0
        for source_ref, rows, quarters in ((slope_ref, HID // 4, 4), (normed_ref, FOLD, 4), (inv_ref, 1, 1)):
            tall = max(rows, GROUP)
            lane = lane_of(tall)
            folded = jnp.zeros((tall, LANES), F32)
            for quarter in range(quarters):
                part = pl.ds(quarter * rows, rows)
                for row in range(ROWS):
                    to = 32 * quarter + REACH * row
                    value = jnp.broadcast_to(source_ref[part, block(row)], (tall, LANES))
                    folded = jnp.where((lane >= to) & (lane < to + REACH), roll(value, to - edge), folded)
            out_ref[pl.ds(at, tall), :] = folded
            at += tall


def unpack_saved(left_ref, right_ref, normed_ref, inv_ref, slope_ref):
    at = 0
    for out_ref, rows, quarters in ((slope_ref, HID // 4, 4), (normed_ref, FOLD, 4), (inv_ref, GROUP, 1)):
        part = pl.ds(at, rows)
        out_ref[...] = unfold(left_ref[part, :], right_ref[part, :], quarters, rows)
        at += rows


def grad_at(cotan, w_out, w_in, normed, inv, slope):
    grad_pre = product(w_out, split(cotan), ROW_COL) * slope
    grad_normed = product(w_in, split(grad_pre), ROW_COL)
    mean = jnp.mean(grad_normed, axis=0, keepdims=True)
    along = jnp.mean(grad_normed * normed, axis=0, keepdims=True)
    return grad_pre, inv * (grad_normed - mean - normed * along)


def step_tile(cotan_refs, saved, grad_ref, keep):
    normed_ref, inv_ref, slope_ref, w_in_gain_ref, w_out_scale_ref = saved
    w_out = split(w_out_scale_ref[...])
    w_in = split(w_in_gain_ref[...])
    for start in range(0, CELLS, CHUNK):
        cells = pl.ds(start, CHUNK)
        cotan = sum(ref[:, cells] for ref in cotan_refs)
        grad_pre, grad = grad_at(cotan, w_out, w_in, normed_ref[:, cells], inv_ref[:, cells], slope_ref[:, cells])
        keep(cells, cotan, grad_pre)
        grad_ref[:, cells] = grad
    return w_out, w_in


def ignore(cells, cotan, grad_pre):
    pass


def first_step(cotan_ref, *refs):
    saved, (grad_ref, right_ref, left_ref) = refs[:5], refs[5:]
    step_tile((cotan_ref,), saved, grad_ref, ignore)
    pack_edges(grad_ref, right_ref, left_ref)


def step_sides(lefts, rights, weights, strips):
    left, right = sum(ref[...] for ref in lefts), sum(ref[...] for ref in rights)
    normed_ref, inv_ref, slope_ref = strips
    cotan = unfold(left, right, C // FOLD, FOLD)
    return grad_at(cotan, *weights, normed_ref[...], inv_ref[:1, :], slope_ref[...])[1]


def middle_step(cotan_ref, from_left, from_right, odd_ref, *refs):
    saved, strips, (grad_ref, strip_ref, a_ref, b_ref) = refs[:5], refs[5:8], refs[8:]
    weights = step_tile((cotan_ref,), saved, grad_ref, ignore)
    strip_ref[...] = step_sides((from_left,), (from_right,), weights, strips)
    write_messages(grad_ref, strip_ref, odd_ref, a_ref, b_ref)


def last_step(count, *refs):
    cotans, lefts, rights = refs[:count], refs[count : 2 * count - 1], refs[2 * count - 1 : 3 * count - 2]
    first_strip, odd_ref = refs[3 * count - 2 : 3 * count]
    refs = refs[3 * count :]
    saved, strips = refs[:5], refs[5:8]
    grad_ref, strip_ref, a_ref, b_ref, cotan_ref, grad_pre_ref = refs[8:]

    def keep(cells, cotan, grad_pre):
        cotan_ref[:, cells] = cotan
        grad_pre_ref[:, cells] = grad_pre

    weights = step_tile(cotans, saved, grad_ref, keep)
    strip_ref[...] = step_sides(lefts, rights, weights, strips) + first_strip[...]
    write_messages(grad_ref, strip_ref, odd_ref, a_ref, b_ref)


def finish(own_ref, a_ref, b_ref, odd_ref, taps_ref, out_ref, right_ref, left_ref):
    def put(group, sums):
        for row in range(ROWS):
            out_ref[pl.ds(group, GROUP), block(row)] = sums[row]

    conv_edges(True, own_ref, a_ref, b_ref, odd_ref, taps_ref, put)
    pack_edges(out_ref, right_ref, left_ref)


def last_finish(own_ref, a_ref, b_ref, odd_ref, taps_ref, out_ref):
    def put(group, sums):
        for row in range(ROWS):
            out_ref[pl.ds(group * ROWS + row, GROUP, stride=ROWS), :] = sums[row]

    conv_edges(True, own_ref, a_ref, b_ref, odd_ref, taps_ref, put)


LIFT_ROWS = C + GROUP
OUT_AT = 0
IN_AT = OUT_AT + C * HID // LANES
TAPS_AT = IN_AT + LIFT_ROWS * HID // LANES
USED_ROWS = TAPS_AT + C


def parameter_terms(
    field_ref, strip_ref, a_ref, b_ref, odd_ref, grad_ref, cotan_ref, hidden_ref, normed_ref, grad_pre_ref,
    payload_ref,
):
    odd = odd_ref[0] == 1
    lane = lane_of(GROUP)

    def taps_group(index, carry):
        group = pl.multiple_of(index * GROUP, GROUP)
        found = outer_rows(group, a_ref, b_ref, odd) | own_rows(pl.ds(group, GROUP), field_ref, strip_ref)
        rows = [found[row] for row in sorted(found)]
        grads = [grad_ref[pl.ds(group, GROUP), block(row)] for row in range(ROWS)]
        result = jnp.zeros((GROUP, LANES), F32)
        for b in range(KS):
            moved = [shifted_row(*row, lane, b - REACH) for row in rows]
            for a in range(KS):
                terms = [grads[row] * moved[row + a] for row in range(ROWS)]
                while len(terms) > 1:
                    terms = [one + two for one, two in zip(terms[0::2], terms[1::2])]
                total = jnp.sum(terms[0], axis=1, keepdims=True)
                result = jnp.where(lane == a * KS + b, total, result)
        payload_ref[pl.ds(TAPS_AT + group, GROUP), :] = result
        return carry

    lax.fori_loop(0, C // GROUP, taps_group, 0)
    grad_w_out = product(split(cotan_ref[...]), split(hidden_ref[...]), ROW_ROW)
    ones = jnp.where(lax.broadcasted_iota(jnp.int32, (GROUP, CELLS), 0) == 0, 1.0, 0.0)
    lifted = jnp.concatenate([normed_ref[...], ones], axis=0)
    grad_w_in = product(split(lifted), split(grad_pre_ref[...]), ROW_ROW)
    for part in range(HID // LANES):
        payload_ref[pl.ds(OUT_AT + part * C, C), :] = grad_w_out[:, part * LANES : (part + 1) * LANES]
        payload_ref[pl.ds(IN_AT + part * LIFT_ROWS, LIFT_ROWS), :] = grad_w_in[:, part * LANES : (part + 1) * LANES]
    payload_ref[pl.ds(USED_ROWS, PAYLOAD_ROWS - USED_ROWS), :] = jnp.zeros((PAYLOAD_ROWS - USED_ROWS, LANES), F32)


def sum_shares(shares_ref, out_ref):
    devices, rows = out_ref.shape[0], out_ref.shape[1]

    def add(device, total):
        return total + shares_ref[device]

    total = lax.fori_loop(1, devices, add, shares_ref[0], unroll=7)

    def put(device, carry):
        out_ref[device] = total
        return carry

    lax.fori_loop(0, devices, put, 0, unroll=8)


def parameter_grads(
    payload_ref, gain_ref, bias_ref, w_in_ref, w_out_ref, scale_ref,
    kernel_out, gain_out, bias_out, w_in_out, b_in_out, w_out_out, scale_out,
):
    kernel_out[:, 0, :] = payload_ref[pl.ds(TAPS_AT, C), :].T[:TAPS, :]
    scale = scale_ref[...]
    sums = [jnp.zeros((C, 1), F32)] * 3
    for part in range(HID // LANES):
        hidden = pl.ds(part * LANES, LANES)
        grad_out = payload_ref[pl.ds(OUT_AT + part * C, C), :]
        w_out_out[:, hidden] = grad_out * scale
        at = IN_AT + part * LIFT_ROWS
        grad_in = payload_ref[pl.ds(at, C), :]
        grad_b = payload_ref[pl.ds(at + C, 1), :]
        b_in_out[:, hidden] = grad_b
        w_in_out[:, hidden] = grad_in * gain_ref[...] + bias_ref[...] * grad_b
        w_in = w_in_ref[:, hidden]
        terms = (w_in * grad_in, w_in * grad_b, w_out_ref[:, hidden] * grad_out)
        sums = [total + jnp.sum(term, axis=1, keepdims=True) for total, term in zip(sums, terms)]
    for total, out in zip(sums, (gain_out, bias_out, scale_out)):
        out[...] = jnp.broadcast_to(total, (C, LANES)).T[:1, :]


def pairs(axis, sections, odd_pairs):
    size = lax.axis_size(axis)
    routes = []
    for section in sections:
        for tile in range(1 if odd_pairs else 0, size - 1, 2):
            here = section * size + tile
            routes += [(here, here + 1), (here + 1, here)]
    return routes


def swap_rows(message_a, message_b, sections):
    axes = ("section", "ty")
    return (
        lax.ppermute(message_a, axes, pairs("ty", sections, False)),
        lax.ppermute(message_b, axes, pairs("ty", sections, True)),
    )


def to_sides(to_right, to_left, sections, back=0):
    size = lax.axis_size("tx")
    right = [(s * size + i, (s - back) * size + i + 1) for s in sections for i in range(size - 1)]
    left = [(s * size + i + 1, (s - back) * size + i) for s in sections for i in range(size - 1)]
    axes = ("section", "tx")
    return lax.ppermute(to_right, axes, right), lax.ppermute(to_left, axes, left)


def sum_over_tiles(payload):
    devices = lax.axis_size(TILES)
    rows = PAYLOAD_ROWS // devices
    shares = lax.all_to_all(payload.reshape(devices, rows, LANES), TILES, 0, 0)
    (copies,) = call(sum_shares, [(devices, rows, LANES)], shares)
    return lax.all_to_all(copies, TILES, 0, 0).reshape(PAYLOAD_ROWS, LANES)


def on_device(acts, top_grad, kernel, ln_gain, ln_bias, w_in, b_in, w_out, layer_scale):
    sections = lax.axis_size("section")
    every = range(sections)
    is_last = (lax.axis_index("section") == sections - 1).astype(F32)
    odd = lax.rem(lax.axis_index("ty"), 2).astype(jnp.int32).reshape(1)
    field_shape, side, wide, hidden_shape = ((C, CELLS), (FOLD, LANES), (C, LANES), (HID, CELLS))
    edge_outs = [wide, MESSAGE, MESSAGE]
    acts_rows, top_rows = (acts.reshape(C * ROWS, LANES), top_grad.reshape(C * ROWS, LANES))

    field, to_right, to_left = call(take_field, [field_shape, side, side], acts_rows)
    left, right = to_sides(to_right, to_left, every)
    parameters = (
        top_rows, jnp.transpose(kernel, (1, 0, 2)), ln_gain, ln_bias, w_in[0], b_in, w_out[0].T, layer_scale,
    )
    cotan, taps, gain, shift_bias, scale, bias_in, weight_in, weight_out, w_in_gain, w_out_scale = call(
        prepare,
        [field_shape, wide, (C, 1), (C, 1), (C, 1), (HID, 1), (C, HID), (C, HID), (C, HID), (HID, C)],
        *parameters, scratch=[p.shape for p in parameters] + [pltpu.SemaphoreType.DMA((len(parameters),))], copied=True,
    )
    strip, message_a, message_b = call(edges, edge_outs, field, left, right, odd)
    from_a, from_b = swap_rows(message_a, message_b, every)
    (own,) = call(functools.partial(conv_own, False), [field_shape], field, strip, taps, flops=CONV_FLOPS)
    around = (field, strip, from_a, from_b, odd)
    normed, inv, slope, hidden = call(
        forward,
        [field_shape, (1, CELLS), hidden_shape, hidden_shape],
        own, from_a, from_b, odd, taps, gain, shift_bias, weight_in, bias_in,
    )
    saved = (normed, inv, slope, w_in_gain, w_out_scale)

    cotan = cotan * is_last
    cotans, lefts, rights = [cotan], [], []
    strips = ()
    for section in reversed(every):
        only = (section,) if section else every
        if section == sections - 1:
            grad, to_right, to_left = call(first_step, [field_shape, side, side], cotan, *saved)
            grad_left, grad_right = to_sides(to_right, to_left, only)
            tile, grad = lax.optimization_barrier((saved[:3], grad))
            saved_right, saved_left = call(pack_saved, [SAVED_SIDE, SAVED_SIDE], *tile)
            grad_left, saved_right, saved_left = lax.optimization_barrier((grad_left, saved_right, saved_left))
            saved_sides = to_sides(saved_right, saved_left, range(sections - 1))
            first_strip, message_a, message_b = call(edges, edge_outs, grad, grad_left, grad_right, odd)
            grad_strip = first_strip
            strips = call(unpack_saved, [wide, (GROUP, LANES), (HID, LANES)], *saved_sides)
        elif section:
            grad, grad_strip, message_a, message_b = call(
                middle_step, [field_shape] + edge_outs, cotan, lefts[-1], rights[-1], odd, *saved, *strips
            )
        else:
            grad, grad_strip, message_a, message_b, cotan, grad_pre = call(
                functools.partial(last_step, len(cotans)), [field_shape] + edge_outs + [field_shape, hidden_shape],
                *cotans, *lefts, *rights, first_strip, odd, *saved, *strips,
            )
            (payload,) = call(
                parameter_terms, [(PAYLOAD_ROWS, LANES)],
                *around, grad, cotan, hidden, normed, grad_pre, flops=4 * CONV_FLOPS,
            )
        grad_a, grad_b = swap_rows(message_a, message_b, only)
        (own,) = call(
            functools.partial(conv_own, True), [field_shape], cotan, grad, grad_strip, taps, flops=CONV_FLOPS
        )
        if section:
            cotan, to_right, to_left = call(finish, [field_shape, side, side], own, grad_a, grad_b, odd, taps)
            cotan = lax.ppermute(cotan, "section", [(section, section - 1)])
            from_left, from_right = to_sides(to_right, to_left, only, 1)
            cotans.append(cotan)
            lefts.append(from_left)
            rights.append(from_right)
    (input_grad,) = call(last_finish, [(C * ROWS, LANES)], own, grad_a, grad_b, odd, taps)
    payload = sum_over_tiles(payload)
    grad_kernel, grad_gain, grad_bias, grad_w_in, grad_b_in, grad_w_out, grad_scale = call(
        parameter_grads,
        [(TAPS, 1, C), (1, C), (1, C), (C, HID), (1, HID), (C, HID), (1, C)],
        payload, gain, shift_bias, weight_in, weight_out, scale,
    )
    return (
        input_grad.reshape(1, 1, C, ROWS, LANES),
        jnp.transpose(grad_kernel, (1, 0, 2)),
        grad_gain,
        grad_bias,
        grad_w_in[None],
        grad_b_in,
        grad_w_out.T[None],
        grad_scale,
    )


def solution(mesh):
    placed = (
        P("section", None, None, "ty", "tx"),
        P(None, None, "ty", "tx"),
        P("section", None, None),
        P("section", None),
        P("section", None),
        P("section", None, None),
        P("section", None),
        P("section", None, None),
        P("section", None),
    )
    return jax.shard_map(
        on_device,
        mesh=mesh,
        in_specs=placed,
        out_specs=(
            P("section", None, None, "ty", "tx"),
            P("section", None, None),
            P("section", None),
            P("section", None),
            P("section", None, None),
            P("section", None),
            P("section", None, None),
            P("section", None),
        ),
        check_vma=False,
    )
```

time: 220 us -> 199 us (0.905)
  blocking collectives: 0 us -> 30.8 us
  starting transfers between devices: 63.5 us -> 36.1 us
  waiting for transfers between devices: 95.9 us -> 68.7 us
  Pallas kernels: 51.3 us -> 54.1 us
    ppermute x3, waiting for transfers between devices: 77.1 us -> 0.01 us  [on_device(): cotan = lax.ppermute(cotan, 'section', [(section, section - 1)])]
    ppermute x20 -> x22, waiting for transfers between devices: 3.11 us -> 64.8 us  [the longest x6 62 us: to_sides(): lax.ppermute(to_left, axes, left)]
    all_to_all x0 -> x1, blocking collectives: none -> 30.8 us  [sum_over_tiles(): shares = lax.all_to_all(payload.reshape(devices, rows, LANES), TILES, 0, 0)]
    all_to_all x1 -> x0, starting transfers between devices: 24.3 us -> none  [sum_over_tiles(): shares = lax.all_to_all(payload.reshape(devices, rows, LANES), TILES, 0, 0)]
    all_to_all x1 -> x0, waiting for transfers between devices: 11.7 us -> none  [sum_over_tiles(): shares = lax.all_to_all(payload.reshape(devices, rows, LANES), TILES, 0, 0)]
    pallas_call x19 -> x23, Pallas kernels: 51.3 us -> 54.1 us  [call(): pl.pallas_call(kernel, out_shape=[jax.ShapeDtypeStruct(shape, F32) for sh...]
    ppermute x20 -> x22, starting transfers between devices: 30.5 us -> 28.7 us  [the longest x6 10.9 us: to_sides(): lax.ppermute(to_right, axes, right)]
    unnamed x44 -> x18, local copies, waits for them, and re-layouts: 7.4 us -> 7.18 us
  transfers between devices with their start and end apart: 25 -> 26, of which waited for: 4 -> 5; matrix products, arithmetic and copies ran while one was open for 0% -> 0% of each run, Pallas kernels for 9% -> 11%
where the time goes in v3:
time: 199 us; the launch traced here: 198 us
  waiting for transfers between devices  68.7 us (35%)
  Pallas kernels  54.1 us (27%)
  starting transfers between devices  36.1 us (18%)
  blocking collectives  30.8 us (15%)
  local copies, waits for them, and re-layouts  7.18 us (4%)
    ppermute x6, waiting for transfers between devices, to_sides(): lax.ppermute(to_left, axes, left)  62 us
    pallas_call x23, Pallas kernels, call(): pl.pallas_call(kernel, out_shape=[jax.ShapeDtypeStruct(shape, F32) for sh...  54.1 us
    all_to_all x1, blocking collectives, sum_over_tiles(): shares = lax.all_to_all(payload.reshape(devices, rows, LANES), TILES, 0, 0)  30.8 us
    ppermute x6, starting transfers between devices, to_sides(): lax.ppermute(to_right, axes, right)  10.9 us
    ppermute x5, starting transfers between devices, swap_rows(): lax.ppermute(message_b, axes, pairs('ty', sections, True))  8.36 us
    unnamed x18, local copies, waits for them, and re-layouts  7.18 us
    ppermute x6, starting transfers between devices, to_sides(): lax.ppermute(to_left, axes, left)  5.86 us
    all_to_all x1, starting transfers between devices, sum_over_tiles(): return lax.all_to_all(copies, TILES, 0, 0).reshape(PAYLOAD_ROWS, LANES)  4.46 us
  transfers between devices with their start and end apart: 26, of which 5 were waited for; matrix products, arithmetic and copies ran while one was open for 0% of the time, Pallas kernels for 11%

profile of v3, /device:TPU:1, one launch (start us, length us, event | category | flops | bytes accessed | tf_op | source)
XLA Modules:
  0.0 197.9 jit_solution(14125190679281485877)
XLA Ops:
  1.9 3.9 %collective-permute-start = (f32[24,128]{1,0:T(8,128)S(1)}, f32[24,128]{1,0:T(8,128)S(1)}, u32[]{:S(2)}, u32[]{:S(2)}) collective-permute-start(f32[24,128]{1,0:T(8,128)S(1)} %get-tuple-element.78), channel_id=1, source_target_pairs={{0,1},{1,2},{2,3},{3,4},{4,5},{5,6},{6,7},{64,65},{65,66},{66,67},... | collective-permute-start | bytes 36872 | tf_op jit(solution)/shard_map/ppermute | solution.py:480
  15.8 3.1 %collective-permute-start.3 = (f32[384,128]{1,0:T(8,128)S(1)}, f32[384,128]{1,0:T(8,128)S(1)}, u32[]{:S(2)}, u32[]{:S(2)}) collective-permute-start(f32[384,128]{1,0:T(8,128)S(1)} %get-tuple-element.83), channel_id=1, source_target_pairs={{8,16},{16,8},{24,32},{32,24},{40,48},{48,40},{72,80},{80,72},{88,... | collective-permute-start | bytes 589832 | tf_op jit(solution)/shard_map/ppermute | solution.py:471
  18.9 3.1 %shard_map.155.own_ref = f32[96,1024]{1,0:T(8,128)S(1)} custom-call(f32[96,1024]{1,0:T(8,128)S(1)} %get-tuple-element.77.field_ref.refs_0_, f32[96,128]{1,0:T(8,128)S(1)} %get-tuple-element.80.refs_1_.strip_ref, f32[96,128]{1,0:T(8,128)S(1)} %get-tuple-element.81.refs_2_.taps_ref.refs_3_), custom_call_target="tpu_custom_call" | custom-call | flops 9633792 | tf_op jit(solution)/shard_map/pallas_call | solution.py:36
  22.8 3.8 %shard_map.156 = (f32[96,1024]{1,0:T(8,128)S(1)}, f32[1,1024]{1,0:T(1,128)S(1)}, f32[384,1024]{1,0:T(8,128)S(1)}, f32[384,1024]{1,0:T(8,128)S(1)}) custom-call(f32[96,1024]{1,0:T(8,128)S(1)} %shard_map.155.own_ref, f32[384,128]{1,0:T(8,128)S(1)} %collective-permute-done.2.a_ref, f32[384,128]{1,0:T(8,128)S(1)} %collective-permute-done.3.b_ref, ...), custom_call_target="tpu_custom_call" | custom-call | tf_op jit(solution)/shard_map/pallas_call | solution.py:36
  26.6 2.5 %shard_map.157 = (f32[96,1024]{1,0:T(8,128)S(1)}, f32[24,128]{1,0:T(8,128)S(1)}, f32[24,128]{1,0:T(8,128)S(1)}) custom-call(f32[96,1024]{1,0:T(8,128)S(1)} %broadcast_multiply_fusion.cotan_ref.refs_0_, f32[96,1024]{1,0:T(8,128)S(1)} %get-tuple-element.96.refs_0_.normed_ref.refs_12_, f32[1,1024]{1,0:T(1,128)S(1)} %get-tuple-element.97.refs_1_.inv_ref.refs_13_, ...), custom_call_target="tpu_custom_call" | custom-call | tf_op jit(solution)/shard_map/pallas_call | solution.py:36
  33.1 3.1 %shard_map.160.own_ref = f32[96,1024]{1,0:T(8,128)S(1)} custom-call(f32[96,1024]{1,0:T(8,128)S(1)} %broadcast_multiply_fusion.cotan_ref.refs_0_, f32[96,1024]{1,0:T(8,128)S(1)} %get-tuple-element.94.field_ref.refs_1_, f32[96,128]{1,0:T(8,128)S(1)} %get-tuple-element.103.refs_2_.refs_10_, f32[96,128]{1,0:T(8,128)S(1)} %get-tuple-element.81.refs_2_.taps_ref.refs_3_), custom_call_target="tpu_custom_call" | custom-call | flops 9633792 | tf_op jit(solution)/shard_map/pallas_call | solution.py:36
  36.2 2.9 %shard_map.161 = (f32[96,1024]{1,0:T(8,128)S(1)}, f32[24,128]{1,0:T(8,128)S(1)}, f32[24,128]{1,0:T(8,128)S(1)}) custom-call(f32[96,1024]{1,0:T(8,128)S(1)} %shard_map.160.own_ref, f32[384,128]{1,0:T(8,128)S(1)} %collective-permute-done.6.a_ref, f32[384,128]{1,0:T(8,128)S(1)} %collective-permute-done.7.b_ref, s32[1]{0:T(128)} %bitcast.6.odd_ref.refs_11_, ...), custom_call_target="tpu_custom_call" | custom-call | tf_op jit(solution)/shard_map/pallas_call | solution.py:36
  39.9 4.3 %collective-permute-start.11 = (f32[128,128]{1,0:T(8,128)S(1)}, f32[128,128]{1,0:T(8,128)S(1)}, u32[]{:S(2)}, u32[]{:S(2)}) collective-permute-start(f32[128,128]{1,0:T(8,128)S(1)} %get-tuple-element.109), channel_id=1, source_target_pairs={{0,1},{1,2},{2,3},{3,4},{4,5},{5,6},{6,7},{64,65},{65,66},{66,67},... | collective-permute-start | bytes 196616 | tf_op jit(solution)/shard_map/ppermute | solution.py:480
  46.8 2.6 %collective-permute-done.12.right_ref = f32[128,128]{1,0:T(8,128)S(1)} collective-permute-done((f32[128,128]{1,0:T(8,128)S(1)}, f32[128,128]{1,0:T(8,128)S(1)}, u32[]{:S(2)}, u32[]{:S(2)}) %collective-permute-start.12) | collective-permute-done | bytes 65568 | tf_op jit(solution)/shard_map/ppermute | solution.py:480
  49.6 2.8 %shard_map.163 = (f32[96,1024]{1,0:T(8,128)S(1)}, f32[96,128]{1,0:T(8,128)S(1)}, f32[384,128]{1,0:T(8,128)S(1)}, f32[384,128]{1,0:T(8,128)S(1)}) custom-call(f32[96,1024]{1,0:T(8,128)S(1)} %collective-permute-done.8.cotan_ref.refs_0_.refs_1_, f32[24,128]{1,0:T(8,128)S(1)} %collective-permute-done.9.from_left.refs_4_, ...), custom_call_target="tpu_custom_call" | custom-call | tf_op jit(solution)/shard_map/pallas_call | solution.py:36
  53.8 3.1 %shard_map.164.own_ref = f32[96,1024]{1,0:T(8,128)S(1)} custom-call(f32[96,1024]{1,0:T(8,128)S(1)} %collective-permute-done.8.cotan_ref.refs_0_.refs_1_, f32[96,1024]{1,0:T(8,128)S(1)} %get-tuple-element.114.refs_1_, f32[96,128]{1,0:T(8,128)S(1)} %get-tuple-element.115.refs_2_, f32[96,128]{1,0:T(8,128)S(1)} %get-tuple-element.81.refs_2_.taps_ref.refs_3_), custom_call_target="tpu_custom_call" | custom-call | flops 9633792 | tf_op jit(solution)/shard_map/pallas_call | solution.py:36
  56.9 2.9 %shard_map.165 = (f32[96,1024]{1,0:T(8,128)S(1)}, f32[24,128]{1,0:T(8,128)S(1)}, f32[24,128]{1,0:T(8,128)S(1)}) custom-call(f32[96,1024]{1,0:T(8,128)S(1)} %shard_map.164.own_ref, f32[384,128]{1,0:T(8,128)S(1)} %collective-permute-done.13.a_ref, f32[384,128]{1,0:T(8,128)S(1)} %collective-permute-done.14.b_ref, s32[1]{0:T(128)} %bitcast.6.odd_ref.refs_11_, ...), custom_call_target="tpu_custom_call" | custom-call | tf_op jit(solution)/shard_map/pallas_call | solution.py:36
  61.9 2.8 %shard_map.166 = (f32[96,1024]{1,0:T(8,128)S(1)}, f32[96,128]{1,0:T(8,128)S(1)}, f32[384,128]{1,0:T(8,128)S(1)}, f32[384,128]{1,0:T(8,128)S(1)}) custom-call(f32[96,1024]{1,0:T(8,128)S(1)} %collective-permute-done.15.cotan_ref.refs_0_.refs_2_, f32[24,128]{1,0:T(8,128)S(1)} %collective-permute-done.16.from_left.refs_5_, ...), custom_call_target="tpu_custom_call" | custom-call | tf_op jit(solution)/shard_map/pallas_call | solution.py:36
  66.1 3.1 %shard_map.167.own_ref = f32[96,1024]{1,0:T(8,128)S(1)} custom-call(f32[96,1024]{1,0:T(8,128)S(1)} %collective-permute-done.15.cotan_ref.refs_0_.refs_2_, f32[96,1024]{1,0:T(8,128)S(1)} %get-tuple-element.121.refs_1_, f32[96,128]{1,0:T(8,128)S(1)} %get-tuple-element.122.refs_2_, f32[96,128]{1,0:T(8,128)S(1)} %get-tuple-element.81.refs_2_.taps_ref.refs_3_), custom_call_target="tpu_custom_call" | custom-call | flops 9633792 | tf_op jit(solution)/shard_map/pallas_call | solution.py:36
  69.2 2.9 %shard_map.168 = (f32[96,1024]{1,0:T(8,128)S(1)}, f32[24,128]{1,0:T(8,128)S(1)}, f32[24,128]{1,0:T(8,128)S(1)}) custom-call(f32[96,1024]{1,0:T(8,128)S(1)} %shard_map.167.own_ref, f32[384,128]{1,0:T(8,128)S(1)} %collective-permute-done.18.a_ref, f32[384,128]{1,0:T(8,128)S(1)} %collective-permute-done.19.b_ref, s32[1]{0:T(128)} %bitcast.6.odd_ref.refs_11_, ...), custom_call_target="tpu_custom_call" | custom-call | tf_op jit(solution)/shard_map/pallas_call | solution.py:36
  75.6 59.4 %collective-permute-done.22.refs_9_ = f32[24,128]{1,0:T(8,128)S(1)} collective-permute-done((f32[24,128]{1,0:T(8,128)S(1)}, f32[24,128]{1,0:T(8,128)S(1)}, u32[]{:S(2)}, u32[]{:S(2)}) %collective-permute-start.22) | collective-permute-done | bytes 12320 | tf_op jit(solution)/shard_map/ppermute | solution.py:480
  135.0 2.8 %shard_map.169 = (f32[96,1024]{1,0:T(8,128)S(1)}, f32[96,128]{1,0:T(8,128)S(1)}, f32[384,128]{1,0:T(8,128)S(1)}, f32[384,128]{1,0:T(8,128)S(1)}, f32[96,1024]{1,0:T(8,128)S(1)}, /*index=5*/f32[384,1024]{1,0:T(8,128)S(1)}) custom-call(f32[96,1024]{1,0:T(8,128)S(1)} %broadcast_multiply_fusion.cotan_ref.refs_0_, ...), custom_call_target="tpu_custom_call" | custom-call | tf_op jit(solution)/shard_map/pallas_call | solution.py:36
  137.9 6.6 %shard_map.172 = f32[1024,128]{1,0:T(8,128)S(1)} custom-call(f32[96,1024]{1,0:T(8,128)S(1)} %get-tuple-element.77.field_ref.refs_0_, f32[96,128]{1,0:T(8,128)S(1)} %get-tuple-element.80.refs_1_.strip_ref, f32[384,128]{1,0:T(8,128)S(1)} %collective-permute-done.2.a_ref, f32[384,128]{1,0:T(8,128)S(1)} %collective-permute-done.3.b_ref, ...), custom_call_target="tpu_custom_call" | custom-call | flops 38535168 | tf_op jit(solution)/shard_map/pallas_call | solution.py:36
  144.4 30.8 %all_to_all.10.shares_ref = f32[64,16,128]{2,1,0:T(8,128)S(1)} all-to-all(f32[64,16,128]{2,1,0:T(8,128)S(1)} %bitcast.16), channel_id=1, replica_groups=mesh['section'=4,'ty'=8,'tx'=8] {'ty','tx'}, dimensions={0} | all-to-all | bytes 1048576 | tf_op jit(solution)/shard_map/all_to_all | solution.py:486
  176.1 4.5 %all-to-all-start.1 = ((f32[64,16,128]{2,1,0:T(8,128)}), f32[64,16,128]{2,1,0:T(8,128)S(1)}, u32[]{:S(2)}, u32[]{:S(2)}) async-start(f32[64,16,128]{2,1,0:T(8,128)} %shard_map.173), calls=%async_computation.1 | async-start | bytes 1048576 | tf_op jit(solution)/shard_map/all_to_all | solution.py:488
  181.2 3.2 %collective-permute-start.24 = (f32[384,128]{1,0:T(8,128)S(1)}, f32[384,128]{1,0:T(8,128)S(1)}, u32[]{:S(2)}, u32[]{:S(2)}) collective-permute-start(f32[384,128]{1,0:T(8,128)S(1)} %get-tuple-element.132), channel_id=1, source_target_pairs={{8,16},{16,8},{24,32},{32,24},{40,48},{48,40},{72,80},{80,72},{88,... | collective-permute-start | bytes 589832 | tf_op jit(solution)/shard_map/ppermute | solution.py:471
  184.4 3.1 %shard_map.170.own_ref = f32[96,1024]{1,0:T(8,128)S(1)} custom-call(f32[96,1024]{1,0:T(8,128)S(1)} %get-tuple-element.128.refs_0_.cotan_ref, f32[96,1024]{1,0:T(8,128)S(1)} %get-tuple-element.129.refs_1_.grad_ref, f32[96,128]{1,0:T(8,128)S(1)} %get-tuple-element.130.refs_2_, f32[96,128]{1,0:T(8,128)S(1)} %get-tuple-element.81.refs_2_.taps_ref.refs_3_), custom_call_target="tpu_custom_call" | custom-call | flops 9633792 | tf_op jit(solution)/shard_map/pallas_call | solution.py:36
  189.6 3.4 %shard_map.171 = f32[768,128]{1,0:T(8,128)} custom-call(f32[96,1024]{1,0:T(8,128)S(1)} %shard_map.170.own_ref, f32[384,128]{1,0:T(8,128)S(1)} %collective-permute-done.23.a_ref, f32[384,128]{1,0:T(8,128)S(1)} %collective-permute-done.24.b_ref, s32[1]{0:T(128)} %bitcast.6.odd_ref.refs_11_, f32[96,128]{1,0:T(8,128)S(1)} %get-tuple-element.81.refs_2_.taps_ref.refs_3_), custom_call_target="tpu_custom_call" | custom-call | tf_op jit(solution)/shard_map/pallas_call | solution.py:36
  193.0 3.9 %all-to-all-done.1 = f32[64,16,128]{2,1,0:T(8,128)S(1)} async-done(((f32[64,16,128]{2,1,0:T(8,128)}), f32[64,16,128]{2,1,0:T(8,128)S(1)}, u32[]{:S(2)}, u32[]{:S(2)}) %all-to-all-start.1) | async-done | bytes 524320 | tf_op jit(solution)/shard_map/all_to_all | solution.py:488
  (71 shorter events, 32.0 us)
Async XLA Ops:
  1.9 12.7 %collective-permute-start = (f32[24,128]{1,0:T(8,128)S(1)}, f32[24,128]{1,0:T(8,128)S(1)}, u32[]{:S(2)}, u32[]{:S(2)}) collective-permute-start(f32[24,128]{1,0:T(8,128)S(1)} %get-tuple-element.78), channel_id=1, source_target_pairs={{0,1},{1,2},{2,3},{3,4},{4,5},{5,6},{6,7},{64,65},{65,66},{66,67},... | collective-permute-start | bytes 36872 | tf_op jit(solution)/shard_map/ppermute | solution.py:480
  5.9 8.8 %collective-permute-start.1 = (f32[24,128]{1,0:T(8,128)S(1)}, f32[24,128]{1,0:T(8,128)S(1)}, u32[]{:S(2)}, u32[]{:S(2)}) collective-permute-start(f32[24,128]{1,0:T(8,128)S(1)} %get-tuple-element.79), channel_id=1, source_target_pairs={{1,0},{2,1},{3,2},{4,3},{5,4},{6,5},{7,6},{65,64},{66,65},{67,66},... | collective-permute-start | bytes 36872 | tf_op jit(solution)/shard_map/ppermute | solution.py:480
  14.7 7.3 %collective-permute-start.2 = (f32[384,128]{1,0:T(8,128)S(1)}, f32[384,128]{1,0:T(8,128)S(1)}, u32[]{:S(2)}, u32[]{:S(2)}) collective-permute-start(f32[384,128]{1,0:T(8,128)S(1)} %get-tuple-element.82), channel_id=1, source_target_pairs={{0,8},{8,0},{16,24},{24,16},{32,40},{40,32},{48,56},{56,48},{64,72... | collective-permute-start | bytes 589832 | tf_op jit(solution)/shard_map/ppermute | solution.py:470
  15.8 7.0 %collective-permute-start.3 = (f32[384,128]{1,0:T(8,128)S(1)}, f32[384,128]{1,0:T(8,128)S(1)}, u32[]{:S(2)}, u32[]{:S(2)}) collective-permute-start(f32[384,128]{1,0:T(8,128)S(1)} %get-tuple-element.83), channel_id=1, source_target_pairs={{8,16},{16,8},{24,32},{32,24},{40,48},{48,40},{72,80},{80,72},{88,... | collective-permute-start | bytes 589832 | tf_op jit(solution)/shard_map/ppermute | solution.py:471
  29.1 2.5 %collective-permute-start.4 = (f32[24,128]{1,0:T(8,128)S(1)}, f32[24,128]{1,0:T(8,128)S(1)}, u32[]{:S(2)}, u32[]{:S(2)}) collective-permute-start(f32[24,128]{1,0:T(8,128)S(1)} %get-tuple-element.95), channel_id=1, source_target_pairs={{192,193},{193,194},{194,195},{195,196},{196,197},{197,198},{198,1... | collective-permute-start | bytes 36872 | tf_op jit(solution)/shard_map/ppermute | solution.py:480
  29.8 1.8 collective-permute-start.5
  31.7 4.5 %collective-permute-start.6 = (f32[384,128]{1,0:T(8,128)S(1)}, f32[384,128]{1,0:T(8,128)S(1)}, u32[]{:S(2)}, u32[]{:S(2)}) collective-permute-start(f32[384,128]{1,0:T(8,128)S(1)} %get-tuple-element.104), channel_id=1, source_target_pairs={{192,200},{200,192},{208,216},{216,208},{224,232},{232,224},{240,2... | collective-permute-start | bytes 589832 | tf_op jit(solution)/shard_map/ppermute | solution.py:470
  32.4 3.8 %collective-permute-start.7 = (f32[384,128]{1,0:T(8,128)S(1)}, f32[384,128]{1,0:T(8,128)S(1)}, u32[]{:S(2)}, u32[]{:S(2)}) collective-permute-start(f32[384,128]{1,0:T(8,128)S(1)} %get-tuple-element.105), channel_id=1, source_target_pairs={{200,208},{208,200},{216,224},{224,216},{232,240},{240,232},{201,2... | collective-permute-start | bytes 589832 | tf_op jit(solution)/shard_map/ppermute | solution.py:471
  39.2 10.4 %collective-permute-start.8 = (f32[96,1024]{1,0:T(8,128)S(1)}, f32[96,1024]{1,0:T(8,128)S(1)}, u32[]{:S(2)}, u32[]{:S(2)}) collective-permute-start(f32[96,1024]{1,0:T(8,128)S(1)} %get-tuple-element.106), channel_id=1, source_target_pairs={{192,128},{193,129},{194,130},{195,131},{196,132},{197,133},{198,1... | collective-permute-start | bytes 1179656 | tf_op jit(solution)/shard_map/ppermute | solution.py:555
  39.9 6.9 %collective-permute-start.11 = (f32[128,128]{1,0:T(8,128)S(1)}, f32[128,128]{1,0:T(8,128)S(1)}, u32[]{:S(2)}, u32[]{:S(2)}) collective-permute-start(f32[128,128]{1,0:T(8,128)S(1)} %get-tuple-element.109), channel_id=1, source_target_pairs={{0,1},{1,2},{2,3},{3,4},{4,5},{5,6},{6,7},{64,65},{65,66},{66,67},... | collective-permute-start | bytes 196616 | tf_op jit(solution)/shard_map/ppermute | solution.py:480
  44.1 5.2 %collective-permute-start.12 = (f32[128,128]{1,0:T(8,128)S(1)}, f32[128,128]{1,0:T(8,128)S(1)}, u32[]{:S(2)}, u32[]{:S(2)}) collective-permute-start(f32[128,128]{1,0:T(8,128)S(1)} %get-tuple-element.110), channel_id=1, source_target_pairs={{1,0},{2,1},{3,2},{4,3},{5,4},{6,5},{7,6},{65,64},{66,65},{67,66},... | collective-permute-start | bytes 196616 | tf_op jit(solution)/shard_map/ppermute | solution.py:480
  45.4 4.1 %collective-permute-start.9 = (f32[24,128]{1,0:T(8,128)S(1)}, f32[24,128]{1,0:T(8,128)S(1)}, u32[]{:S(2)}, u32[]{:S(2)}) collective-permute-start(f32[24,128]{1,0:T(8,128)S(1)} %get-tuple-element.107), channel_id=1, source_target_pairs={{192,129},{193,130},{194,131},{195,132},{196,133},{197,134},{198,1... | collective-permute-start | bytes 36872 | tf_op jit(solution)/shard_map/ppermute | solution.py:480
  46.1 3.4 %collective-permute-start.10 = (f32[24,128]{1,0:T(8,128)S(1)}, f32[24,128]{1,0:T(8,128)S(1)}, u32[]{:S(2)}, u32[]{:S(2)}) collective-permute-start(f32[24,128]{1,0:T(8,128)S(1)} %get-tuple-element.108), channel_id=1, source_target_pairs={{193,128},{194,129},{195,130},{196,131},{197,132},{198,133},{199,1... | collective-permute-start | bytes 36872 | tf_op jit(solution)/shard_map/ppermute | solution.py:480
  52.4 4.5 %collective-permute-start.13 = (f32[384,128]{1,0:T(8,128)S(1)}, f32[384,128]{1,0:T(8,128)S(1)}, u32[]{:S(2)}, u32[]{:S(2)}) collective-permute-start(f32[384,128]{1,0:T(8,128)S(1)} %get-tuple-element.116), channel_id=1, source_target_pairs={{128,136},{136,128},{144,152},{152,144},{160,168},{168,160},{176,1... | collective-permute-start | bytes 589832 | tf_op jit(solution)/shard_map/ppermute | solution.py:470
  53.1 3.8 %collective-permute-start.14 = (f32[384,128]{1,0:T(8,128)S(1)}, f32[384,128]{1,0:T(8,128)S(1)}, u32[]{:S(2)}, u32[]{:S(2)}) collective-permute-start(f32[384,128]{1,0:T(8,128)S(1)} %get-tuple-element.117), channel_id=1, source_target_pairs={{136,144},{144,136},{152,160},{160,152},{168,176},{176,168},{137,1... | collective-permute-start | bytes 589832 | tf_op jit(solution)/shard_map/ppermute | solution.py:471
  59.8 2.1 %collective-permute-start.15 = (f32[96,1024]{1,0:T(8,128)S(1)}, f32[96,1024]{1,0:T(8,128)S(1)}, u32[]{:S(2)}, u32[]{:S(2)}) collective-permute-start(f32[96,1024]{1,0:T(8,128)S(1)} %get-tuple-element.118), channel_id=1, source_target_pairs={{128,64},{129,65},{130,66},{131,67},{132,68},{133,69},{134,70},{13... | collective-permute-start | bytes 1179656 | tf_op jit(solution)/shard_map/ppermute | solution.py:555
  64.7 4.5 %collective-permute-start.18 = (f32[384,128]{1,0:T(8,128)S(1)}, f32[384,128]{1,0:T(8,128)S(1)}, u32[]{:S(2)}, u32[]{:S(2)}) collective-permute-start(f32[384,128]{1,0:T(8,128)S(1)} %get-tuple-element.123), channel_id=1, source_target_pairs={{64,72},{72,64},{80,88},{88,80},{96,104},{104,96},{112,120},{120,1... | collective-permute-start | bytes 589832 | tf_op jit(solution)/shard_map/ppermute | solution.py:470
  65.4 3.8 %collective-permute-start.19 = (f32[384,128]{1,0:T(8,128)S(1)}, f32[384,128]{1,0:T(8,128)S(1)}, u32[]{:S(2)}, u32[]{:S(2)}) collective-permute-start(f32[384,128]{1,0:T(8,128)S(1)} %get-tuple-element.124), channel_id=1, source_target_pairs={{72,80},{80,72},{88,96},{96,88},{104,112},{112,104},{73,81},{81,73... | collective-permute-start | bytes 589832 | tf_op jit(solution)/shard_map/ppermute | solution.py:471
  72.2 62.8 %collective-permute-start.20 = (f32[96,1024]{1,0:T(8,128)S(1)}, f32[96,1024]{1,0:T(8,128)S(1)}, u32[]{:S(2)}, u32[]{:S(2)}) collective-permute-start(f32[96,1024]{1,0:T(8,128)S(1)} %get-tuple-element.125), channel_id=1, source_target_pairs={{64,0},{65,1},{66,2},{67,3},{68,4},{69,5},{70,6},{71,7},{72,8},{73... | collective-permute-start | bytes 1179656 | tf_op jit(solution)/shard_map/ppermute | solution.py:555
  73.7 2.0 collective-permute-start.21
  74.3 60.7 %collective-permute-start.22 = (f32[24,128]{1,0:T(8,128)S(1)}, f32[24,128]{1,0:T(8,128)S(1)}, u32[]{:S(2)}, u32[]{:S(2)}) collective-permute-start(f32[24,128]{1,0:T(8,128)S(1)} %get-tuple-element.127), channel_id=1, source_target_pairs={{65,0},{66,1},{67,2},{68,3},{69,4},{70,5},{71,6},{73,8},{74,9},{75... | collective-permute-start | bytes 36872 | tf_op jit(solution)/shard_map/ppermute | solution.py:480
  176.1 20.8 %all-to-all-start.1 = ((f32[64,16,128]{2,1,0:T(8,128)}), f32[64,16,128]{2,1,0:T(8,128)S(1)}, u32[]{:S(2)}, u32[]{:S(2)}) async-start(f32[64,16,128]{2,1,0:T(8,128)} %shard_map.173), calls=%async_computation.1 | async-start | bytes 1048576 | tf_op jit(solution)/shard_map/all_to_all | solution.py:488
  180.6 7.0 %collective-permute-start.23 = (f32[384,128]{1,0:T(8,128)S(1)}, f32[384,128]{1,0:T(8,128)S(1)}, u32[]{:S(2)}, u32[]{:S(2)}) collective-permute-start(f32[384,128]{1,0:T(8,128)S(1)} %get-tuple-element.131), channel_id=1, source_target_pairs={{0,8},{8,0},{16,24},{24,16},{32,40},{40,32},{48,56},{56,48},{64,72... | collective-permute-start | bytes 589832 | tf_op jit(solution)/shard_map/ppermute | solution.py:470
  181.2 8.4 %collective-permute-start.24 = (f32[384,128]{1,0:T(8,128)S(1)}, f32[384,128]{1,0:T(8,128)S(1)}, u32[]{:S(2)}, u32[]{:S(2)}) collective-permute-start(f32[384,128]{1,0:T(8,128)S(1)} %get-tuple-element.132), channel_id=1, source_target_pairs={{8,16},{16,8},{24,32},{32,24},{40,48},{48,40},{72,80},{80,72},{88,... | collective-permute-start | bytes 589832 | tf_op jit(solution)/shard_map/ppermute | solution.py:471
  (11 other events, 9.2 us)

commit v4 on v3

--- a/solution.py
+++ b/solution.py
@@ -111,8 +111,8 @@
     return value, roll(strip, LANES - REACH - REACH * row), roll(strip, -SIDE - REACH * row)
 
 
-def tap_of(taps, tap):
-    return jnp.broadcast_to(taps[:, tap : tap + 1], (GROUP, LANES))
+def tap_of(taps_ref, tap, group):
+    return taps_ref[pl.ds(tap * C + group, GROUP), :]
 
 
 def take_field(acts_ref, field_ref, right_ref, left_ref):
@@ -138,7 +138,9 @@
     cotan_ref, taps_ref, gain_ref, bias_ref, scale_ref, b_in_ref, w_in_out, w_out_out, w_in_gain_ref, w_out_scale_ref = outs
     for row in range(ROWS):
         cotan_ref[:, block(row)] = top_ref[pl.ds(row, C, stride=ROWS), :]
-    taps_ref[:, :TAPS] = kernel_ref[:, 0, :].T
+    taps = kernel_ref[:, 0, :].T
+    for tap in range(TAPS):
+        taps_ref[pl.ds(tap * C, C), :] = jnp.broadcast_to(taps[:, tap : tap + 1], (C, LANES))
     gain_ref[...] = column(gain_row[...])
     bias_ref[...] = column(bias_row[...])
     scale_ref[...] = column(scale_row[...])
@@ -197,8 +199,8 @@
     lane = lane_of(GROUP)
 
     def conv_group(index, carry):
-        channels = pl.ds(pl.multiple_of(index * GROUP, GROUP), GROUP)
-        taps = taps_ref[channels, :]
+        group = pl.multiple_of(index * GROUP, GROUP)
+        channels = pl.ds(group, GROUP)
         rows = own_rows(channels, field_ref, strip_ref)
         if flipped:
             sums = [start_ref[channels, block(row)] for row in range(ROWS)]
@@ -207,7 +209,7 @@
         for b in range(KS):
             moved = [shifted_row(*rows[row], lane, b - REACH) for row in range(ROWS)]
             for a in range(KS):
-                weight = tap_of(taps, tap_index(a, b, flipped))
+                weight = tap_of(taps_ref, tap_index(a, b, flipped), group)
                 for row in range(ROWS):
                     if 0 <= row + a - REACH < ROWS:
                         sums[row] = sums[row] + weight * moved[row + a - REACH]
@@ -225,7 +227,6 @@
     def conv_group(index, carry):
         group = pl.multiple_of(index * GROUP, GROUP)
         channels = pl.ds(group, GROUP)
-        taps = taps_ref[channels, :]
         rows = outer_rows(group, a_ref, b_ref, odd)
         sums = [own_ref[channels, block(row)] for row in range(ROWS)]
         for b in range(KS):
@@ -233,7 +234,7 @@
             for a in range(KS):
                 if a == REACH:
                     continue
-                weight = tap_of(taps, tap_index(a, b, flipped))
+                weight = tap_of(taps_ref, tap_index(a, b, flipped), group)
                 for row in range(ROWS):
                     if row + a - REACH in moved:
                         sums[row] = sums[row] + weight * moved[row + a - REACH]
@@ -381,9 +382,17 @@
 USED_ROWS = TAPS_AT + C
 
 
+HALF = PAYLOAD_ROWS // 2
+
+
+def half_of(odd):
+    return pl.ds(pl.multiple_of(odd * HALF, HALF), HALF)
+
+
 def parameter_terms(
     field_ref, strip_ref, a_ref, b_ref, odd_ref, grad_ref, cotan_ref, hidden_ref, normed_ref, grad_pre_ref,
-    payload_ref,
+    gain_ref, bias_ref, scale_ref, w_in_ref, w_out_ref,
+    mine_ref, theirs_ref, payload_ref,
 ):
     odd = odd_ref[0] == 1
     lane = lane_of(GROUP)
@@ -410,48 +419,52 @@
     ones = jnp.where(lax.broadcasted_iota(jnp.int32, (GROUP, CELLS), 0) == 0, 1.0, 0.0)
     lifted = jnp.concatenate([normed_ref[...], ones], axis=0)
     grad_w_in = product(split(lifted), split(grad_pre_ref[...]), ROW_ROW)
+    grad_b_in = grad_w_in[C : C + 1, :]
+    columns = (w_in_ref[...] * grad_w_in[:C, :], w_in_ref[...] * grad_b_in, w_out_ref[...] * grad_w_out)
+    lane = lane_of(C)
+    for index, terms in enumerate(columns):
+        total = jnp.sum(terms, axis=1, keepdims=True)
+        taps = payload_ref[pl.ds(TAPS_AT, C), :]
+        payload_ref[pl.ds(TAPS_AT, C), :] = jnp.where(lane == TAPS + index, total, taps)
+    grad_w_out = grad_w_out * scale_ref[...]
+    grad_weights = grad_w_in[:C, :] * gain_ref[...] + bias_ref[...] * grad_b_in
     for part in range(HID // LANES):
-        payload_ref[pl.ds(OUT_AT + part * C, C), :] = grad_w_out[:, part * LANES : (part + 1) * LANES]
-        payload_ref[pl.ds(IN_AT + part * LIFT_ROWS, LIFT_ROWS), :] = grad_w_in[:, part * LANES : (part + 1) * LANES]
+        lanes = slice(part * LANES, (part + 1) * LANES)
+        at = IN_AT + part * LIFT_ROWS
+        payload_ref[pl.ds(OUT_AT + part * C, C), :] = grad_w_out[:, lanes]
+        payload_ref[pl.ds(at, C), :] = grad_weights[:, lanes]
+        payload_ref[pl.ds(at + C, GROUP), :] = grad_w_in[C:, lanes]
     payload_ref[pl.ds(USED_ROWS, PAYLOAD_ROWS - USED_ROWS), :] = jnp.zeros((PAYLOAD_ROWS - USED_ROWS, LANES), F32)
+    mine_ref[...] = payload_ref[half_of(odd_ref[0]), :]
+    theirs_ref[...] = payload_ref[half_of(1 - odd_ref[0]), :]
 
 
 def sum_shares(shares_ref, out_ref):
-    devices, rows = out_ref.shape[0], out_ref.shape[1]
-
-    def add(device, total):
-        return total + shares_ref[device]
-
-    total = lax.fori_loop(1, devices, add, shares_ref[0], unroll=7)
-
-    def put(device, carry):
-        out_ref[device] = total
-        return carry
-
-    lax.fori_loop(0, devices, put, 0, unroll=8)
+    devices = out_ref.shape[0]
+    terms = [shares_ref[device] for device in range(devices)]
+    while len(terms) > 1:
+        terms = [one + two for one, two in zip(terms[0::2], terms[1::2])]
+    for device in range(devices):
+        out_ref[device] = terms[0]
 
 
 def parameter_grads(
-    payload_ref, gain_ref, bias_ref, w_in_ref, w_out_ref, scale_ref,
+    mine_ref, theirs_ref, odd_ref,
     kernel_out, gain_out, bias_out, w_in_out, b_in_out, w_out_out, scale_out,
+    payload_ref,
 ):
-    kernel_out[:, 0, :] = payload_ref[pl.ds(TAPS_AT, C), :].T[:TAPS, :]
-    scale = scale_ref[...]
-    sums = [jnp.zeros((C, 1), F32)] * 3
+    payload_ref[half_of(odd_ref[0]), :] = mine_ref[...]
+    payload_ref[half_of(1 - odd_ref[0]), :] = theirs_ref[...]
+    by_tap = payload_ref[pl.ds(TAPS_AT, C), :].T
+    kernel_out[:, 0, :] = by_tap[:TAPS, :]
+    for index, out_ref in enumerate((gain_out, bias_out, scale_out)):
+        out_ref[...] = by_tap[TAPS + index : TAPS + index + 1, :]
     for part in range(HID // LANES):
         hidden = pl.ds(part * LANES, LANES)
-        grad_out = payload_ref[pl.ds(OUT_AT + part * C, C), :]
-        w_out_out[:, hidden] = grad_out * scale
         at = IN_AT + part * LIFT_ROWS
-        grad_in = payload_ref[pl.ds(at, C), :]
-        grad_b = payload_ref[pl.ds(at + C, 1), :]
-        b_in_out[:, hidden] = grad_b
-        w_in_out[:, hidden] = grad_in * gain_ref[...] + bias_ref[...] * grad_b
-        w_in = w_in_ref[:, hidden]
-        terms = (w_in * grad_in, w_in * grad_b, w_out_ref[:, hidden] * grad_out)
-        sums = [total + jnp.sum(term, axis=1, keepdims=True) for total, term in zip(sums, terms)]
-    for total, out in zip(sums, (gain_out, bias_out, scale_out)):
-        out[...] = jnp.broadcast_to(total, (C, LANES)).T[:1, :]
+        w_out_out[:, hidden] = payload_ref[pl.ds(OUT_AT + part * C, C), :]
+        w_in_out[:, hidden] = payload_ref[pl.ds(at, C), :]
+        b_in_out[:, hidden] = payload_ref[pl.ds(at + C, 1), :]
 
 
 def pairs(axis, sections, odd_pairs):
@@ -480,12 +493,24 @@
     return lax.ppermute(to_right, axes, right), lax.ppermute(to_left, axes, left)
 
 
-def sum_over_tiles(payload):
-    devices = lax.axis_size(TILES)
-    rows = PAYLOAD_ROWS // devices
-    shares = lax.all_to_all(payload.reshape(devices, rows, LANES), TILES, 0, 0)
-    (copies,) = call(sum_shares, [(devices, rows, LANES)], shares)
-    return lax.all_to_all(copies, TILES, 0, 0).reshape(PAYLOAD_ROWS, LANES)
+def swap_pairs(half):
+    return lax.ppermute(half, "ty", [(tile, tile ^ 1) for tile in range(lax.axis_size("ty"))])
+
+
+def sum_over_tiles(mine, theirs, beside):
+    columns = lax.axis_size("tx")
+    tiles = lax.axis_size("ty")
+    groups = [[tile * columns + i for tile in range(odd, tiles, 2) for i in range(columns)] for odd in range(2)]
+    devices = len(groups[0])
+
+    def to_all(shares):
+        return lax.all_to_all(shares, TILES, 0, 0, axis_index_groups=groups)
+
+    half = mine + swap_pairs(theirs)
+    shares = to_all(half.reshape(devices, HALF // devices, LANES))
+    (copies,) = call(sum_shares, [shares.shape], shares)
+    mine, beside = lax.optimization_barrier((to_all(copies).reshape(HALF, LANES), beside))
+    return mine, swap_pairs(mine), beside
 
 
 def on_device(acts, top_grad, kernel, ln_gain, ln_bias, w_in, b_in, w_out, layer_scale):
@@ -504,7 +529,7 @@
     )
     cotan, taps, gain, shift_bias, scale, bias_in, weight_in, weight_out, w_in_gain, w_out_scale = call(
         prepare,
-        [field_shape, wide, (C, 1), (C, 1), (C, 1), (HID, 1), (C, HID), (C, HID), (C, HID), (HID, C)],
+        [field_shape, (TAPS * C, LANES), (C, 1), (C, 1), (C, 1), (HID, 1), (C, HID), (C, HID), (C, HID), (HID, C)],
         *parameters, scratch=[p.shape for p in parameters] + [pltpu.SemaphoreType.DMA((len(parameters),))], copied=True,
     )
     strip, message_a, message_b = call(edges, edge_outs, field, left, right, odd)
@@ -542,9 +567,10 @@
                 functools.partial(last_step, len(cotans)), [field_shape] + edge_outs + [field_shape, hidden_shape],
                 *cotans, *lefts, *rights, first_strip, odd, *saved, *strips,
             )
-            (payload,) = call(
-                parameter_terms, [(PAYLOAD_ROWS, LANES)],
-                *around, grad, cotan, hidden, normed, grad_pre, flops=4 * CONV_FLOPS,
+            payload = call(
+                parameter_terms, [(HALF, LANES)] * 2,
+                *around, grad, cotan, hidden, normed, grad_pre, gain, shift_bias, scale, weight_in, weight_out,
+                scratch=[(PAYLOAD_ROWS, LANES)], flops=4 * CONV_FLOPS,
             )
         grad_a, grad_b = swap_rows(message_a, message_b, only)
         (own,) = call(
@@ -557,12 +583,12 @@
             cotans.append(cotan)
             lefts.append(from_left)
             rights.append(from_right)
+    *payload, own = sum_over_tiles(*payload, own)
     (input_grad,) = call(last_finish, [(C * ROWS, LANES)], own, grad_a, grad_b, odd, taps)
-    payload = sum_over_tiles(payload)
     grad_kernel, grad_gain, grad_bias, grad_w_in, grad_b_in, grad_w_out, grad_scale = call(
         parameter_grads,
         [(TAPS, 1, C), (1, C), (1, C), (C, HID), (1, HID), (C, HID), (1, C)],
-        payload, gain, shift_bias, weight_in, weight_out, scale,
+        *payload, odd, scratch=[(PAYLOAD_ROWS, LANES)],
     )
     return (
         input_grad.reshape(1, 1, C, ROWS, LANES),

time: 199 us -> 201 us (1.010)
  waiting for transfers between devices: 68.7 us -> 77 us
  blocking collectives: 30.8 us -> 24.5 us
  Pallas kernels: 54.1 us -> 48.6 us
  starting transfers between devices: 36.1 us -> 39 us
  local copies, waits for them, and re-layouts: 7.18 us -> 9.65 us
    all_to_all x1, blocking collectives: 30.8 us -> 24.5 us  [to_all(): return lax.all_to_all(shares, TILES, 0, 0, axis_index_groups=groups)]
    pallas_call x23, Pallas kernels: 54.1 us -> 48.6 us  [call(): pl.pallas_call(kernel, out_shape=[jax.ShapeDtypeStruct(shape, F32) for sh...]
    all_to_all x1, waiting for transfers between devices: 3.92 us -> 8.55 us  [to_all(): return lax.all_to_all(shares, TILES, 0, 0, axis_index_groups=groups)]
    ppermute x0 -> x2, starting transfers between devices: none -> 4.57 us  [swap_pairs(): lax.ppermute(half, 'ty', [(tile, tile ^ 1) for tile in range(lax.axis_siz...]
    ppermute x5, waiting for transfers between devices: 2.77 us -> 5.76 us  [swap_rows(): lax.ppermute(message_b, axes, pairs('ty', sections, True))]
    unnamed x18 -> x32, local copies, waits for them, and re-layouts: 7.18 us -> 9.65 us
  transfers between devices with their start and end apart: 26 -> 28, of which waited for: 5 -> 6; matrix products, arithmetic and copies ran while one was open for 0% -> 0% of each run, Pallas kernels for 11% -> 9%
where the time goes in v4:
time: 201 us; the launch traced here: 200 us
  waiting for transfers between devices  77 us (38%)
  Pallas kernels  48.6 us (24%)
  starting transfers between devices  39 us (19%)
  blocking collectives  24.5 us (12%)
  local copies, waits for them, and re-layouts  9.65 us (5%)
    ppermute x6, waiting for transfers between devices, to_sides(): lax.ppermute(to_left, axes, left)  61.1 us
    pallas_call x23, Pallas kernels, call(): pl.pallas_call(kernel, out_shape=[jax.ShapeDtypeStruct(shape, F32) for sh...  48.6 us
    all_to_all x1, blocking collectives, to_all(): return lax.all_to_all(shares, TILES, 0, 0, axis_index_groups=groups)  24.5 us
    ppermute x6, starting transfers between devices, to_sides(): lax.ppermute(to_right, axes, right)  10.9 us
    unnamed x32, local copies, waits for them, and re-layouts  9.65 us
    all_to_all x1, waiting for transfers between devices, to_all(): return lax.all_to_all(shares, TILES, 0, 0, axis_index_groups=groups)  8.55 us
    ppermute x5, starting transfers between devices, swap_rows(): lax.ppermute(message_b, axes, pairs('ty', sections, True))  7.93 us
    ppermute x6, starting transfers between devices, to_sides(): lax.ppermute(to_left, axes, left)  5.86 us
  transfers between devices with their start and end apart: 28, of which 6 were waited for; matrix products, arithmetic and copies ran while one was open for 0% of the time, Pallas kernels for 9%

profile of v4, /device:TPU:1, one launch (start us, length us, event | category | flops | bytes accessed | tf_op | source)
XLA Modules:
  0.0 200.1 jit_solution(3482592870177717867)
XLA Ops:
  1.9 3.9 %collective-permute-start = (f32[24,128]{1,0:T(8,128)S(1)}, f32[24,128]{1,0:T(8,128)S(1)}, u32[]{:S(2)}, u32[]{:S(2)}) collective-permute-start(f32[24,128]{1,0:T(8,128)S(1)} %get-tuple-element.81), channel_id=1, source_target_pairs={{0,1},{1,2},{2,3},{3,4},{4,5},{5,6},{6,7},{64,65},{65,66},{66,67},... | collective-permute-start | bytes 36872 | tf_op jit(solution)/shard_map/ppermute | solution.py:493
  16.4 3.1 %collective-permute-start.3 = (f32[384,128]{1,0:T(8,128)S(1)}, f32[384,128]{1,0:T(8,128)S(1)}, u32[]{:S(2)}, u32[]{:S(2)}) collective-permute-start(f32[384,128]{1,0:T(8,128)S(1)} %get-tuple-element.85), channel_id=1, source_target_pairs={{8,16},{16,8},{24,32},{32,24},{40,48},{48,40},{72,80},{80,72},{88,... | collective-permute-start | bytes 589832 | tf_op jit(solution)/shard_map/ppermute | solution.py:484
  19.6 2.6 %shard_map.155.own_ref = f32[96,1024]{1,0:T(8,128)S(1)} custom-call(f32[96,1024]{1,0:T(8,128)S(1)} %get-tuple-element.80.field_ref.refs_0_, f32[96,128]{1,0:T(8,128)S(1)} %get-tuple-element.83.refs_1_.strip_ref, f32[4704,128]{1,0:T(8,128)S(1)} %get-tuple-element.87.refs_2_.taps_ref.refs_3_), custom_call_target="tpu_custom_call" | custom-call | flops 9633792 | tf_op jit(solution)/shard_map/pallas_call | solution.py:36
  23.4 3.3 %shard_map.156 = (f32[96,1024]{1,0:T(8,128)S(1)}, f32[1,1024]{1,0:T(1,128)S(1)}, f32[384,1024]{1,0:T(8,128)S(1)}, f32[384,1024]{1,0:T(8,128)S(1)}) custom-call(f32[96,1024]{1,0:T(8,128)S(1)} %shard_map.155.own_ref, f32[384,128]{1,0:T(8,128)S(1)} %collective-permute-done.2.a_ref, f32[384,128]{1,0:T(8,128)S(1)} %collective-permute-done.3.b_ref, ...), custom_call_target="tpu_custom_call" | custom-call | tf_op jit(solution)/shard_map/pallas_call | solution.py:36
  26.7 2.5 %shard_map.157 = (f32[96,1024]{1,0:T(8,128)S(1)}, f32[24,128]{1,0:T(8,128)S(1)}, f32[24,128]{1,0:T(8,128)S(1)}) custom-call(f32[96,1024]{1,0:T(8,128)S(1)} %broadcast_multiply_fusion.cotan_ref.refs_0_, f32[96,1024]{1,0:T(8,128)S(1)} %get-tuple-element.100.refs_0_.normed_ref.refs_12_, f32[1,1024]{1,0:T(1,128)S(1)} %get-tuple-element.101.refs_1_.inv_ref.refs_13_, ...), custom_call_target="tpu_custom_call" | custom-call | tf_op jit(solution)/shard_map/pallas_call | solution.py:36
  33.2 2.6 %shard_map.160.own_ref = f32[96,1024]{1,0:T(8,128)S(1)} custom-call(f32[96,1024]{1,0:T(8,128)S(1)} %broadcast_multiply_fusion.cotan_ref.refs_0_, f32[96,1024]{1,0:T(8,128)S(1)} %get-tuple-element.98.field_ref.refs_1_, f32[96,128]{1,0:T(8,128)S(1)} %get-tuple-element.107.refs_2_.refs_10_, f32[4704,128]{1,0:T(8,128)S(1)} %get-tuple-element.87.refs_2_.taps_ref.refs_3_), custom_call_target="tpu_custom_call" | custom-call | flops 9633792 | tf_op jit(solution)/shard_map/pallas_call | solution.py:36
  35.8 2.4 %shard_map.161 = (f32[96,1024]{1,0:T(8,128)S(1)}, f32[24,128]{1,0:T(8,128)S(1)}, f32[24,128]{1,0:T(8,128)S(1)}) custom-call(f32[96,1024]{1,0:T(8,128)S(1)} %shard_map.160.own_ref, f32[384,128]{1,0:T(8,128)S(1)} %collective-permute-done.6.a_ref, f32[384,128]{1,0:T(8,128)S(1)} %collective-permute-done.7.b_ref, s32[1]{0:T(128)} %bitcast.1.odd_ref.refs_11_, ...), custom_call_target="tpu_custom_call" | custom-call | tf_op jit(solution)/shard_map/pallas_call | solution.py:36
  39.0 4.3 %collective-permute-start.11 = (f32[128,128]{1,0:T(8,128)S(1)}, f32[128,128]{1,0:T(8,128)S(1)}, u32[]{:S(2)}, u32[]{:S(2)}) collective-permute-start(f32[128,128]{1,0:T(8,128)S(1)} %get-tuple-element.113), channel_id=1, source_target_pairs={{0,1},{1,2},{2,3},{3,4},{4,5},{5,6},{6,7},{64,65},{65,66},{66,67},... | collective-permute-start | bytes 196616 | tf_op jit(solution)/shard_map/ppermute | solution.py:493
  48.5 2.8 %shard_map.163 = (f32[96,1024]{1,0:T(8,128)S(1)}, f32[96,128]{1,0:T(8,128)S(1)}, f32[384,128]{1,0:T(8,128)S(1)}, f32[384,128]{1,0:T(8,128)S(1)}) custom-call(f32[96,1024]{1,0:T(8,128)S(1)} %collective-permute-done.8.cotan_ref.refs_0_.refs_1_, f32[24,128]{1,0:T(8,128)S(1)} %collective-permute-done.9.from_left.refs_4_, ...), custom_call_target="tpu_custom_call" | custom-call | tf_op jit(solution)/shard_map/pallas_call | solution.py:36
  52.6 2.6 %shard_map.164.own_ref = f32[96,1024]{1,0:T(8,128)S(1)} custom-call(f32[96,1024]{1,0:T(8,128)S(1)} %collective-permute-done.8.cotan_ref.refs_0_.refs_1_, f32[96,1024]{1,0:T(8,128)S(1)} %get-tuple-element.118.refs_1_, f32[96,128]{1,0:T(8,128)S(1)} %get-tuple-element.119.refs_2_, f32[4704,128]{1,0:T(8,128)S(1)} %get-tuple-element.87.refs_2_.taps_ref.refs_3_), custom_call_target="tpu_custom_call" | custom-call | flops 9633792 | tf_op jit(solution)/shard_map/pallas_call | solution.py:36
  55.2 2.4 %shard_map.165 = (f32[96,1024]{1,0:T(8,128)S(1)}, f32[24,128]{1,0:T(8,128)S(1)}, f32[24,128]{1,0:T(8,128)S(1)}) custom-call(f32[96,1024]{1,0:T(8,128)S(1)} %shard_map.164.own_ref, f32[384,128]{1,0:T(8,128)S(1)} %collective-permute-done.13.a_ref, f32[384,128]{1,0:T(8,128)S(1)} %collective-permute-done.14.b_ref, s32[1]{0:T(128)} %bitcast.1.odd_ref.refs_11_, ...), custom_call_target="tpu_custom_call" | custom-call | tf_op jit(solution)/shard_map/pallas_call | solution.py:36
  59.7 2.8 %shard_map.166 = (f32[96,1024]{1,0:T(8,128)S(1)}, f32[96,128]{1,0:T(8,128)S(1)}, f32[384,128]{1,0:T(8,128)S(1)}, f32[384,128]{1,0:T(8,128)S(1)}) custom-call(f32[96,1024]{1,0:T(8,128)S(1)} %collective-permute-done.15.cotan_ref.refs_0_.refs_2_, f32[24,128]{1,0:T(8,128)S(1)} %collective-permute-done.16.from_left.refs_5_, ...), custom_call_target="tpu_custom_call" | custom-call | tf_op jit(solution)/shard_map/pallas_call | solution.py:36
  64.1 2.6 %shard_map.167.own_ref = f32[96,1024]{1,0:T(8,128)S(1)} custom-call(f32[96,1024]{1,0:T(8,128)S(1)} %collective-permute-done.15.cotan_ref.refs_0_.refs_2_, f32[96,1024]{1,0:T(8,128)S(1)} %get-tuple-element.125.refs_1_, f32[96,128]{1,0:T(8,128)S(1)} %get-tuple-element.126.refs_2_, f32[4704,128]{1,0:T(8,128)S(1)} %get-tuple-element.87.refs_2_.taps_ref.refs_3_), custom_call_target="tpu_custom_call" | custom-call | flops 9633792 | tf_op jit(solution)/shard_map/pallas_call | solution.py:36
  72.4 58.7 %collective-permute-done.22.refs_9_ = f32[24,128]{1,0:T(8,128)S(1)} collective-permute-done((f32[24,128]{1,0:T(8,128)S(1)}, f32[24,128]{1,0:T(8,128)S(1)}, u32[]{:S(2)}, u32[]{:S(2)}) %collective-permute-start.22) | collective-permute-done | bytes 12320 | tf_op jit(solution)/shard_map/ppermute | solution.py:493
  131.2 2.8 %shard_map.169 = (f32[96,1024]{1,0:T(8,128)S(1)}, f32[96,128]{1,0:T(8,128)S(1)}, f32[384,128]{1,0:T(8,128)S(1)}, f32[384,128]{1,0:T(8,128)S(1)}, f32[96,1024]{1,0:T(8,128)S(1)}, /*index=5*/f32[384,1024]{1,0:T(8,128)S(1)}) custom-call(f32[96,1024]{1,0:T(8,128)S(1)} %broadcast_multiply_fusion.cotan_ref.refs_0_, ...), custom_call_target="tpu_custom_call" | custom-call | tf_op jit(solution)/shard_map/pallas_call | solution.py:36
  134.1 6.7 %shard_map.170 = (f32[512,128]{1,0:T(8,128)S(1)}, f32[512,128]{1,0:T(8,128)S(1)}) custom-call(f32[96,1024]{1,0:T(8,128)S(1)} %get-tuple-element.80.field_ref.refs_0_, f32[96,128]{1,0:T(8,128)S(1)} %get-tuple-element.83.refs_1_.strip_ref, f32[384,128]{1,0:T(8,128)S(1)} %collective-permute-done.2.a_ref, f32[384,128]{1,0:T(8,128)S(1)} %collective-permute-done.3.b_ref, ...), custom_call_target="tpu_custom_call" | custom-call | flops 38535168 | tf_op jit(solution)/shard_map/pallas_call | solution.py:36
  142.5 24.5 %all_to_all.10.shares_ref = f32[32,16,128]{2,1,0:T(8,128)S(1)} all-to-all(f32[32,16,128]{2,1,0:T(8,128)S(1)} %bitcast.23), channel_id=1, replica_groups={{0,1,2,3,4,5,6,7,16,17,18,19,20,21,22,23,32,33,34,35,36,37,38,39,48,49,..., dimensions={0} | all-to-all | bytes 524288 | tf_op jit(solution)/shard_map/all_to_all | solution.py:507
  167.8 4.1 %all-to-all-start.1 = ((f32[32,16,128]{2,1,0:T(8,128)}), f32[32,16,128]{2,1,0:T(8,128)S(1)}, u32[]{:S(2)}, u32[]{:S(2)}) async-start(f32[32,16,128]{2,1,0:T(8,128)} %copy-done.4), calls=%async_computation.1 | async-start | bytes 524288 | tf_op jit(solution)/shard_map/all_to_all | solution.py:507
  171.9 2.6 %shard_map.172.own_ref = f32[96,1024]{1,0:T(8,128)S(1)} custom-call(f32[96,1024]{1,0:T(8,128)S(1)} %copy-done.1, f32[96,1024]{1,0:T(8,128)S(1)} %get-tuple-element.132.grad_ref.refs_1_, f32[96,128]{1,0:T(8,128)S(1)} %get-tuple-element.140.refs_2_, f32[4704,128]{1,0:T(8,128)S(1)} %get-tuple-element.87.refs_2_.taps_ref.refs_3_), custom_call_target="tpu_custom_call" | custom-call | flops 9633792 | tf_op jit(solution)/shard_map/pallas_call | solution.py:36
  175.2 8.5 %all-to-all-done.1 = f32[32,16,128]{2,1,0:T(8,128)S(1)} async-done(((f32[32,16,128]{2,1,0:T(8,128)}), f32[32,16,128]{2,1,0:T(8,128)S(1)}, u32[]{:S(2)}, u32[]{:S(2)}) %all-to-all-start.1) | async-done | bytes 262176 | tf_op jit(solution)/shard_map/all_to_all | solution.py:507
  183.7 4.5 %collective-permute-start.26 = (f32[512,128]{1,0:T(8,128)S(1)}, f32[512,128]{1,0:T(8,128)S(1)}, u32[]{:S(2)}, u32[]{:S(2)}) collective-permute-start(f32[512,128]{1,0:T(8,128)S(1)} %bitcast.16), channel_id=1, source_target_pairs={{0,8},{8,0},{16,24},{24,16},{32,40},{40,32},{48,56},{56,48},{1,9},... | collective-permute-start | bytes 786440 | tf_op jit(solution)/shard_map/ppermute | solution.py:497
  188.2 2.6 %collective-permute-start.25 = (f32[384,128]{1,0:T(8,128)}, f32[384,128]{1,0:T(8,128)S(1)}, u32[]{:S(2)}, u32[]{:S(2)}) collective-permute-start(f32[384,128]{1,0:T(8,128)} %copy-done.14), channel_id=1, source_target_pairs={{8,16},{16,8},{24,32},{32,24},{40,48},{48,40},{72,80},{80,72},{88,... | collective-permute-start | bytes 589832 | tf_op jit(solution)/shard_map/ppermute | solution.py:484
  190.9 4.5 %collective-permute-done.25.b_ref = f32[384,128]{1,0:T(8,128)S(1)} collective-permute-done((f32[384,128]{1,0:T(8,128)}, f32[384,128]{1,0:T(8,128)S(1)}, u32[]{:S(2)}, u32[]{:S(2)}) %collective-permute-start.25) | collective-permute-done | bytes 196640 | tf_op jit(solution)/shard_map/ppermute | solution.py:484
  196.4 2.9 %shard_map.173 = f32[768,128]{1,0:T(8,128)} custom-call(f32[96,1024]{1,0:T(8,128)S(1)} %copy-done.3, f32[384,128]{1,0:T(8,128)S(1)} %collective-permute-done.24.a_ref, f32[384,128]{1,0:T(8,128)S(1)} %collective-permute-done.25.b_ref, s32[1]{0:T(128)} %bitcast.1.odd_ref.refs_11_, f32[4704,128]{1,0:T(8,128)S(1)} %get-tuple-element.87.refs_2_.taps_ref.refs_3_), custom_call_target="tpu_custom_call" | custom-call | tf_op jit(solution)/shard_map/pallas_call | solution.py:36
  (90 shorter events, 38.3 us)
Async XLA Ops:
  1.9 13.4 %collective-permute-start = (f32[24,128]{1,0:T(8,128)S(1)}, f32[24,128]{1,0:T(8,128)S(1)}, u32[]{:S(2)}, u32[]{:S(2)}) collective-permute-start(f32[24,128]{1,0:T(8,128)S(1)} %get-tuple-element.81), channel_id=1, source_target_pairs={{0,1},{1,2},{2,3},{3,4},{4,5},{5,6},{6,7},{64,65},{65,66},{66,67},... | collective-permute-start | bytes 36872 | tf_op jit(solution)/shard_map/ppermute | solution.py:493
  5.9 9.4 %collective-permute-start.1 = (f32[24,128]{1,0:T(8,128)S(1)}, f32[24,128]{1,0:T(8,128)S(1)}, u32[]{:S(2)}, u32[]{:S(2)}) collective-permute-start(f32[24,128]{1,0:T(8,128)S(1)} %get-tuple-element.82), channel_id=1, source_target_pairs={{1,0},{2,1},{3,2},{4,3},{5,4},{6,5},{7,6},{65,64},{66,65},{67,66},... | collective-permute-start | bytes 36872 | tf_op jit(solution)/shard_map/ppermute | solution.py:493
  15.4 6.8 %collective-permute-start.2 = (f32[384,128]{1,0:T(8,128)S(1)}, f32[384,128]{1,0:T(8,128)S(1)}, u32[]{:S(2)}, u32[]{:S(2)}) collective-permute-start(f32[384,128]{1,0:T(8,128)S(1)} %get-tuple-element.84), channel_id=1, source_target_pairs={{0,8},{8,0},{16,24},{24,16},{32,40},{40,32},{48,56},{56,48},{64,72... | collective-permute-start | bytes 589832 | tf_op jit(solution)/shard_map/ppermute | solution.py:483
  16.4 7.0 %collective-permute-start.3 = (f32[384,128]{1,0:T(8,128)S(1)}, f32[384,128]{1,0:T(8,128)S(1)}, u32[]{:S(2)}, u32[]{:S(2)}) collective-permute-start(f32[384,128]{1,0:T(8,128)S(1)} %get-tuple-element.85), channel_id=1, source_target_pairs={{8,16},{16,8},{24,32},{32,24},{40,48},{48,40},{72,80},{80,72},{88,... | collective-permute-start | bytes 589832 | tf_op jit(solution)/shard_map/ppermute | solution.py:484
  29.3 2.5 %collective-permute-start.4 = (f32[24,128]{1,0:T(8,128)S(1)}, f32[24,128]{1,0:T(8,128)S(1)}, u32[]{:S(2)}, u32[]{:S(2)}) collective-permute-start(f32[24,128]{1,0:T(8,128)S(1)} %get-tuple-element.99), channel_id=1, source_target_pairs={{192,193},{193,194},{194,195},{195,196},{196,197},{197,198},{198,1... | collective-permute-start | bytes 36872 | tf_op jit(solution)/shard_map/ppermute | solution.py:493
  31.9 4.0 %collective-permute-start.6 = (f32[384,128]{1,0:T(8,128)S(1)}, f32[384,128]{1,0:T(8,128)S(1)}, u32[]{:S(2)}, u32[]{:S(2)}) collective-permute-start(f32[384,128]{1,0:T(8,128)S(1)} %get-tuple-element.108), channel_id=1, source_target_pairs={{192,200},{200,192},{208,216},{216,208},{224,232},{232,224},{240,2... | collective-permute-start | bytes 589832 | tf_op jit(solution)/shard_map/ppermute | solution.py:483
  32.5 3.3 %collective-permute-start.7 = (f32[384,128]{1,0:T(8,128)S(1)}, f32[384,128]{1,0:T(8,128)S(1)}, u32[]{:S(2)}, u32[]{:S(2)}) collective-permute-start(f32[384,128]{1,0:T(8,128)S(1)} %get-tuple-element.109), channel_id=1, source_target_pairs={{200,208},{208,200},{216,224},{224,216},{232,240},{240,232},{201,2... | collective-permute-start | bytes 589832 | tf_op jit(solution)/shard_map/ppermute | solution.py:484
  38.3 10.2 %collective-permute-start.8 = (f32[96,1024]{1,0:T(8,128)S(1)}, f32[96,1024]{1,0:T(8,128)S(1)}, u32[]{:S(2)}, u32[]{:S(2)}) collective-permute-start(f32[96,1024]{1,0:T(8,128)S(1)} %get-tuple-element.110), channel_id=1, source_target_pairs={{192,128},{193,129},{194,130},{195,131},{196,132},{197,133},{198,1... | collective-permute-start | bytes 1179656 | tf_op jit(solution)/shard_map/ppermute | solution.py:581
  39.0 6.9 %collective-permute-start.11 = (f32[128,128]{1,0:T(8,128)S(1)}, f32[128,128]{1,0:T(8,128)S(1)}, u32[]{:S(2)}, u32[]{:S(2)}) collective-permute-start(f32[128,128]{1,0:T(8,128)S(1)} %get-tuple-element.113), channel_id=1, source_target_pairs={{0,1},{1,2},{2,3},{3,4},{4,5},{5,6},{6,7},{64,65},{65,66},{66,67},... | collective-permute-start | bytes 196616 | tf_op jit(solution)/shard_map/ppermute | solution.py:493
  43.2 5.0 %collective-permute-start.12 = (f32[128,128]{1,0:T(8,128)S(1)}, f32[128,128]{1,0:T(8,128)S(1)}, u32[]{:S(2)}, u32[]{:S(2)}) collective-permute-start(f32[128,128]{1,0:T(8,128)S(1)} %get-tuple-element.114), channel_id=1, source_target_pairs={{1,0},{2,1},{3,2},{4,3},{5,4},{6,5},{7,6},{65,64},{66,65},{67,66},... | collective-permute-start | bytes 196616 | tf_op jit(solution)/shard_map/ppermute | solution.py:493
  44.5 3.9 %collective-permute-start.9 = (f32[24,128]{1,0:T(8,128)S(1)}, f32[24,128]{1,0:T(8,128)S(1)}, u32[]{:S(2)}, u32[]{:S(2)}) collective-permute-start(f32[24,128]{1,0:T(8,128)S(1)} %get-tuple-element.111), channel_id=1, source_target_pairs={{192,129},{193,130},{194,131},{195,132},{196,133},{197,134},{198,1... | collective-permute-start | bytes 36872 | tf_op jit(solution)/shard_map/ppermute | solution.py:493
  45.2 3.2 %collective-permute-start.10 = (f32[24,128]{1,0:T(8,128)S(1)}, f32[24,128]{1,0:T(8,128)S(1)}, u32[]{:S(2)}, u32[]{:S(2)}) collective-permute-start(f32[24,128]{1,0:T(8,128)S(1)} %get-tuple-element.112), channel_id=1, source_target_pairs={{193,128},{194,129},{195,130},{196,131},{197,132},{198,133},{199,1... | collective-permute-start | bytes 36872 | tf_op jit(solution)/shard_map/ppermute | solution.py:493
  51.3 4.0 %collective-permute-start.13 = (f32[384,128]{1,0:T(8,128)S(1)}, f32[384,128]{1,0:T(8,128)S(1)}, u32[]{:S(2)}, u32[]{:S(2)}) collective-permute-start(f32[384,128]{1,0:T(8,128)S(1)} %get-tuple-element.120), channel_id=1, source_target_pairs={{128,136},{136,128},{144,152},{152,144},{160,168},{168,160},{176,1... | collective-permute-start | bytes 589832 | tf_op jit(solution)/shard_map/ppermute | solution.py:483
  52.0 3.3 %collective-permute-start.14 = (f32[384,128]{1,0:T(8,128)S(1)}, f32[384,128]{1,0:T(8,128)S(1)}, u32[]{:S(2)}, u32[]{:S(2)}) collective-permute-start(f32[384,128]{1,0:T(8,128)S(1)} %get-tuple-element.121), channel_id=1, source_target_pairs={{136,144},{144,136},{152,160},{160,152},{168,176},{176,168},{137,1... | collective-permute-start | bytes 589832 | tf_op jit(solution)/shard_map/ppermute | solution.py:484
  57.7 2.1 %collective-permute-start.15 = (f32[96,1024]{1,0:T(8,128)S(1)}, f32[96,1024]{1,0:T(8,128)S(1)}, u32[]{:S(2)}, u32[]{:S(2)}) collective-permute-start(f32[96,1024]{1,0:T(8,128)S(1)} %get-tuple-element.122), channel_id=1, source_target_pairs={{128,64},{129,65},{130,66},{131,67},{132,68},{133,69},{134,70},{13... | collective-permute-start | bytes 1179656 | tf_op jit(solution)/shard_map/ppermute | solution.py:581
  62.6 4.1 %collective-permute-start.18 = (f32[384,128]{1,0:T(8,128)S(1)}, f32[384,128]{1,0:T(8,128)S(1)}, u32[]{:S(2)}, u32[]{:S(2)}) collective-permute-start(f32[384,128]{1,0:T(8,128)S(1)} %get-tuple-element.127), channel_id=1, source_target_pairs={{64,72},{72,64},{80,88},{88,80},{96,104},{104,96},{112,120},{120,1... | collective-permute-start | bytes 589832 | tf_op jit(solution)/shard_map/ppermute | solution.py:483
  63.3 3.5 %collective-permute-start.19 = (f32[384,128]{1,0:T(8,128)S(1)}, f32[384,128]{1,0:T(8,128)S(1)}, u32[]{:S(2)}, u32[]{:S(2)}) collective-permute-start(f32[384,128]{1,0:T(8,128)S(1)} %get-tuple-element.128), channel_id=1, source_target_pairs={{72,80},{80,72},{88,96},{96,88},{104,112},{112,104},{73,81},{81,73... | collective-permute-start | bytes 589832 | tf_op jit(solution)/shard_map/ppermute | solution.py:484
  69.2 62.0 %collective-permute-start.20 = (f32[96,1024]{1,0:T(8,128)S(1)}, f32[96,1024]{1,0:T(8,128)S(1)}, u32[]{:S(2)}, u32[]{:S(2)}) collective-permute-start(f32[96,1024]{1,0:T(8,128)S(1)} %get-tuple-element.129), channel_id=1, source_target_pairs={{64,0},{65,1},{66,2},{67,3},{68,4},{69,5},{70,6},{71,7},{72,8},{73... | collective-permute-start | bytes 1179656 | tf_op jit(solution)/shard_map/ppermute | solution.py:581
  70.5 2.0 collective-permute-start.21
  71.1 60.0 %collective-permute-start.22 = (f32[24,128]{1,0:T(8,128)S(1)}, f32[24,128]{1,0:T(8,128)S(1)}, u32[]{:S(2)}, u32[]{:S(2)}) collective-permute-start(f32[24,128]{1,0:T(8,128)S(1)} %get-tuple-element.131), channel_id=1, source_target_pairs={{65,0},{66,1},{67,2},{68,3},{69,4},{70,5},{71,6},{73,8},{74,9},{75... | collective-permute-start | bytes 36872 | tf_op jit(solution)/shard_map/ppermute | solution.py:493
  167.8 16.0 %all-to-all-start.1 = ((f32[32,16,128]{2,1,0:T(8,128)}), f32[32,16,128]{2,1,0:T(8,128)S(1)}, u32[]{:S(2)}, u32[]{:S(2)}) async-start(f32[32,16,128]{2,1,0:T(8,128)} %copy-done.4), calls=%async_computation.1 | async-start | bytes 524288 | tf_op jit(solution)/shard_map/all_to_all | solution.py:507
  183.7 15.6 %collective-permute-start.26 = (f32[512,128]{1,0:T(8,128)S(1)}, f32[512,128]{1,0:T(8,128)S(1)}, u32[]{:S(2)}, u32[]{:S(2)}) collective-permute-start(f32[512,128]{1,0:T(8,128)S(1)} %bitcast.16), channel_id=1, source_target_pairs={{0,8},{8,0},{16,24},{24,16},{32,40},{40,32},{48,56},{56,48},{1,9},... | collective-permute-start | bytes 786440 | tf_op jit(solution)/shard_map/ppermute | solution.py:497
  188.2 2.6 %collective-permute-start.24 = (f32[384,128]{1,0:T(8,128)}, f32[384,128]{1,0:T(8,128)S(1)}, u32[]{:S(2)}, u32[]{:S(2)}) collective-permute-start(f32[384,128]{1,0:T(8,128)} %copy-done.15), channel_id=1, source_target_pairs={{0,8},{8,0},{16,24},{24,16},{32,40},{40,32},{48,56},{56,48},{64,72... | collective-permute-start | bytes 589832 | tf_op jit(solution)/shard_map/ppermute | solution.py:483
  188.2 7.2 %collective-permute-start.25 = (f32[384,128]{1,0:T(8,128)}, f32[384,128]{1,0:T(8,128)S(1)}, u32[]{:S(2)}, u32[]{:S(2)}) collective-permute-start(f32[384,128]{1,0:T(8,128)} %copy-done.14), channel_id=1, source_target_pairs={{8,16},{16,8},{24,32},{32,24},{40,48},{48,40},{72,80},{80,72},{88,... | collective-permute-start | bytes 589832 | tf_op jit(solution)/shard_map/ppermute | solution.py:484
  (20 other events, 94.4 us)

commit v5 on v4

--- a/solution.py
+++ b/solution.py
@@ -74,28 +74,30 @@
 ROW_ROW = ((1,), (1,))
 
 
-def pack_edges(field_ref, right_ref, left_ref):
-    lane = lane_of(FOLD)
-    for edge, out_ref in ((LANES - REACH, right_ref), (0, left_ref)):
-        folded = jnp.zeros((FOLD, LANES), F32)
-        for quarter in range(C // FOLD):
-            part = pl.ds(quarter * FOLD, FOLD)
+ACTS_REACH = 2 * REACH
+ACTS_SIDE = 64
+SIDE = 32
+
+
+def pack_edges(field_ref, right_ref, left_ref, width=REACH, side=SIDE):
+    rows = out_rows = C * side // LANES
+    lane = lane_of(out_rows)
+    for edge, out_ref in ((LANES - width, right_ref), (0, left_ref)):
+        folded = jnp.zeros((out_rows, LANES), F32)
+        for part in range(LANES // side):
             for row in range(ROWS):
-                at = 32 * quarter + REACH * row
-                moved = roll(field_ref[part, block(row)], at - edge)
-                folded = jnp.where((lane >= at) & (lane < at + REACH), moved, folded)
+                at = side * part + width * row
+                moved = roll(field_ref[pl.ds(part * rows, rows), block(row)], at - edge)
+                folded = jnp.where((lane >= at) & (lane < at + width), moved, folded)
         out_ref[...] = folded
 
 
-SIDE = 32
-
-
-def unfold(left, right, quarters, rows):
-    lane = lane_of(rows)
+def unfold(left, right, side=SIDE):
+    lane = lane_of(left.shape[0])
     parts = []
-    for quarter in range(quarters):
-        theirs = roll(left, -32 * quarter)
-        parts.append(jnp.where(lane < SIDE, theirs, jnp.where(lane < 2 * SIDE, roll(right, SIDE - 32 * quarter), 0.0)))
+    for part in range(LANES // side):
+        theirs = roll(left, -side * part)
+        parts.append(jnp.where(lane < side, theirs, jnp.where(lane < 2 * side, roll(right, side - side * part), 0.0)))
     return jnp.concatenate(parts, axis=0)
 
 
@@ -107,8 +109,13 @@
     return row
 
 
-def with_edges(value, strip, row):
-    return value, roll(strip, LANES - REACH - REACH * row), roll(strip, -SIDE - REACH * row)
+NEAR = (REACH, 0, SIDE)
+WIDE = (ACTS_REACH, REACH, ACTS_SIDE)
+
+
+def with_edges(value, strip, row, layout):
+    width, skipped, side = layout
+    return value, roll(strip, LANES - REACH - skipped - width * row), roll(strip, -side - width * row)
 
 
 def tap_of(taps_ref, tap, group):
@@ -118,7 +125,7 @@
 def take_field(acts_ref, field_ref, right_ref, left_ref):
     for row in range(ROWS):
         field_ref[:, block(row)] = acts_ref[pl.ds(row, C, stride=ROWS), :]
-    pack_edges(field_ref, right_ref, left_ref)
+    pack_edges(field_ref, right_ref, left_ref, ACTS_REACH, ACTS_SIDE)
 
 
 def column(row):
@@ -135,9 +142,11 @@
     for copy in copies:
         copy.wait()
     top_ref, kernel_ref, gain_row, bias_row, w_in_ref, b_in_row, w_out_ref, scale_row = held
-    cotan_ref, taps_ref, gain_ref, bias_ref, scale_ref, b_in_ref, w_in_out, w_out_out, w_in_gain_ref, w_out_scale_ref = outs
+    cotan_ref, right_ref, left_ref, taps_ref, gain_ref, bias_ref, scale_ref, b_in_ref = outs[:8]
+    w_in_out, w_out_out, w_in_gain_ref, w_out_scale_ref = outs[8:]
     for row in range(ROWS):
         cotan_ref[:, block(row)] = top_ref[pl.ds(row, C, stride=ROWS), :]
+    pack_edges(cotan_ref, right_ref, left_ref)
     taps = kernel_ref[:, 0, :].T
     for tap in range(TAPS):
         taps_ref[pl.ds(tap * C, C), :] = jnp.broadcast_to(taps[:, tap : tap + 1], (C, LANES))
@@ -164,7 +173,7 @@
         out_ref[pl.ds(STRIP_AT, C), :] = strip_ref[...]
 
 
-def outer_rows(group, a_ref, b_ref, odd):
+def outer_pieces(group, a_ref, b_ref, odd):
     rows = {}
     for index in range(REACH + 1):
         at = pl.ds(index * C + group, GROUP)
@@ -173,18 +182,26 @@
     above, below = rows.pop(REACH)
     found = {}
     for index in range(REACH):
-        found[index - REACH] = with_edges(rows[index][0], above, ROWS - REACH + index)
-        found[ROWS + index] = with_edges(rows[index][1], below, index)
+        found[index - REACH] = (rows[index][0], above, ROWS - REACH + index)
+        found[ROWS + index] = (rows[index][1], below, index)
     return found
 
 
-def own_rows(channels, field_ref, strip_ref):
+def outer_rows(group, a_ref, b_ref, odd, layout):
+    return {at: with_edges(*piece, layout) for at, piece in outer_pieces(group, a_ref, b_ref, odd).items()}
+
+
+def own_pieces(channels, field_ref, strip_ref):
     strip = strip_ref[channels, :]
-    return {row: with_edges(field_ref[channels, block(row)], strip, row) for row in range(ROWS)}
+    return {row: (field_ref[channels, block(row)], strip, row) for row in range(ROWS)}
+
+
+def own_rows(channels, field_ref, strip_ref, layout):
+    return {at: with_edges(*piece, layout) for at, piece in own_pieces(channels, field_ref, strip_ref).items()}
 
 
 def edges(field_ref, left_ref, right_ref, odd_ref, strip_ref, a_ref, b_ref):
-    strip_ref[...] = unfold(left_ref[...], right_ref[...], C // FOLD, FOLD)
+    strip_ref[...] = unfold(left_ref[...], right_ref[...], ACTS_SIDE)
     write_messages(field_ref, strip_ref, odd_ref, a_ref, b_ref)
 
 
@@ -201,7 +218,7 @@
     def conv_group(index, carry):
         group = pl.multiple_of(index * GROUP, GROUP)
         channels = pl.ds(group, GROUP)
-        rows = own_rows(channels, field_ref, strip_ref)
+        rows = own_rows(channels, field_ref, strip_ref, NEAR if flipped else WIDE)
         if flipped:
             sums = [start_ref[channels, block(row)] for row in range(ROWS)]
         else:
@@ -227,7 +244,7 @@
     def conv_group(index, carry):
         group = pl.multiple_of(index * GROUP, GROUP)
         channels = pl.ds(group, GROUP)
-        rows = outer_rows(group, a_ref, b_ref, odd)
+        rows = outer_rows(group, a_ref, b_ref, odd, NEAR if flipped else WIDE)
         sums = [own_ref[channels, block(row)] for row in range(ROWS)]
         for b in range(KS):
             moved = {at: shifted_row(*row, lane, b - REACH) for at, row in rows.items()}
@@ -244,57 +261,67 @@
     lax.fori_loop(0, C // GROUP, conv_group, 0)
 
 
+SPAN = 3 * REACH
+
+
+def side_sums(side, pieces, taps_ref, group, lane):
+    packed = jnp.zeros((GROUP, LANES), F32)
+    for place, at in enumerate(sorted(pieces)):
+        row, strip, index = pieces[at]
+        start = SPAN * place
+        if side == 0:
+            parts = ((strip, ACTS_REACH * index, start, ACTS_REACH), (row, 0, start + ACTS_REACH, REACH))
+        else:
+            parts = ((row, LANES - REACH, start, REACH), (strip, ACTS_SIDE + ACTS_REACH * index, start + REACH, ACTS_REACH))
+        for value, origin, to, width in parts:
+            packed = jnp.where((lane >= to) & (lane < to + width), roll(value, to - origin), packed)
+    total = jnp.zeros((GROUP, LANES), F32)
+    for tap in range(TAPS):
+        total = total + tap_of(taps_ref, tap, group) * roll(packed, -(SPAN * (tap // KS) + tap % KS))
+    result = jnp.zeros((GROUP, LANES), F32)
+    for row in range(ROWS):
+        to = SIDE * side + REACH * row
+        result = jnp.where((lane >= to) & (lane < to + REACH), roll(total, to - SPAN * row), result)
+    return result
+
+
 def forward(
-    own_ref, a_ref, b_ref, odd_ref, taps_ref, gain_ref, bias_ref, w_in_ref, b_in_ref,
-    normed_ref, inv_ref, slope_ref, hidden_ref,
+    field_ref, strip_ref, own_ref, a_ref, b_ref, odd_ref, taps_ref, gain_ref, bias_ref, w_in_ref, b_in_ref,
+    normed_ref, inv_ref, slope_ref, hidden_ref, side_normed_ref, side_inv_ref, side_slope_ref,
 ):
     def put(group, sums):
         for row in range(ROWS):
             normed_ref[pl.ds(group, GROUP), block(row)] = sums[row]
 
     conv_edges(False, own_ref, a_ref, b_ref, odd_ref, taps_ref, put)
+    odd = odd_ref[0] == 1
+    lane = lane_of(GROUP)
+
+    def side_group(index, carry):
+        group = pl.multiple_of(index * GROUP, GROUP)
+        channels = pl.ds(group, GROUP)
+        pieces = outer_pieces(group, a_ref, b_ref, odd) | own_pieces(channels, field_ref, strip_ref)
+        left, right = (side_sums(side, pieces, taps_ref, group, lane) for side in range(2))
+        side_normed_ref[channels, :] = left + right
+        return carry
+
+    lax.fori_loop(0, C // GROUP, side_group, 0)
     w_in = split(w_in_ref[...])
-    for start in range(0, CELLS, CHUNK):
-        cells = pl.ds(start, CHUNK)
-        conv_out = normed_ref[:, cells]
+
+    def finish_cells(conv_out):
         centred = conv_out - jnp.mean(conv_out, axis=0, keepdims=True)
         inv = lax.rsqrt(jnp.mean(centred * centred, axis=0, keepdims=True) + EPSILON)
         normed = centred * inv
-        normed_ref[:, cells] = normed
-        inv_ref[:, cells] = inv
         lifted = normed * gain_ref[...] + bias_ref[...]
         pre_act = product(w_in, split(lifted), COL_COL) + b_in_ref[...]
         gate = 0.5 * (1.0 + lax.erf(pre_act * 0.7071067811865476))
-        hidden_ref[:, cells] = pre_act * gate
-        slope_ref[:, cells] = gate + pre_act * jnp.exp(-0.5 * pre_act * pre_act) * 0.3989422804014327
-
-
-SAVED_SIDE = (HID // 4 + FOLD + GROUP, LANES)
-
-
-def pack_saved(normed_ref, inv_ref, slope_ref, right_ref, left_ref):
-    for edge, out_ref in ((LANES - REACH, right_ref), (0, left_ref)):
-        at = 0
-        for source_ref, rows, quarters in ((slope_ref, HID // 4, 4), (normed_ref, FOLD, 4), (inv_ref, 1, 1)):
-            tall = max(rows, GROUP)
-            lane = lane_of(tall)
-            folded = jnp.zeros((tall, LANES), F32)
-            for quarter in range(quarters):
-                part = pl.ds(quarter * rows, rows)
-                for row in range(ROWS):
-                    to = 32 * quarter + REACH * row
-                    value = jnp.broadcast_to(source_ref[part, block(row)], (tall, LANES))
-                    folded = jnp.where((lane >= to) & (lane < to + REACH), roll(value, to - edge), folded)
-            out_ref[pl.ds(at, tall), :] = folded
-            at += tall
-
-
-def unpack_saved(left_ref, right_ref, normed_ref, inv_ref, slope_ref):
-    at = 0
-    for out_ref, rows, quarters in ((slope_ref, HID // 4, 4), (normed_ref, FOLD, 4), (inv_ref, GROUP, 1)):
-        part = pl.ds(at, rows)
-        out_ref[...] = unfold(left_ref[part, :], right_ref[part, :], quarters, rows)
-        at += rows
+        slope = gate + pre_act * jnp.exp(-0.5 * pre_act * pre_act) * 0.3989422804014327
+        return normed, inv, slope, pre_act * gate
+
+    for start in range(0, CELLS, CHUNK):
+        cells = pl.ds(start, CHUNK)
+        normed_ref[:, cells], inv_ref[:, cells], slope_ref[:, cells], hidden_ref[:, cells] = finish_cells(normed_ref[:, cells])
+    side_normed_ref[...], side_inv_ref[...], side_slope_ref[...], unused = finish_cells(side_normed_ref[...])
 
 
 def grad_at(cotan, w_out, w_in, normed, inv, slope):
@@ -322,17 +349,11 @@
     pass
 
 
-def first_step(cotan_ref, *refs):
-    saved, (grad_ref, right_ref, left_ref) = refs[:5], refs[5:]
-    step_tile((cotan_ref,), saved, grad_ref, ignore)
-    pack_edges(grad_ref, right_ref, left_ref)
-
-
 def step_sides(lefts, rights, weights, strips):
     left, right = sum(ref[...] for ref in lefts), sum(ref[...] for ref in rights)
     normed_ref, inv_ref, slope_ref = strips
-    cotan = unfold(left, right, C // FOLD, FOLD)
-    return grad_at(cotan, *weights, normed_ref[...], inv_ref[:1, :], slope_ref[...])[1]
+    cotan = unfold(left, right)
+    return grad_at(cotan, *weights, normed_ref[...], inv_ref[...], slope_ref[...])[1]
 
 
 def middle_step(cotan_ref, from_left, from_right, odd_ref, *refs):
@@ -343,9 +364,8 @@
 
 
 def last_step(count, *refs):
-    cotans, lefts, rights = refs[:count], refs[count : 2 * count - 1], refs[2 * count - 1 : 3 * count - 2]
-    first_strip, odd_ref = refs[3 * count - 2 : 3 * count]
-    refs = refs[3 * count :]
+    cotans, lefts, rights, odd_ref = refs[:count], refs[count : 2 * count], refs[2 * count : 3 * count], refs[3 * count]
+    refs = refs[3 * count + 1 :]
     saved, strips = refs[:5], refs[5:8]
     grad_ref, strip_ref, a_ref, b_ref, cotan_ref, grad_pre_ref = refs[8:]
 
@@ -354,7 +374,7 @@
         grad_pre_ref[:, cells] = grad_pre
 
     weights = step_tile(cotans, saved, grad_ref, keep)
-    strip_ref[...] = step_sides(lefts, rights, weights, strips) + first_strip[...]
+    strip_ref[...] = step_sides(lefts, rights, weights, strips)
     write_messages(grad_ref, strip_ref, odd_ref, a_ref, b_ref)
 
 
@@ -399,7 +419,7 @@
 
     def taps_group(index, carry):
         group = pl.multiple_of(index * GROUP, GROUP)
-        found = outer_rows(group, a_ref, b_ref, odd) | own_rows(pl.ds(group, GROUP), field_ref, strip_ref)
+        found = outer_rows(group, a_ref, b_ref, odd, WIDE) | own_rows(pl.ds(group, GROUP), field_ref, strip_ref, WIDE)
         rows = [found[row] for row in sorted(found)]
         grads = [grad_ref[pl.ds(group, GROUP), block(row)] for row in range(ROWS)]
         result = jnp.zeros((GROUP, LANES), F32)
@@ -439,6 +459,10 @@
     theirs_ref[...] = payload_ref[half_of(1 - odd_ref[0]), :]
 
 
+def add_halves(mine_ref, theirs_ref, a_ref, b_ref, out_ref):
+    out_ref[...] = mine_ref[...] + theirs_ref[...]
+
+
 def sum_shares(shares_ref, out_ref):
     devices = out_ref.shape[0]
     terms = [shares_ref[device] for device in range(devices)]
@@ -497,7 +521,7 @@
     return lax.ppermute(half, "ty", [(tile, tile ^ 1) for tile in range(lax.axis_size("ty"))])
 
 
-def sum_over_tiles(mine, theirs, beside):
+def sum_over_tiles(mine, theirs, rows):
     columns = lax.axis_size("tx")
     tiles = lax.axis_size("ty")
     groups = [[tile * columns + i for tile in range(odd, tiles, 2) for i in range(columns)] for odd in range(2)]
@@ -506,11 +530,11 @@
     def to_all(shares):
         return lax.all_to_all(shares, TILES, 0, 0, axis_index_groups=groups)
 
-    half = mine + swap_pairs(theirs)
+    (half,) = call(add_halves, [(HALF, LANES)], mine, swap_pairs(theirs), *rows)
     shares = to_all(half.reshape(devices, HALF // devices, LANES))
     (copies,) = call(sum_shares, [shares.shape], shares)
-    mine, beside = lax.optimization_barrier((to_all(copies).reshape(HALF, LANES), beside))
-    return mine, swap_pairs(mine), beside
+    mine = to_all(copies).reshape(HALF, LANES)
+    return mine, swap_pairs(mine)
 
 
 def on_device(acts, top_grad, kernel, ln_gain, ln_bias, w_in, b_in, w_out, layer_scale):
@@ -522,50 +546,41 @@
     edge_outs = [wide, MESSAGE, MESSAGE]
     acts_rows, top_rows = (acts.reshape(C * ROWS, LANES), top_grad.reshape(C * ROWS, LANES))
 
-    field, to_right, to_left = call(take_field, [field_shape, side, side], acts_rows)
+    acts_side = (C * ACTS_SIDE // LANES, LANES)
+    field, to_right, to_left = call(take_field, [field_shape, acts_side, acts_side], acts_rows)
     left, right = to_sides(to_right, to_left, every)
     parameters = (
         top_rows, jnp.transpose(kernel, (1, 0, 2)), ln_gain, ln_bias, w_in[0], b_in, w_out[0].T, layer_scale,
     )
-    cotan, taps, gain, shift_bias, scale, bias_in, weight_in, weight_out, w_in_gain, w_out_scale = call(
+    cotan, top_right, top_left, taps, gain, shift_bias, scale, bias_in, weight_in, weight_out, w_in_gain, w_out_scale = call(
         prepare,
-        [field_shape, (TAPS * C, LANES), (C, 1), (C, 1), (C, 1), (HID, 1), (C, HID), (C, HID), (C, HID), (HID, C)],
+        [field_shape, side, side, (TAPS * C, LANES), (C, 1), (C, 1), (C, 1), (HID, 1), (C, HID), (C, HID), (C, HID), (HID, C)],
         *parameters, scratch=[p.shape for p in parameters] + [pltpu.SemaphoreType.DMA((len(parameters),))], copied=True,
     )
+    top_left, top_right = to_sides(top_right, top_left, (sections - 1,))
     strip, message_a, message_b = call(edges, edge_outs, field, left, right, odd)
     from_a, from_b = swap_rows(message_a, message_b, every)
     (own,) = call(functools.partial(conv_own, False), [field_shape], field, strip, taps, flops=CONV_FLOPS)
     around = (field, strip, from_a, from_b, odd)
-    normed, inv, slope, hidden = call(
+    normed, inv, slope, hidden, *strips = call(
         forward,
-        [field_shape, (1, CELLS), hidden_shape, hidden_shape],
-        own, from_a, from_b, odd, taps, gain, shift_bias, weight_in, bias_in,
+        [field_shape, (1, CELLS), hidden_shape, hidden_shape, wide, (1, LANES), (HID, LANES)],
+        field, strip, own, from_a, from_b, odd, taps, gain, shift_bias, weight_in, bias_in,
     )
     saved = (normed, inv, slope, w_in_gain, w_out_scale)
 
     cotan = cotan * is_last
-    cotans, lefts, rights = [cotan], [], []
-    strips = ()
+    cotans, lefts, rights = [cotan], [top_left], [top_right]
     for section in reversed(every):
         only = (section,) if section else every
-        if section == sections - 1:
-            grad, to_right, to_left = call(first_step, [field_shape, side, side], cotan, *saved)
-            grad_left, grad_right = to_sides(to_right, to_left, only)
-            tile, grad = lax.optimization_barrier((saved[:3], grad))
-            saved_right, saved_left = call(pack_saved, [SAVED_SIDE, SAVED_SIDE], *tile)
-            grad_left, saved_right, saved_left = lax.optimization_barrier((grad_left, saved_right, saved_left))
-            saved_sides = to_sides(saved_right, saved_left, range(sections - 1))
-            first_strip, message_a, message_b = call(edges, edge_outs, grad, grad_left, grad_right, odd)
-            grad_strip = first_strip
-            strips = call(unpack_saved, [wide, (GROUP, LANES), (HID, LANES)], *saved_sides)
-        elif section:
+        if section:
             grad, grad_strip, message_a, message_b = call(
                 middle_step, [field_shape] + edge_outs, cotan, lefts[-1], rights[-1], odd, *saved, *strips
             )
         else:
             grad, grad_strip, message_a, message_b, cotan, grad_pre = call(
                 functools.partial(last_step, len(cotans)), [field_shape] + edge_outs + [field_shape, hidden_shape],
-                *cotans, *lefts, *rights, first_strip, odd, *saved, *strips,
+                *cotans, *lefts, *rights, odd, *saved, *strips,
             )
             payload = call(
                 parameter_terms, [(HALF, LANES)] * 2,
@@ -578,12 +593,12 @@
         )
         if section:
             cotan, to_right, to_left = call(finish, [field_shape, side, side], own, grad_a, grad_b, odd, taps)
+            from_left, from_right = to_sides(to_right, to_left, only, 1)
             cotan = lax.ppermute(cotan, "section", [(section, section - 1)])
-            from_left, from_right = to_sides(to_right, to_left, only, 1)
             cotans.append(cotan)
             lefts.append(from_left)
             rights.append(from_right)
-    *payload, own = sum_over_tiles(*payload, own)
+    payload = sum_over_tiles(*payload, (grad_a, grad_b))
     (input_grad,) = call(last_finish, [(C * ROWS, LANES)], own, grad_a, grad_b, odd, taps)
     grad_kernel, grad_gain, grad_bias, grad_w_in, grad_b_in, grad_w_out, grad_scale = call(
         parameter_grads,

time: 201 us -> 209 us (1.040)
  blocking collectives: 24.5 us -> 42 us
  waiting for transfers between devices: 77 us -> 61.1 us
  Pallas kernels: 48.6 us -> 55.3 us
    all_to_all x1 -> x2, blocking collectives: 24.5 us -> 42 us  [to_all(): return lax.all_to_all(shares, TILES, 0, 0, axis_index_groups=groups)]
    ppermute x5, starting transfers between devices: 7.93 us -> 16.7 us  [swap_rows(): lax.ppermute(message_b, axes, pairs('ty', sections, True))]
    all_to_all x1 -> x0, waiting for transfers between devices: 8.55 us -> none  [to_all(): return lax.all_to_all(shares, TILES, 0, 0, axis_index_groups=groups)]
    pallas_call x23 -> x21, Pallas kernels: 48.6 us -> 55.3 us  [call(): pl.pallas_call(kernel, out_shape=[jax.ShapeDtypeStruct(shape, F32) for sh...]
    all_to_all x1 -> x0, starting transfers between devices: 4.05 us -> none  [to_all(): return lax.all_to_all(shares, TILES, 0, 0, axis_index_groups=groups)]
    ppermute x6 -> x5, starting transfers between devices: 10.9 us -> 7.17 us  [to_sides(): lax.ppermute(to_right, axes, right)]
    ppermute x6 -> x5, waiting for transfers between devices: 61.1 us -> 57.6 us  [to_sides(): lax.ppermute(to_left, axes, left)]
    ppermute x2, starting transfers between devices: 4.57 us -> 2.25 us  [swap_pairs(): lax.ppermute(half, 'ty', [(tile, tile ^ 1) for tile in range(lax.axis_siz...]
  transfers between devices with their start and end apart: 28 -> 25, of which waited for: 6 -> 3; matrix products, arithmetic and copies ran while one was open for 0% -> 0% of each run, Pallas kernels for 9% -> 13%
where the time goes in v5:
time: 209 us; the launch traced here: 208 us
  waiting for transfers between devices  61.1 us (29%)
  Pallas kernels  55.3 us (26%)
  blocking collectives  42 us (20%)
  starting transfers between devices  37.8 us (18%)
  local copies, waits for them, and re-layouts  9.23 us (4%)
    ppermute x5, waiting for transfers between devices, to_sides(): lax.ppermute(to_left, axes, left)  57.6 us
    pallas_call x21, Pallas kernels, call(): pl.pallas_call(kernel, out_shape=[jax.ShapeDtypeStruct(shape, F32) for sh...  55.3 us
    all_to_all x2, blocking collectives, to_all(): return lax.all_to_all(shares, TILES, 0, 0, axis_index_groups=groups)  42 us
    ppermute x5, starting transfers between devices, swap_rows(): lax.ppermute(message_b, axes, pairs('ty', sections, True))  16.7 us
    unnamed x28, local copies, waits for them, and re-layouts  9.23 us
    ppermute x5, starting transfers between devices, to_sides(): lax.ppermute(to_right, axes, right)  7.17 us
    ppermute x5, starting transfers between devices, to_sides(): lax.ppermute(to_left, axes, left)  5.47 us
  transfers between devices with their start and end apart: 25, of which 3 were waited for; matrix products, arithmetic and copies ran while one was open for 0% of the time, Pallas kernels for 13%

profile of v5, /device:TPU:1, one launch (start us, length us, event | category | flops | bytes accessed | tf_op | source)
XLA Modules:
  0.0 207.6 jit_solution(4504735140878869194)
XLA Ops:
  2.5 4.5 %collective-permute-start.2 = (f32[48,128]{1,0:T(8,128)}, f32[48,128]{1,0:T(8,128)}, u32[]{:S(2)}, u32[]{:S(2)}) collective-permute-start(f32[48,128]{1,0:T(8,128)} %get-tuple-element.73), channel_id=1, source_target_pairs={{0,1},{1,2},{2,3},{3,4},{4,5},{5,6},{6,7},{64,65},{65,66},{66,67},... | collective-permute-start | bytes 73736 | tf_op jit(solution)/shard_map/ppermute | solution.py:517
  14.5 2.3 %shard_map.152 = (f32[96,1024]{1,0:T(8,128)S(1)}, f32[24,128]{1,0:T(8,128)}, f32[24,128]{1,0:T(8,128)}, f32[4704,128]{1,0:T(8,128)S(1)}, f32[96,1]{1,0:T(8,128)S...) custom-call(f32[768,128]{1,0:T(8,128)S(1)} %bitcast.20, ...), custom_call_target="tpu_custom_call" | custom-call | tf_op jit(solution)/shard_map/pallas_call | solution.py:36
  22.8 3.1 %collective-permute-start.5 = (f32[384,128]{1,0:T(8,128)S(1)}, f32[384,128]{1,0:T(8,128)S(1)}, u32[]{:S(2)}, u32[]{:S(2)}) collective-permute-start(f32[384,128]{1,0:T(8,128)S(1)} %get-tuple-element.78), channel_id=1, source_target_pairs={{8,16},{16,8},{24,32},{32,24},{40,48},{48,40},{72,80},{80,72},{88,... | collective-permute-start | bytes 589832 | tf_op jit(solution)/shard_map/ppermute | solution.py:508
  26.9 2.6 %shard_map.155.own_ref = f32[96,1024]{1,0:T(8,128)S(1)} custom-call(f32[96,1024]{1,0:T(8,128)S(1)} %get-tuple-element.72.field_ref.refs_0_, f32[96,128]{1,0:T(8,128)S(1)} %get-tuple-element.75.refs_1_.strip_ref, f32[4704,128]{1,0:T(8,128)S(1)} %get-tuple-element.76.refs_2_.taps_ref.refs_3_), custom_call_target="tpu_custom_call" | custom-call | flops 9633792 | tf_op jit(solution)/shard_map/pallas_call | solution.py:36
  29.8 7.8 %shard_map.156 = (f32[96,1024]{1,0:T(8,128)S(1)}, f32[1,1024]{1,0:T(1,128)S(1)}, f32[384,1024]{1,0:T(8,128)S(1)}, f32[384,1024]{1,0:T(8,128)S(1)}, f32[96,128]{1...) custom-call(f32[96,1024]{1,0:T(8,128)S(1)} %get-tuple-element.72.field_ref.refs_0_, ...), custom_call_target="tpu_custom_call" | custom-call | tf_op jit(solution)/shard_map/pallas_call | solution.py:36
  37.6 3.5 %shard_map.157 = (f32[96,1024]{1,0:T(8,128)S(1)}, f32[96,128]{1,0:T(8,128)S(1)}, f32[384,128]{1,0:T(8,128)S(1)}, f32[384,128]{1,0:T(8,128)S(1)}) custom-call(f32[96,1024]{1,0:T(8,128)S(1)} %broadcast_multiply_fusion.cotan_ref.refs_0_, f32[24,128]{1,0:T(8,128)S(1)} %collective-permute-done.from_left.refs_4_, ...), custom_call_target="tpu_custom_call" | custom-call | tf_op jit(solution)/shard_map/pallas_call | solution.py:36
  42.5 2.6 %shard_map.158.own_ref = f32[96,1024]{1,0:T(8,128)S(1)} custom-call(f32[96,1024]{1,0:T(8,128)S(1)} %broadcast_multiply_fusion.cotan_ref.refs_0_, f32[96,1024]{1,0:T(8,128)S(1)} %get-tuple-element.91.refs_1_, f32[96,128]{1,0:T(8,128)S(1)} %get-tuple-element.92.refs_2_, f32[4704,128]{1,0:T(8,128)S(1)} %get-tuple-element.76.refs_2_.taps_ref.refs_3_), custom_call_target="tpu_custom_call" | custom-call | flops 9633792 | tf_op jit(solution)/shard_map/pallas_call | solution.py:36
  45.1 2.4 %shard_map.159 = (f32[96,1024]{1,0:T(8,128)S(1)}, f32[24,128]{1,0:T(8,128)S(1)}, f32[24,128]{1,0:T(8,128)S(1)}) custom-call(f32[96,1024]{1,0:T(8,128)S(1)} %shard_map.158.own_ref, f32[384,128]{1,0:T(8,128)S(1)} %collective-permute-done.6.a_ref, f32[384,128]{1,0:T(8,128)S(1)} %collective-permute-done.7.b_ref, s32[1]{0:T(128)} %bitcast.5.odd_ref.refs_12_, ...), custom_call_target="tpu_custom_call" | custom-call | tf_op jit(solution)/shard_map/pallas_call | solution.py:36
  49.6 2.8 %shard_map.160 = (f32[96,1024]{1,0:T(8,128)S(1)}, f32[96,128]{1,0:T(8,128)S(1)}, f32[384,128]{1,0:T(8,128)S(1)}, f32[384,128]{1,0:T(8,128)S(1)}) custom-call(f32[96,1024]{1,0:T(8,128)S(1)} %collective-permute-done.8.cotan_ref.refs_0_.refs_1_, f32[24,128]{1,0:T(8,128)S(1)} %collective-permute-done.9.from_left.refs_5_, ...), custom_call_target="tpu_custom_call" | custom-call | tf_op jit(solution)/shard_map/pallas_call | solution.py:36
  53.8 2.6 %shard_map.161.own_ref = f32[96,1024]{1,0:T(8,128)S(1)} custom-call(f32[96,1024]{1,0:T(8,128)S(1)} %collective-permute-done.8.cotan_ref.refs_0_.refs_1_, f32[96,1024]{1,0:T(8,128)S(1)} %get-tuple-element.98.refs_1_, f32[96,128]{1,0:T(8,128)S(1)} %get-tuple-element.99.refs_2_, f32[4704,128]{1,0:T(8,128)S(1)} %get-tuple-element.76.refs_2_.taps_ref.refs_3_), custom_call_target="tpu_custom_call" | custom-call | flops 9633792 | tf_op jit(solution)/shard_map/pallas_call | solution.py:36
  56.4 2.4 %shard_map.162 = (f32[96,1024]{1,0:T(8,128)S(1)}, f32[24,128]{1,0:T(8,128)S(1)}, f32[24,128]{1,0:T(8,128)S(1)}) custom-call(f32[96,1024]{1,0:T(8,128)S(1)} %shard_map.161.own_ref, f32[384,128]{1,0:T(8,128)S(1)} %collective-permute-done.11.a_ref, f32[384,128]{1,0:T(8,128)S(1)} %collective-permute-done.12.b_ref, s32[1]{0:T(128)} %bitcast.5.odd_ref.refs_12_, ...), custom_call_target="tpu_custom_call" | custom-call | tf_op jit(solution)/shard_map/pallas_call | solution.py:36
  60.9 2.8 %shard_map.163 = (f32[96,1024]{1,0:T(8,128)S(1)}, f32[96,128]{1,0:T(8,128)S(1)}, f32[384,128]{1,0:T(8,128)S(1)}, f32[384,128]{1,0:T(8,128)S(1)}) custom-call(f32[96,1024]{1,0:T(8,128)S(1)} %collective-permute-done.13.cotan_ref.refs_0_.refs_2_, f32[24,128]{1,0:T(8,128)S(1)} %collective-permute-done.14.from_left.refs_6_, ...), custom_call_target="tpu_custom_call" | custom-call | tf_op jit(solution)/shard_map/pallas_call | solution.py:36
  65.1 2.6 %shard_map.164.own_ref = f32[96,1024]{1,0:T(8,128)S(1)} custom-call(f32[96,1024]{1,0:T(8,128)S(1)} %collective-permute-done.13.cotan_ref.refs_0_.refs_2_, f32[96,1024]{1,0:T(8,128)S(1)} %get-tuple-element.105.refs_1_, f32[96,128]{1,0:T(8,128)S(1)} %get-tuple-element.106.refs_2_, f32[4704,128]{1,0:T(8,128)S(1)} %get-tuple-element.76.refs_2_.taps_ref.refs_3_), custom_call_target="tpu_custom_call" | custom-call | flops 9633792 | tf_op jit(solution)/shard_map/pallas_call | solution.py:36
  67.7 2.4 %shard_map.165 = (f32[96,1024]{1,0:T(8,128)S(1)}, f32[24,128]{1,0:T(8,128)S(1)}, f32[24,128]{1,0:T(8,128)S(1)}) custom-call(f32[96,1024]{1,0:T(8,128)S(1)} %shard_map.164.own_ref, f32[384,128]{1,0:T(8,128)S(1)} %collective-permute-done.16.a_ref, f32[384,128]{1,0:T(8,128)S(1)} %collective-permute-done.17.b_ref, s32[1]{0:T(128)} %bitcast.5.odd_ref.refs_12_, ...), custom_call_target="tpu_custom_call" | custom-call | tf_op jit(solution)/shard_map/pallas_call | solution.py:36
  73.8 57.5 %collective-permute-done.20.refs_11_ = f32[24,128]{1,0:T(8,128)S(1)} collective-permute-done((f32[24,128]{1,0:T(8,128)S(1)}, f32[24,128]{1,0:T(8,128)S(1)}, u32[]{:S(2)}, u32[]{:S(2)}) %collective-permute-start.20) | collective-permute-done | bytes 12320 | tf_op jit(solution)/shard_map/ppermute | solution.py:517
  131.3 3.6 %shard_map.166 = (f32[96,1024]{1,0:T(8,128)S(1)}, f32[96,128]{1,0:T(8,128)S(1)}, f32[384,128]{1,0:T(8,128)S(1)}, f32[384,128]{1,0:T(8,128)S(1)}, f32[96,1024]{1,0:T(8,128)S(1)}, /*index=5*/f32[384,1024]{1,0:T(8,128)S(1)}) custom-call(f32[96,1024]{1,0:T(8,128)S(1)} %broadcast_multiply_fusion.cotan_ref.refs_0_, ...), custom_call_target="tpu_custom_call" | custom-call | tf_op jit(solution)/shard_map/pallas_call | solution.py:36
  134.9 6.7 %shard_map.169 = (f32[512,128]{1,0:T(8,128)S(1)}, f32[512,128]{1,0:T(8,128)S(1)}) custom-call(f32[96,1024]{1,0:T(8,128)S(1)} %get-tuple-element.72.field_ref.refs_0_, f32[96,128]{1,0:T(8,128)S(1)} %get-tuple-element.75.refs_1_.strip_ref, f32[384,128]{1,0:T(8,128)S(1)} %collective-permute-done.4.a_ref, f32[384,128]{1,0:T(8,128)S(1)} %collective-permute-done.5.b_ref, ...), custom_call_target="tpu_custom_call" | custom-call | flops 38535168 | tf_op jit(solution)/shard_map/pallas_call | solution.py:36
  142.2 11.6 %collective-permute-start.22 = (f32[384,128]{1,0:T(8,128)S(1)}, f32[384,128]{1,0:T(8,128)S(1)}, u32[]{:S(2)}, u32[]{:S(2)}) collective-permute-start(f32[384,128]{1,0:T(8,128)S(1)} %get-tuple-element.116), channel_id=1, source_target_pairs={{8,16},{16,8},{24,32},{32,24},{40,48},{48,40},{72,80},{80,72},{88,... | collective-permute-start | bytes 589832 | tf_op jit(solution)/shard_map/ppermute | solution.py:508
  153.8 3.3 %collective-permute-done.22.b_ref = f32[384,128]{1,0:T(8,128)S(1)} collective-permute-done((f32[384,128]{1,0:T(8,128)S(1)}, f32[384,128]{1,0:T(8,128)S(1)}, u32[]{:S(2)}, u32[]{:S(2)}) %collective-permute-start.22) | collective-permute-done | bytes 196640 | tf_op jit(solution)/shard_map/ppermute | solution.py:508
  157.1 23.3 %all_to_all.10.shares_ref = f32[32,16,128]{2,1,0:T(8,128)S(1)} all-to-all(f32[32,16,128]{2,1,0:T(8,128)S(1)} %bitcast.18), channel_id=1, replica_groups={{0,1,2,3,4,5,6,7,16,17,18,19,20,21,22,23,32,33,34,35,36,37,38,39,48,49,..., dimensions={0} | all-to-all | bytes 524288 | tf_op jit(solution)/shard_map/all_to_all | solution.py:531
  180.4 18.7 %all_to_all.11 = f32[32,16,128]{2,1,0:T(8,128)S(1)} all-to-all(f32[32,16,128]{2,1,0:T(8,128)S(1)} %shard_map.171), channel_id=1, replica_groups={{0,1,2,3,4,5,6,7,16,17,18,19,20,21,22,23,32,33,34,35,36,37,38,39,48,49,..., dimensions={0} | all-to-all | bytes 524288 | tf_op jit(solution)/shard_map/all_to_all | solution.py:531
  199.2 2.2 %collective-permute-start.24 = (f32[512,128]{1,0:T(8,128)S(1)}, f32[512,128]{1,0:T(8,128)S(1)}, u32[]{:S(2)}, u32[]{:S(2)}) collective-permute-start(f32[512,128]{1,0:T(8,128)S(1)} %bitcast.16), channel_id=1, source_target_pairs={{0,8},{8,0},{16,24},{24,16},{32,40},{40,32},{48,56},{56,48},{1,9},... | collective-permute-start | bytes 786440 | tf_op jit(solution)/shard_map/ppermute | solution.py:521
  201.3 2.6 %shard_map.167.own_ref = f32[96,1024]{1,0:T(8,128)S(1)} custom-call(f32[96,1024]{1,0:T(8,128)S(1)} %get-tuple-element.112.refs_0_.cotan_ref, f32[96,1024]{1,0:T(8,128)S(1)} %get-tuple-element.113.refs_1_.grad_ref, f32[96,128]{1,0:T(8,128)S(1)} %get-tuple-element.114.refs_2_, f32[4704,128]{1,0:T(8,128)S(1)} %get-tuple-element.76.refs_2_.taps_ref.refs_3_), custom_call_target="tpu_custom_call" | custom-call | flops 9633792 | tf_op jit(solution)/shard_map/pallas_call | solution.py:36
  203.9 2.9 %shard_map.168 = f32[768,128]{1,0:T(8,128)} custom-call(f32[96,1024]{1,0:T(8,128)S(1)} %shard_map.167.own_ref, f32[384,128]{1,0:T(8,128)S(1)} %collective-permute-done.21.a_ref, f32[384,128]{1,0:T(8,128)S(1)} %collective-permute-done.22.b_ref, s32[1]{0:T(128)} %bitcast.5.odd_ref.refs_12_, f32[4704,128]{1,0:T(8,128)S(1)} %get-tuple-element.76.refs_2_.taps_ref.refs_3_), custom_call_target="tpu_custom_call" | custom-call | tf_op jit(solution)/shard_map/pallas_call | solution.py:36
  (78 shorter events, 29.5 us)
Async XLA Ops:
  2.5 18.4 %collective-permute-start.2 = (f32[48,128]{1,0:T(8,128)}, f32[48,128]{1,0:T(8,128)}, u32[]{:S(2)}, u32[]{:S(2)}) collective-permute-start(f32[48,128]{1,0:T(8,128)} %get-tuple-element.73), channel_id=1, source_target_pairs={{0,1},{1,2},{2,3},{3,4},{4,5},{5,6},{6,7},{64,65},{65,66},{66,67},... | collective-permute-start | bytes 73736 | tf_op jit(solution)/shard_map/ppermute | solution.py:517
  7.0 13.8 %collective-permute-start.3 = (f32[48,128]{1,0:T(8,128)}, f32[48,128]{1,0:T(8,128)}, u32[]{:S(2)}, u32[]{:S(2)}) collective-permute-start(f32[48,128]{1,0:T(8,128)} %get-tuple-element.74), channel_id=1, source_target_pairs={{1,0},{2,1},{3,2},{4,3},{5,4},{6,5},{7,6},{65,64},{66,65},{67,66},... | collective-permute-start | bytes 73736 | tf_op jit(solution)/shard_map/ppermute | solution.py:517
  18.9 18.7 %collective-permute-start = (f32[24,128]{1,0:T(8,128)}, f32[24,128]{1,0:T(8,128)S(1)}, u32[]{:S(2)}, u32[]{:S(2)}) collective-permute-start(f32[24,128]{1,0:T(8,128)} %get-tuple-element.70), channel_id=1, source_target_pairs={{192,193},{193,194},{194,195},{195,196},{196,197},{197,198},{198,1... | collective-permute-start | bytes 36872 | tf_op jit(solution)/shard_map/ppermute | solution.py:517
  19.6 18.0 %collective-permute-start.1 = (f32[24,128]{1,0:T(8,128)}, f32[24,128]{1,0:T(8,128)}, u32[]{:S(2)}, u32[]{:S(2)}) collective-permute-start(f32[24,128]{1,0:T(8,128)} %get-tuple-element.71), channel_id=1, source_target_pairs={{193,192},{194,193},{195,194},{196,195},{197,196},{198,197},{199,1... | collective-permute-start | bytes 36872 | tf_op jit(solution)/shard_map/ppermute | solution.py:517
  21.8 7.8 %collective-permute-start.4 = (f32[384,128]{1,0:T(8,128)S(1)}, f32[384,128]{1,0:T(8,128)S(1)}, u32[]{:S(2)}, u32[]{:S(2)}) collective-permute-start(f32[384,128]{1,0:T(8,128)S(1)} %get-tuple-element.77), channel_id=1, source_target_pairs={{0,8},{8,0},{16,24},{24,16},{32,40},{40,32},{48,56},{56,48},{64,72... | collective-permute-start | bytes 589832 | tf_op jit(solution)/shard_map/ppermute | solution.py:507
  22.8 7.0 %collective-permute-start.5 = (f32[384,128]{1,0:T(8,128)S(1)}, f32[384,128]{1,0:T(8,128)S(1)}, u32[]{:S(2)}, u32[]{:S(2)}) collective-permute-start(f32[384,128]{1,0:T(8,128)S(1)} %get-tuple-element.78), channel_id=1, source_target_pairs={{8,16},{16,8},{24,32},{32,24},{40,48},{48,40},{72,80},{80,72},{88,... | collective-permute-start | bytes 589832 | tf_op jit(solution)/shard_map/ppermute | solution.py:508
  41.2 4.0 %collective-permute-start.6 = (f32[384,128]{1,0:T(8,128)S(1)}, f32[384,128]{1,0:T(8,128)S(1)}, u32[]{:S(2)}, u32[]{:S(2)}) collective-permute-start(f32[384,128]{1,0:T(8,128)S(1)} %get-tuple-element.93), channel_id=1, source_target_pairs={{192,200},{200,192},{208,216},{216,208},{224,232},{232,224},{240,2... | collective-permute-start | bytes 589832 | tf_op jit(solution)/shard_map/ppermute | solution.py:507
  41.9 3.3 %collective-permute-start.7 = (f32[384,128]{1,0:T(8,128)S(1)}, f32[384,128]{1,0:T(8,128)S(1)}, u32[]{:S(2)}, u32[]{:S(2)}) collective-permute-start(f32[384,128]{1,0:T(8,128)S(1)} %get-tuple-element.94), channel_id=1, source_target_pairs={{200,208},{208,200},{216,224},{224,216},{232,240},{240,232},{201,2... | collective-permute-start | bytes 589832 | tf_op jit(solution)/shard_map/ppermute | solution.py:508
  47.6 2.1 collective-permute-start.8
  48.3 1.3 collective-permute-start.9
  48.9 0.7 collective-permute-start.10
  52.5 4.0 %collective-permute-start.11 = (f32[384,128]{1,0:T(8,128)S(1)}, f32[384,128]{1,0:T(8,128)S(1)}, u32[]{:S(2)}, u32[]{:S(2)}) collective-permute-start(f32[384,128]{1,0:T(8,128)S(1)} %get-tuple-element.100), channel_id=1, source_target_pairs={{128,136},{136,128},{144,152},{152,144},{160,168},{168,160},{176,1... | collective-permute-start | bytes 589832 | tf_op jit(solution)/shard_map/ppermute | solution.py:507
  53.1 3.3 %collective-permute-start.12 = (f32[384,128]{1,0:T(8,128)S(1)}, f32[384,128]{1,0:T(8,128)S(1)}, u32[]{:S(2)}, u32[]{:S(2)}) collective-permute-start(f32[384,128]{1,0:T(8,128)S(1)} %get-tuple-element.101), channel_id=1, source_target_pairs={{136,144},{144,136},{152,160},{160,152},{168,176},{176,168},{137,1... | collective-permute-start | bytes 589832 | tf_op jit(solution)/shard_map/ppermute | solution.py:508
  58.9 2.1 collective-permute-start.13
  59.6 1.3 collective-permute-start.14
  63.7 4.0 %collective-permute-start.16 = (f32[384,128]{1,0:T(8,128)S(1)}, f32[384,128]{1,0:T(8,128)S(1)}, u32[]{:S(2)}, u32[]{:S(2)}) collective-permute-start(f32[384,128]{1,0:T(8,128)S(1)} %get-tuple-element.107), channel_id=1, source_target_pairs={{64,72},{72,64},{80,88},{88,80},{96,104},{104,96},{112,120},{120,1... | collective-permute-start | bytes 589832 | tf_op jit(solution)/shard_map/ppermute | solution.py:507
  64.4 3.3 %collective-permute-start.17 = (f32[384,128]{1,0:T(8,128)S(1)}, f32[384,128]{1,0:T(8,128)S(1)}, u32[]{:S(2)}, u32[]{:S(2)}) collective-permute-start(f32[384,128]{1,0:T(8,128)S(1)} %get-tuple-element.108), channel_id=1, source_target_pairs={{72,80},{80,72},{88,96},{96,88},{104,112},{112,104},{73,81},{81,73... | collective-permute-start | bytes 589832 | tf_op jit(solution)/shard_map/ppermute | solution.py:508
  70.2 61.2 %collective-permute-start.18 = (f32[96,1024]{1,0:T(8,128)S(1)}, f32[96,1024]{1,0:T(8,128)S(1)}, u32[]{:S(2)}, u32[]{:S(2)}) collective-permute-start(f32[96,1024]{1,0:T(8,128)S(1)} %get-tuple-element.109), channel_id=1, source_target_pairs={{64,0},{65,1},{66,2},{67,3},{68,4},{69,5},{70,6},{71,7},{72,8},{73... | collective-permute-start | bytes 1179656 | tf_op jit(solution)/shard_map/ppermute | solution.py:597
  71.5 2.3 %collective-permute-start.19 = (f32[24,128]{1,0:T(8,128)S(1)}, f32[24,128]{1,0:T(8,128)S(1)}, u32[]{:S(2)}, u32[]{:S(2)}) collective-permute-start(f32[24,128]{1,0:T(8,128)S(1)} %get-tuple-element.110), channel_id=1, source_target_pairs={{64,1},{65,2},{66,3},{67,4},{68,5},{69,6},{70,7},{72,9},{73,10},{7... | collective-permute-start | bytes 36872 | tf_op jit(solution)/shard_map/ppermute | solution.py:517
  72.1 59.2 %collective-permute-start.20 = (f32[24,128]{1,0:T(8,128)S(1)}, f32[24,128]{1,0:T(8,128)S(1)}, u32[]{:S(2)}, u32[]{:S(2)}) collective-permute-start(f32[24,128]{1,0:T(8,128)S(1)} %get-tuple-element.111), channel_id=1, source_target_pairs={{65,0},{66,1},{67,2},{68,3},{69,4},{70,5},{71,6},{73,8},{74,9},{75... | collective-permute-start | bytes 36872 | tf_op jit(solution)/shard_map/ppermute | solution.py:517
  141.6 15.5 %collective-permute-start.23 = (f32[512,128]{1,0:T(8,128)S(1)}, f32[512,128]{1,0:T(8,128)S(1)}, u32[]{:S(2)}, u32[]{:S(2)}) collective-permute-start(f32[512,128]{1,0:T(8,128)S(1)} %get-tuple-element.122), channel_id=1, source_target_pairs={{0,8},{8,0},{16,24},{24,16},{32,40},{40,32},{48,56},{56,48},{1,9},... | collective-permute-start | bytes 786440 | tf_op jit(solution)/shard_map/ppermute | solution.py:521
  141.7 12.1 %collective-permute-start.21 = (f32[384,128]{1,0:T(8,128)S(1)}, f32[384,128]{1,0:T(8,128)S(1)}, u32[]{:S(2)}, u32[]{:S(2)}) collective-permute-start(f32[384,128]{1,0:T(8,128)S(1)} %get-tuple-element.115), channel_id=1, source_target_pairs={{0,8},{8,0},{16,24},{24,16},{32,40},{40,32},{48,56},{56,48},{64,72... | collective-permute-start | bytes 589832 | tf_op jit(solution)/shard_map/ppermute | solution.py:507
  142.2 14.9 %collective-permute-start.22 = (f32[384,128]{1,0:T(8,128)S(1)}, f32[384,128]{1,0:T(8,128)S(1)}, u32[]{:S(2)}, u32[]{:S(2)}) collective-permute-start(f32[384,128]{1,0:T(8,128)S(1)} %get-tuple-element.116), channel_id=1, source_target_pairs={{8,16},{16,8},{24,32},{32,24},{40,48},{48,40},{72,80},{80,72},{88,... | collective-permute-start | bytes 589832 | tf_op jit(solution)/shard_map/ppermute | solution.py:508
  199.2 7.7 %collective-permute-start.24 = (f32[512,128]{1,0:T(8,128)S(1)}, f32[512,128]{1,0:T(8,128)S(1)}, u32[]{:S(2)}, u32[]{:S(2)}) collective-permute-start(f32[512,128]{1,0:T(8,128)S(1)} %bitcast.16), channel_id=1, source_target_pairs={{0,8},{8,0},{16,24},{24,16},{32,40},{40,32},{48,56},{56,48},{1,9},... | collective-permute-start | bytes 786440 | tf_op jit(solution)/shard_map/ppermute | solution.py:521
  (15 other events, 75.5 us)

commit v6 on v5

--- a/solution.py
+++ b/solution.py
@@ -122,10 +122,17 @@
     return taps_ref[pl.ds(tap * C + group, GROUP), :]
 
 
-def take_field(acts_ref, field_ref, right_ref, left_ref):
+ACTS_ROWS = C * ACTS_SIDE // LANES
+SIDE_MESSAGE = (ACTS_ROWS + FOLD, LANES)
+
+
+def take_fields(acts_ref, top_ref, field_ref, cotan_ref, right_ref, left_ref):
     for row in range(ROWS):
         field_ref[:, block(row)] = acts_ref[pl.ds(row, C, stride=ROWS), :]
-    pack_edges(field_ref, right_ref, left_ref, ACTS_REACH, ACTS_SIDE)
+        cotan_ref[:, block(row)] = top_ref[pl.ds(row, C, stride=ROWS), :]
+    wide, near = pl.ds(0, ACTS_ROWS), pl.ds(ACTS_ROWS, FOLD)
+    pack_edges(field_ref, right_ref.at[wide, :], left_ref.at[wide, :], ACTS_REACH, ACTS_SIDE)
+    pack_edges(cotan_ref, right_ref.at[near, :], left_ref.at[near, :])
 
 
 def column(row):
@@ -133,7 +140,7 @@
 
 
 def prepare(*refs):
-    count = 8
+    count = 7
     sources, outs, held = refs[: count], refs[count : -count - 1], refs[-count - 1 : -1]
     sems = refs[-1]
     copies = [pltpu.make_async_copy(source, target, sems.at[i]) for i, (source, target) in enumerate(zip(sources, held))]
@@ -141,12 +148,8 @@
         copy.start()
     for copy in copies:
         copy.wait()
-    top_ref, kernel_ref, gain_row, bias_row, w_in_ref, b_in_row, w_out_ref, scale_row = held
-    cotan_ref, right_ref, left_ref, taps_ref, gain_ref, bias_ref, scale_ref, b_in_ref = outs[:8]
-    w_in_out, w_out_out, w_in_gain_ref, w_out_scale_ref = outs[8:]
-    for row in range(ROWS):
-        cotan_ref[:, block(row)] = top_ref[pl.ds(row, C, stride=ROWS), :]
-    pack_edges(cotan_ref, right_ref, left_ref)
+    kernel_ref, gain_row, bias_row, w_in_ref, b_in_row, w_out_ref, scale_row = held
+    taps_ref, gain_ref, bias_ref, scale_ref, b_in_ref, w_in_out, w_out_out, w_in_gain_ref, w_out_scale_ref = outs
     taps = kernel_ref[:, 0, :].T
     for tap in range(TAPS):
         taps_ref[pl.ds(tap * C, C), :] = jnp.broadcast_to(taps[:, tap : tap + 1], (C, LANES))
@@ -201,7 +204,8 @@
 
 
 def edges(field_ref, left_ref, right_ref, odd_ref, strip_ref, a_ref, b_ref):
-    strip_ref[...] = unfold(left_ref[...], right_ref[...], ACTS_SIDE)
+    wide = pl.ds(0, ACTS_ROWS)
+    strip_ref[...] = unfold(left_ref[wide, :], right_ref[wide, :], ACTS_SIDE)
     write_messages(field_ref, strip_ref, odd_ref, a_ref, b_ref)
 
 
@@ -402,17 +406,10 @@
 USED_ROWS = TAPS_AT + C
 
 
-HALF = PAYLOAD_ROWS // 2
-
-
-def half_of(odd):
-    return pl.ds(pl.multiple_of(odd * HALF, HALF), HALF)
-
-
 def parameter_terms(
     field_ref, strip_ref, a_ref, b_ref, odd_ref, grad_ref, cotan_ref, hidden_ref, normed_ref, grad_pre_ref,
     gain_ref, bias_ref, scale_ref, w_in_ref, w_out_ref,
-    mine_ref, theirs_ref, payload_ref,
+    payload_ref,
 ):
     odd = odd_ref[0] == 1
     lane = lane_of(GROUP)
@@ -455,12 +452,6 @@
         payload_ref[pl.ds(at, C), :] = grad_weights[:, lanes]
         payload_ref[pl.ds(at + C, GROUP), :] = grad_w_in[C:, lanes]
     payload_ref[pl.ds(USED_ROWS, PAYLOAD_ROWS - USED_ROWS), :] = jnp.zeros((PAYLOAD_ROWS - USED_ROWS, LANES), F32)
-    mine_ref[...] = payload_ref[half_of(odd_ref[0]), :]
-    theirs_ref[...] = payload_ref[half_of(1 - odd_ref[0]), :]
-
-
-def add_halves(mine_ref, theirs_ref, a_ref, b_ref, out_ref):
-    out_ref[...] = mine_ref[...] + theirs_ref[...]
 
 
 def sum_shares(shares_ref, out_ref):
@@ -473,12 +464,9 @@
 
 
 def parameter_grads(
-    mine_ref, theirs_ref, odd_ref,
+    payload_ref,
     kernel_out, gain_out, bias_out, w_in_out, b_in_out, w_out_out, scale_out,
-    payload_ref,
 ):
-    payload_ref[half_of(odd_ref[0]), :] = mine_ref[...]
-    payload_ref[half_of(1 - odd_ref[0]), :] = theirs_ref[...]
     by_tap = payload_ref[pl.ds(TAPS_AT, C), :].T
     kernel_out[:, 0, :] = by_tap[:TAPS, :]
     for index, out_ref in enumerate((gain_out, bias_out, scale_out)):
@@ -517,24 +505,11 @@
     return lax.ppermute(to_right, axes, right), lax.ppermute(to_left, axes, left)
 
 
-def swap_pairs(half):
-    return lax.ppermute(half, "ty", [(tile, tile ^ 1) for tile in range(lax.axis_size("ty"))])
-
-
-def sum_over_tiles(mine, theirs, rows):
-    columns = lax.axis_size("tx")
-    tiles = lax.axis_size("ty")
-    groups = [[tile * columns + i for tile in range(odd, tiles, 2) for i in range(columns)] for odd in range(2)]
-    devices = len(groups[0])
-
-    def to_all(shares):
-        return lax.all_to_all(shares, TILES, 0, 0, axis_index_groups=groups)
-
-    (half,) = call(add_halves, [(HALF, LANES)], mine, swap_pairs(theirs), *rows)
-    shares = to_all(half.reshape(devices, HALF // devices, LANES))
+def sum_over_tiles(payload):
+    devices = lax.axis_size(TILES)
+    shares = lax.all_to_all(payload.reshape(devices, PAYLOAD_ROWS // devices, LANES), TILES, 0, 0)
     (copies,) = call(sum_shares, [shares.shape], shares)
-    mine = to_all(copies).reshape(HALF, LANES)
-    return mine, swap_pairs(mine)
+    return lax.all_to_all(copies, TILES, 0, 0).reshape(PAYLOAD_ROWS, LANES)
 
 
 def on_device(acts, top_grad, kernel, ln_gain, ln_bias, w_in, b_in, w_out, layer_scale):
@@ -546,18 +521,18 @@
     edge_outs = [wide, MESSAGE, MESSAGE]
     acts_rows, top_rows = (acts.reshape(C * ROWS, LANES), top_grad.reshape(C * ROWS, LANES))
 
-    acts_side = (C * ACTS_SIDE // LANES, LANES)
-    field, to_right, to_left = call(take_field, [field_shape, acts_side, acts_side], acts_rows)
+    field, cotan, to_right, to_left = call(
+        take_fields, [field_shape, field_shape, SIDE_MESSAGE, SIDE_MESSAGE], acts_rows, top_rows
+    )
     left, right = to_sides(to_right, to_left, every)
     parameters = (
-        top_rows, jnp.transpose(kernel, (1, 0, 2)), ln_gain, ln_bias, w_in[0], b_in, w_out[0].T, layer_scale,
-    )
-    cotan, top_right, top_left, taps, gain, shift_bias, scale, bias_in, weight_in, weight_out, w_in_gain, w_out_scale = call(
+        jnp.transpose(kernel, (1, 0, 2)), ln_gain, ln_bias, w_in[0], b_in, w_out[0].T, layer_scale,
+    )
+    taps, gain, shift_bias, scale, bias_in, weight_in, weight_out, w_in_gain, w_out_scale = call(
         prepare,
-        [field_shape, side, side, (TAPS * C, LANES), (C, 1), (C, 1), (C, 1), (HID, 1), (C, HID), (C, HID), (C, HID), (HID, C)],
+        [(TAPS * C, LANES), (C, 1), (C, 1), (C, 1), (HID, 1), (C, HID), (C, HID), (C, HID), (HID, C)],
         *parameters, scratch=[p.shape for p in parameters] + [pltpu.SemaphoreType.DMA((len(parameters),))], copied=True,
     )
-    top_left, top_right = to_sides(top_right, top_left, (sections - 1,))
     strip, message_a, message_b = call(edges, edge_outs, field, left, right, odd)
     from_a, from_b = swap_rows(message_a, message_b, every)
     (own,) = call(functools.partial(conv_own, False), [field_shape], field, strip, taps, flops=CONV_FLOPS)
@@ -570,7 +545,7 @@
     saved = (normed, inv, slope, w_in_gain, w_out_scale)
 
     cotan = cotan * is_last
-    cotans, lefts, rights = [cotan], [top_left], [top_right]
+    cotans, lefts, rights = [cotan], [left[ACTS_ROWS:] * is_last], [right[ACTS_ROWS:] * is_last]
     for section in reversed(every):
         only = (section,) if section else every
         if section:
@@ -582,10 +557,10 @@
                 functools.partial(last_step, len(cotans)), [field_shape] + edge_outs + [field_shape, hidden_shape],
                 *cotans, *lefts, *rights, odd, *saved, *strips,
             )
-            payload = call(
-                parameter_terms, [(HALF, LANES)] * 2,
+            (payload,) = call(
+                parameter_terms, [(PAYLOAD_ROWS, LANES)],
                 *around, grad, cotan, hidden, normed, grad_pre, gain, shift_bias, scale, weight_in, weight_out,
-                scratch=[(PAYLOAD_ROWS, LANES)], flops=4 * CONV_FLOPS,
+                flops=4 * CONV_FLOPS,
             )
         grad_a, grad_b = swap_rows(message_a, message_b, only)
         (own,) = call(
@@ -598,12 +573,12 @@
             cotans.append(cotan)
             lefts.append(from_left)
             rights.append(from_right)
-    payload = sum_over_tiles(*payload, (grad_a, grad_b))
+    payload = sum_over_tiles(payload)
     (input_grad,) = call(last_finish, [(C * ROWS, LANES)], own, grad_a, grad_b, odd, taps)
     grad_kernel, grad_gain, grad_bias, grad_w_in, grad_b_in, grad_w_out, grad_scale = call(
         parameter_grads,
         [(TAPS, 1, C), (1, C), (1, C), (C, HID), (1, HID), (C, HID), (1, C)],
-        *payload, odd, scratch=[(PAYLOAD_ROWS, LANES)],
+        payload,
     )
     return (
         input_grad.reshape(1, 1, C, ROWS, LANES),

time: 209 us -> 190 us (0.909)
  blocking collectives: 42 us -> 34.7 us
  starting transfers between devices: 37.8 us -> 31.4 us
  local copies, waits for them, and re-layouts: 9.23 us -> 5.65 us
    ppermute x5, starting transfers between devices: 16.7 us -> 8.37 us  [swap_rows(): lax.ppermute(message_b, axes, pairs('ty', sections, True))]
    all_to_all x2 -> x1, blocking collectives: 42 us -> 34.7 us  [sum_over_tiles(): lax.all_to_all(payload.reshape(devices, PAYLOAD_ROWS // devices, LANES),...]
    all_to_all x0 -> x1, starting transfers between devices: none -> 6.19 us  [sum_over_tiles(): return lax.all_to_all(copies, TILES, 0, 0).reshape(PAYLOAD_ROWS, LANES)]
    all_to_all x0 -> x1, waiting for transfers between devices: none -> 4.42 us  [sum_over_tiles(): return lax.all_to_all(copies, TILES, 0, 0).reshape(PAYLOAD_ROWS, LANES)]
    unnamed x28 -> x30, local copies, waits for them, and re-layouts: 9.23 us -> 5.65 us
    ppermute x5 -> x4, waiting for transfers between devices: 57.6 us -> 55.2 us  [to_sides(): lax.ppermute(to_left, axes, left)]
    ppermute x2 -> x0, starting transfers between devices: 2.25 us -> none  [swap_pairs(): lax.ppermute(half, 'ty', [(tile, tile ^ 1) for tile in range(lax.axis_siz...]
    ppermute x5 -> x4, starting transfers between devices: 5.47 us -> 4.09 us  [to_sides(): lax.ppermute(to_left, axes, left)]
  transfers between devices with their start and end apart: 25 -> 22, of which waited for: 3 -> 4; matrix products, arithmetic and copies ran while one was open for 0% -> 0% of each run, Pallas kernels for 13% -> 9%
where the time goes in v6:
time: 190 us
  waiting for transfers between devices  61.8 us (33%)
  Pallas kernels  54.1 us (28%)
  blocking collectives  34.7 us (18%)
  starting transfers between devices  31.4 us (17%)
  local copies, waits for them, and re-layouts  5.65 us (3%)
    ppermute x4, waiting for transfers between devices, to_sides(): lax.ppermute(to_left, axes, left)  55.2 us
    pallas_call x20, Pallas kernels, call(): pl.pallas_call(kernel, out_shape=[jax.ShapeDtypeStruct(shape, F32) for sh...  54.1 us
    all_to_all x1, blocking collectives, sum_over_tiles(): lax.all_to_all(payload.reshape(devices, PAYLOAD_ROWS // devices, LANES),...  34.7 us
    ppermute x5, starting transfers between devices, swap_rows(): lax.ppermute(message_b, axes, pairs('ty', sections, True))  8.37 us
    all_to_all x1, starting transfers between devices, sum_over_tiles(): return lax.all_to_all(copies, TILES, 0, 0).reshape(PAYLOAD_ROWS, LANES)  6.19 us
    ppermute x4, starting transfers between devices, to_sides(): lax.ppermute(to_right, axes, right)  5.92 us
    unnamed x30, local copies, waits for them, and re-layouts  5.65 us
    all_to_all x1, waiting for transfers between devices, sum_over_tiles(): return lax.all_to_all(copies, TILES, 0, 0).reshape(PAYLOAD_ROWS, LANES)  4.42 us
  transfers between devices with their start and end apart: 22, of which 4 were waited for; matrix products, arithmetic and copies ran while one was open for 0% of the time, Pallas kernels for 9%

profile of v6, /device:TPU:1, one launch (start us, length us, event | category | flops | bytes accessed | tf_op | source)
XLA Modules:
  0.0 189.6 jit_solution(11471171210515632072)
XLA Ops:
  3.7 3.9 %collective-permute-start = (f32[72,128]{1,0:T(8,128)}, f32[72,128]{1,0:T(8,128)S(1)}, u32[]{:S(2)}, u32[]{:S(2)}) collective-permute-start(f32[72,128]{1,0:T(8,128)} %get-tuple-element.66), channel_id=1, source_target_pairs={{0,1},{1,2},{2,3},{3,4},{4,5},{5,6},{6,7},{64,65},{65,66},{66,67},... | collective-permute-start | bytes 110600 | tf_op jit(solution)/shard_map/ppermute | solution.py:505
  14.2 1.6 collective-permute-start.2
  15.8 3.1 %collective-permute-start.3 = (f32[384,128]{1,0:T(8,128)S(1)}, f32[384,128]{1,0:T(8,128)S(1)}, u32[]{:S(2)}, u32[]{:S(2)}) collective-permute-start(f32[384,128]{1,0:T(8,128)S(1)} %get-tuple-element.72), channel_id=1, source_target_pairs={{8,16},{16,8},{24,32},{32,24},{40,48},{48,40},{72,80},{80,72},{88,... | collective-permute-start | bytes 589832 | tf_op jit(solution)/shard_map/ppermute | solution.py:496
  18.9 2.6 %shard_map.155.own_ref = f32[96,1024]{1,0:T(8,128)S(1)} custom-call(f32[96,1024]{1,0:T(8,128)S(1)} %get-tuple-element.68.field_ref.refs_0_, f32[96,128]{1,0:T(8,128)S(1)} %get-tuple-element.69.refs_1_.strip_ref, f32[4704,128]{1,0:T(8,128)S(1)} %get-tuple-element.70.refs_2_.taps_ref.refs_3_), custom_call_target="tpu_custom_call" | custom-call | flops 9633792 | tf_op jit(solution)/shard_map/pallas_call | solution.py:36
  22.8 7.8 %shard_map.156 = (f32[96,1024]{1,0:T(8,128)S(1)}, f32[1,1024]{1,0:T(1,128)S(1)}, f32[384,1024]{1,0:T(8,128)S(1)}, f32[384,1024]{1,0:T(8,128)S(1)}, f32[96,128]{1...) custom-call(f32[96,1024]{1,0:T(8,128)S(1)} %get-tuple-element.68.field_ref.refs_0_, ...), custom_call_target="tpu_custom_call" | custom-call | tf_op jit(solution)/shard_map/pallas_call | solution.py:36
  30.6 2.8 %shard_map.157 = (f32[96,1024]{1,0:T(8,128)S(1)}, f32[96,128]{1,0:T(8,128)S(1)}, f32[384,128]{1,0:T(8,128)S(1)}, f32[384,128]{1,0:T(8,128)S(1)}) custom-call(f32[96,1024]{1,0:T(8,128)S(1)} %broadcast_multiply_fusion.cotan_ref.refs_0_, f32[24,128]{1,0:T(8,128)S(1)} %slice_multiply_fusion.1.from_left.refs_4_, ...), custom_call_target="tpu_custom_call" | custom-call | tf_op jit(solution)/shard_map/pallas_call | solution.py:36
  34.8 2.6 %shard_map.158.own_ref = f32[96,1024]{1,0:T(8,128)S(1)} custom-call(f32[96,1024]{1,0:T(8,128)S(1)} %broadcast_multiply_fusion.cotan_ref.refs_0_, f32[96,1024]{1,0:T(8,128)S(1)} %get-tuple-element.85.refs_1_, f32[96,128]{1,0:T(8,128)S(1)} %get-tuple-element.86.refs_2_, f32[4704,128]{1,0:T(8,128)S(1)} %get-tuple-element.70.refs_2_.taps_ref.refs_3_), custom_call_target="tpu_custom_call" | custom-call | flops 9633792 | tf_op jit(solution)/shard_map/pallas_call | solution.py:36
  37.4 2.4 %shard_map.159 = (f32[96,1024]{1,0:T(8,128)S(1)}, f32[24,128]{1,0:T(8,128)S(1)}, f32[24,128]{1,0:T(8,128)S(1)}) custom-call(f32[96,1024]{1,0:T(8,128)S(1)} %shard_map.158.own_ref, f32[384,128]{1,0:T(8,128)S(1)} %collective-permute-done.4.a_ref, f32[384,128]{1,0:T(8,128)S(1)} %collective-permute-done.5.b_ref, s32[1]{0:T(128)} %bitcast.2.odd_ref.refs_12_, ...), custom_call_target="tpu_custom_call" | custom-call | tf_op jit(solution)/shard_map/pallas_call | solution.py:36
  41.9 2.8 %shard_map.160 = (f32[96,1024]{1,0:T(8,128)S(1)}, f32[96,128]{1,0:T(8,128)S(1)}, f32[384,128]{1,0:T(8,128)S(1)}, f32[384,128]{1,0:T(8,128)S(1)}) custom-call(f32[96,1024]{1,0:T(8,128)S(1)} %collective-permute-done.6.cotan_ref.refs_0_.refs_1_, f32[24,128]{1,0:T(8,128)S(1)} %collective-permute-done.7.from_left.refs_5_, ...), custom_call_target="tpu_custom_call" | custom-call | tf_op jit(solution)/shard_map/pallas_call | solution.py:36
  46.1 2.6 %shard_map.161.own_ref = f32[96,1024]{1,0:T(8,128)S(1)} custom-call(f32[96,1024]{1,0:T(8,128)S(1)} %collective-permute-done.6.cotan_ref.refs_0_.refs_1_, f32[96,1024]{1,0:T(8,128)S(1)} %get-tuple-element.92.refs_1_, f32[96,128]{1,0:T(8,128)S(1)} %get-tuple-element.93.refs_2_, f32[4704,128]{1,0:T(8,128)S(1)} %get-tuple-element.70.refs_2_.taps_ref.refs_3_), custom_call_target="tpu_custom_call" | custom-call | flops 9633792 | tf_op jit(solution)/shard_map/pallas_call | solution.py:36
  48.7 2.4 %shard_map.162 = (f32[96,1024]{1,0:T(8,128)S(1)}, f32[24,128]{1,0:T(8,128)S(1)}, f32[24,128]{1,0:T(8,128)S(1)}) custom-call(f32[96,1024]{1,0:T(8,128)S(1)} %shard_map.161.own_ref, f32[384,128]{1,0:T(8,128)S(1)} %collective-permute-done.9.a_ref, f32[384,128]{1,0:T(8,128)S(1)} %collective-permute-done.10.b_ref, s32[1]{0:T(128)} %bitcast.2.odd_ref.refs_12_, ...), custom_call_target="tpu_custom_call" | custom-call | tf_op jit(solution)/shard_map/pallas_call | solution.py:36
  53.2 2.8 %shard_map.163 = (f32[96,1024]{1,0:T(8,128)S(1)}, f32[96,128]{1,0:T(8,128)S(1)}, f32[384,128]{1,0:T(8,128)S(1)}, f32[384,128]{1,0:T(8,128)S(1)}) custom-call(f32[96,1024]{1,0:T(8,128)S(1)} %collective-permute-done.11.cotan_ref.refs_0_.refs_2_, f32[24,128]{1,0:T(8,128)S(1)} %collective-permute-done.12.from_left.refs_6_, ...), custom_call_target="tpu_custom_call" | custom-call | tf_op jit(solution)/shard_map/pallas_call | solution.py:36
  57.4 2.6 %shard_map.164.own_ref = f32[96,1024]{1,0:T(8,128)S(1)} custom-call(f32[96,1024]{1,0:T(8,128)S(1)} %collective-permute-done.11.cotan_ref.refs_0_.refs_2_, f32[96,1024]{1,0:T(8,128)S(1)} %get-tuple-element.99.refs_1_, f32[96,128]{1,0:T(8,128)S(1)} %get-tuple-element.100.refs_2_, f32[4704,128]{1,0:T(8,128)S(1)} %get-tuple-element.70.refs_2_.taps_ref.refs_3_), custom_call_target="tpu_custom_call" | custom-call | flops 9633792 | tf_op jit(solution)/shard_map/pallas_call | solution.py:36
  60.0 2.4 %shard_map.165 = (f32[96,1024]{1,0:T(8,128)S(1)}, f32[24,128]{1,0:T(8,128)S(1)}, f32[24,128]{1,0:T(8,128)S(1)}) custom-call(f32[96,1024]{1,0:T(8,128)S(1)} %shard_map.164.own_ref, f32[384,128]{1,0:T(8,128)S(1)} %collective-permute-done.14.a_ref, f32[384,128]{1,0:T(8,128)S(1)} %collective-permute-done.15.b_ref, s32[1]{0:T(128)} %bitcast.2.odd_ref.refs_12_, ...), custom_call_target="tpu_custom_call" | custom-call | tf_op jit(solution)/shard_map/pallas_call | solution.py:36
  65.9 55.2 %collective-permute-done.18.refs_11_ = f32[24,128]{1,0:T(8,128)S(1)} collective-permute-done((f32[24,128]{1,0:T(8,128)S(1)}, f32[24,128]{1,0:T(8,128)S(1)}, u32[]{:S(2)}, u32[]{:S(2)}) %collective-permute-start.18) | collective-permute-done | bytes 12320 | tf_op jit(solution)/shard_map/ppermute | solution.py:505
  121.1 2.9 %shard_map.166 = (f32[96,1024]{1,0:T(8,128)S(1)}, f32[96,128]{1,0:T(8,128)S(1)}, f32[384,128]{1,0:T(8,128)S(1)}, f32[384,128]{1,0:T(8,128)S(1)}, f32[96,1024]{1,0:T(8,128)S(1)}, /*index=5*/f32[384,1024]{1,0:T(8,128)S(1)}) custom-call(f32[96,1024]{1,0:T(8,128)S(1)} %broadcast_multiply_fusion.cotan_ref.refs_0_, ...), custom_call_target="tpu_custom_call" | custom-call | tf_op jit(solution)/shard_map/pallas_call | solution.py:36
  124.0 6.7 %shard_map.169 = f32[1024,128]{1,0:T(8,128)S(1)} custom-call(f32[96,1024]{1,0:T(8,128)S(1)} %get-tuple-element.68.field_ref.refs_0_, f32[96,128]{1,0:T(8,128)S(1)} %get-tuple-element.69.refs_1_.strip_ref, f32[384,128]{1,0:T(8,128)S(1)} %collective-permute-done.2.a_ref, f32[384,128]{1,0:T(8,128)S(1)} %collective-permute-done.3.b_ref, ...), custom_call_target="tpu_custom_call" | custom-call | flops 38535168 | tf_op jit(solution)/shard_map/pallas_call | solution.py:36
  130.7 34.7 %all_to_all.10.shares_ref = f32[64,16,128]{2,1,0:T(8,128)S(1)} all-to-all(f32[64,16,128]{2,1,0:T(8,128)S(1)} %bitcast.16), channel_id=1, replica_groups=mesh['section'=4,'ty'=8,'tx'=8] {'ty','tx'}, dimensions={0} | all-to-all | bytes 1048576 | tf_op jit(solution)/shard_map/all_to_all | solution.py:510
  166.3 6.2 %all-to-all-start.1 = ((f32[64,16,128]{2,1,0:T(8,128)}), f32[64,16,128]{2,1,0:T(8,128)S(1)}, u32[]{:S(2)}, u32[]{:S(2)}) async-start(f32[64,16,128]{2,1,0:T(8,128)} %shard_map.170), calls=%async_computation.1 | async-start | bytes 1048576 | tf_op jit(solution)/shard_map/all_to_all | solution.py:512
  173.1 3.2 %collective-permute-start.20 = (f32[384,128]{1,0:T(8,128)}, f32[384,128]{1,0:T(8,128)S(1)}, u32[]{:S(2)}, u32[]{:S(2)}) collective-permute-start(f32[384,128]{1,0:T(8,128)} %copy-done.13), channel_id=1, source_target_pairs={{8,16},{16,8},{24,32},{32,24},{40,48},{48,40},{72,80},{80,72},{88,... | collective-permute-start | bytes 589832 | tf_op jit(solution)/shard_map/ppermute | solution.py:496
  177.3 2.6 %shard_map.167.own_ref = f32[96,1024]{1,0:T(8,128)S(1)} custom-call(f32[96,1024]{1,0:T(8,128)S(1)} %copy-done.3, f32[96,1024]{1,0:T(8,128)S(1)} %copy-done.1, f32[96,128]{1,0:T(8,128)S(1)} %get-tuple-element.108.refs_2_, f32[4704,128]{1,0:T(8,128)S(1)} %get-tuple-element.70.refs_2_.taps_ref.refs_3_), custom_call_target="tpu_custom_call" | custom-call | flops 9633792 | tf_op jit(solution)/shard_map/pallas_call | solution.py:36
  179.9 1.6 collective-permute-done.20.b_ref
  181.5 2.9 %shard_map.168 = f32[768,128]{1,0:T(8,128)} custom-call(f32[96,1024]{1,0:T(8,128)S(1)} %shard_map.167.own_ref, f32[384,128]{1,0:T(8,128)S(1)} %collective-permute-done.19.a_ref, f32[384,128]{1,0:T(8,128)S(1)} %collective-permute-done.20.b_ref, s32[1]{0:T(128)} %bitcast.2.odd_ref.refs_12_, f32[4704,128]{1,0:T(8,128)S(1)} %get-tuple-element.70.refs_2_.taps_ref.refs_3_), custom_call_target="tpu_custom_call" | custom-call | tf_op jit(solution)/shard_map/pallas_call | solution.py:36
  184.4 4.4 %all-to-all-done.1 = f32[64,16,128]{2,1,0:T(8,128)S(1)} async-done(((f32[64,16,128]{2,1,0:T(8,128)}), f32[64,16,128]{2,1,0:T(8,128)S(1)}, u32[]{:S(2)}, u32[]{:S(2)}) %all-to-all-start.1) | async-done | bytes 524320 | tf_op jit(solution)/shard_map/all_to_all | solution.py:512
  (74 shorter events, 25.4 us)
Async XLA Ops:
  3.7 9.5 %collective-permute-start = (f32[72,128]{1,0:T(8,128)}, f32[72,128]{1,0:T(8,128)S(1)}, u32[]{:S(2)}, u32[]{:S(2)}) collective-permute-start(f32[72,128]{1,0:T(8,128)} %get-tuple-element.66), channel_id=1, source_target_pairs={{0,1},{1,2},{2,3},{3,4},{4,5},{5,6},{6,7},{64,65},{65,66},{66,67},... | collective-permute-start | bytes 110600 | tf_op jit(solution)/shard_map/ppermute | solution.py:505
  7.7 5.6 %collective-permute-start.1 = (f32[72,128]{1,0:T(8,128)}, f32[72,128]{1,0:T(8,128)}, u32[]{:S(2)}, u32[]{:S(2)}) collective-permute-start(f32[72,128]{1,0:T(8,128)} %get-tuple-element.67), channel_id=1, source_target_pairs={{1,0},{2,1},{3,2},{4,3},{5,4},{6,5},{7,6},{65,64},{66,65},{67,66},... | collective-permute-start | bytes 110600 | tf_op jit(solution)/shard_map/ppermute | solution.py:505
  14.2 8.1 %collective-permute-start.2 = (f32[384,128]{1,0:T(8,128)S(1)}, f32[384,128]{1,0:T(8,128)S(1)}, u32[]{:S(2)}, u32[]{:S(2)}) collective-permute-start(f32[384,128]{1,0:T(8,128)S(1)} %get-tuple-element.71), channel_id=1, source_target_pairs={{0,8},{8,0},{16,24},{24,16},{32,40},{40,32},{48,56},{56,48},{64,72... | collective-permute-start | bytes 589832 | tf_op jit(solution)/shard_map/ppermute | solution.py:495
  15.8 7.0 %collective-permute-start.3 = (f32[384,128]{1,0:T(8,128)S(1)}, f32[384,128]{1,0:T(8,128)S(1)}, u32[]{:S(2)}, u32[]{:S(2)}) collective-permute-start(f32[384,128]{1,0:T(8,128)S(1)} %get-tuple-element.72), channel_id=1, source_target_pairs={{8,16},{16,8},{24,32},{32,24},{40,48},{48,40},{72,80},{80,72},{88,... | collective-permute-start | bytes 589832 | tf_op jit(solution)/shard_map/ppermute | solution.py:496
  33.4 4.0 %collective-permute-start.4 = (f32[384,128]{1,0:T(8,128)S(1)}, f32[384,128]{1,0:T(8,128)S(1)}, u32[]{:S(2)}, u32[]{:S(2)}) collective-permute-start(f32[384,128]{1,0:T(8,128)S(1)} %get-tuple-element.87), channel_id=1, source_target_pairs={{192,200},{200,192},{208,216},{216,208},{224,232},{232,224},{240,2... | collective-permute-start | bytes 589832 | tf_op jit(solution)/shard_map/ppermute | solution.py:495
  34.1 3.3 %collective-permute-start.5 = (f32[384,128]{1,0:T(8,128)S(1)}, f32[384,128]{1,0:T(8,128)S(1)}, u32[]{:S(2)}, u32[]{:S(2)}) collective-permute-start(f32[384,128]{1,0:T(8,128)S(1)} %get-tuple-element.88), channel_id=1, source_target_pairs={{200,208},{208,200},{216,224},{224,216},{232,240},{240,232},{201,2... | collective-permute-start | bytes 589832 | tf_op jit(solution)/shard_map/ppermute | solution.py:496
  39.8 2.1 %collective-permute-start.6 = (f32[96,1024]{1,0:T(8,128)S(1)}, f32[96,1024]{1,0:T(8,128)S(1)}, u32[]{:S(2)}, u32[]{:S(2)}) collective-permute-start(f32[96,1024]{1,0:T(8,128)S(1)} %get-tuple-element.89), channel_id=1, source_target_pairs={{192,128},{193,129},{194,130},{195,131},{196,132},{197,133},{198,1... | collective-permute-start | bytes 1179656 | tf_op jit(solution)/shard_map/ppermute | solution.py:572
  40.5 1.3 collective-permute-start.7
  41.2 0.7 collective-permute-start.8
  44.7 4.0 %collective-permute-start.9 = (f32[384,128]{1,0:T(8,128)S(1)}, f32[384,128]{1,0:T(8,128)S(1)}, u32[]{:S(2)}, u32[]{:S(2)}) collective-permute-start(f32[384,128]{1,0:T(8,128)S(1)} %get-tuple-element.94), channel_id=1, source_target_pairs={{128,136},{136,128},{144,152},{152,144},{160,168},{168,160},{176,1... | collective-permute-start | bytes 589832 | tf_op jit(solution)/shard_map/ppermute | solution.py:495
  45.4 3.3 %collective-permute-start.10 = (f32[384,128]{1,0:T(8,128)S(1)}, f32[384,128]{1,0:T(8,128)S(1)}, u32[]{:S(2)}, u32[]{:S(2)}) collective-permute-start(f32[384,128]{1,0:T(8,128)S(1)} %get-tuple-element.95), channel_id=1, source_target_pairs={{136,144},{144,136},{152,160},{160,152},{168,176},{176,168},{137,1... | collective-permute-start | bytes 589832 | tf_op jit(solution)/shard_map/ppermute | solution.py:496
  51.1 2.1 %collective-permute-start.11 = (f32[96,1024]{1,0:T(8,128)S(1)}, f32[96,1024]{1,0:T(8,128)S(1)}, u32[]{:S(2)}, u32[]{:S(2)}) collective-permute-start(f32[96,1024]{1,0:T(8,128)S(1)} %get-tuple-element.96), channel_id=1, source_target_pairs={{128,64},{129,65},{130,66},{131,67},{132,68},{133,69},{134,70},{13... | collective-permute-start | bytes 1179656 | tf_op jit(solution)/shard_map/ppermute | solution.py:572
  51.8 1.3 collective-permute-start.12
  52.5 0.7 collective-permute-start.13
  56.0 4.0 %collective-permute-start.14 = (f32[384,128]{1,0:T(8,128)S(1)}, f32[384,128]{1,0:T(8,128)S(1)}, u32[]{:S(2)}, u32[]{:S(2)}) collective-permute-start(f32[384,128]{1,0:T(8,128)S(1)} %get-tuple-element.101), channel_id=1, source_target_pairs={{64,72},{72,64},{80,88},{88,80},{96,104},{104,96},{112,120},{120,1... | collective-permute-start | bytes 589832 | tf_op jit(solution)/shard_map/ppermute | solution.py:495
  56.7 3.3 %collective-permute-start.15 = (f32[384,128]{1,0:T(8,128)S(1)}, f32[384,128]{1,0:T(8,128)S(1)}, u32[]{:S(2)}, u32[]{:S(2)}) collective-permute-start(f32[384,128]{1,0:T(8,128)S(1)} %get-tuple-element.102), channel_id=1, source_target_pairs={{72,80},{80,72},{88,96},{96,88},{104,112},{112,104},{73,81},{81,73... | collective-permute-start | bytes 589832 | tf_op jit(solution)/shard_map/ppermute | solution.py:496
  62.4 58.7 %collective-permute-start.16 = (f32[96,1024]{1,0:T(8,128)S(1)}, f32[96,1024]{1,0:T(8,128)S(1)}, u32[]{:S(2)}, u32[]{:S(2)}) collective-permute-start(f32[96,1024]{1,0:T(8,128)S(1)} %get-tuple-element.103), channel_id=1, source_target_pairs={{64,0},{65,1},{66,2},{67,3},{68,4},{69,5},{70,6},{71,7},{72,8},{73... | collective-permute-start | bytes 1179656 | tf_op jit(solution)/shard_map/ppermute | solution.py:572
  63.7 2.2 %collective-permute-start.17 = (f32[24,128]{1,0:T(8,128)S(1)}, f32[24,128]{1,0:T(8,128)S(1)}, u32[]{:S(2)}, u32[]{:S(2)}) collective-permute-start(f32[24,128]{1,0:T(8,128)S(1)} %get-tuple-element.104), channel_id=1, source_target_pairs={{64,1},{65,2},{66,3},{67,4},{68,5},{69,6},{70,7},{72,9},{73,10},{7... | collective-permute-start | bytes 36872 | tf_op jit(solution)/shard_map/ppermute | solution.py:505
  64.4 56.7 %collective-permute-start.18 = (f32[24,128]{1,0:T(8,128)S(1)}, f32[24,128]{1,0:T(8,128)S(1)}, u32[]{:S(2)}, u32[]{:S(2)}) collective-permute-start(f32[24,128]{1,0:T(8,128)S(1)} %get-tuple-element.105), channel_id=1, source_target_pairs={{65,0},{66,1},{67,2},{68,3},{69,4},{70,5},{71,6},{73,8},{74,9},{75... | collective-permute-start | bytes 36872 | tf_op jit(solution)/shard_map/ppermute | solution.py:505
  124.0 41.5 %copy-start.13 = (f32[384,128]{1,0:T(8,128)}, f32[384,128]{1,0:T(8,128)S(1)}, u32[]{:S(2)}) copy-start(f32[384,128]{1,0:T(8,128)S(1)} %get-tuple-element.110) | copy-start | bytes 589828
  130.7 45.6 %copy-start.1 = (f32[96,1024]{1,0:T(8,128)S(1)}, f32[96,1024]{1,0:T(8,128)}, u32[]{:S(2)}) copy-start(f32[96,1024]{1,0:T(8,128)} %copy-done) | copy-start | bytes 1179652
  166.3 22.5 %all-to-all-start.1 = ((f32[64,16,128]{2,1,0:T(8,128)}), f32[64,16,128]{2,1,0:T(8,128)S(1)}, u32[]{:S(2)}, u32[]{:S(2)}) async-start(f32[64,16,128]{2,1,0:T(8,128)} %shard_map.170), calls=%async_computation.1 | async-start | bytes 1048576 | tf_op jit(solution)/shard_map/all_to_all | solution.py:512
  172.5 7.4 %collective-permute-start.19 = (f32[384,128]{1,0:T(8,128)}, f32[384,128]{1,0:T(8,128)S(1)}, u32[]{:S(2)}, u32[]{:S(2)}) collective-permute-start(f32[384,128]{1,0:T(8,128)} %copy-done.14), channel_id=1, source_target_pairs={{0,8},{8,0},{16,24},{24,16},{32,40},{40,32},{48,56},{56,48},{64,72... | collective-permute-start | bytes 589832 | tf_op jit(solution)/shard_map/ppermute | solution.py:495
  173.1 8.4 %collective-permute-start.20 = (f32[384,128]{1,0:T(8,128)}, f32[384,128]{1,0:T(8,128)S(1)}, u32[]{:S(2)}, u32[]{:S(2)}) collective-permute-start(f32[384,128]{1,0:T(8,128)} %copy-done.13), channel_id=1, source_target_pairs={{8,16},{16,8},{24,32},{32,24},{40,48},{48,40},{72,80},{80,72},{88,... | collective-permute-start | bytes 589832 | tf_op jit(solution)/shard_map/ppermute | solution.py:496
  (13 other events, 79.8 us)

commit v7 on v6

--- a/solution.py
+++ b/solution.py
@@ -279,9 +279,11 @@
             parts = ((row, LANES - REACH, start, REACH), (strip, ACTS_SIDE + ACTS_REACH * index, start + REACH, ACTS_REACH))
         for value, origin, to, width in parts:
             packed = jnp.where((lane >= to) & (lane < to + width), roll(value, to - origin), packed)
-    total = jnp.zeros((GROUP, LANES), F32)
-    for tap in range(TAPS):
-        total = total + tap_of(taps_ref, tap, group) * roll(packed, -(SPAN * (tap // KS) + tap % KS))
+    sums = [jnp.zeros((GROUP, LANES), F32)] * KS
+    for a in range(KS):
+        for b in range(KS):
+            sums[b] = sums[b] + tap_of(taps_ref, a * KS + b, group) * roll(packed, -(SPAN * a + b))
+    total = (sums[0] + sums[1]) + (sums[2] + sums[3]) + ((sums[4] + sums[5]) + sums[6])
     result = jnp.zeros((GROUP, LANES), F32)
     for row in range(ROWS):
         to = SIDE * side + REACH * row

time: 190 us -> 190 us (level)
  no operation moved by 1% of the time
where the time goes in v7:
time: 190 us
  waiting for transfers between devices  61.8 us (33%)
  Pallas kernels  54.1 us (28%)
  blocking collectives  34.7 us (18%)
  starting transfers between devices  31.4 us (17%)
  local copies, waits for them, and re-layouts  5.65 us (3%)
    ppermute x4, waiting for transfers between devices, to_sides(): lax.ppermute(to_left, axes, left)  55.2 us
    pallas_call x20, Pallas kernels, call(): pl.pallas_call(kernel, out_shape=[jax.ShapeDtypeStruct(shape, F32) for sh...  54.1 us
    all_to_all x1, blocking collectives, sum_over_tiles(): lax.all_to_all(payload.reshape(devices, PAYLOAD_ROWS // devices, LANES),...  34.7 us
    ppermute x5, starting transfers between devices, swap_rows(): lax.ppermute(message_b, axes, pairs('ty', sections, True))  8.37 us
    all_to_all x1, starting transfers between devices, sum_over_tiles(): return lax.all_to_all(copies, TILES, 0, 0).reshape(PAYLOAD_ROWS, LANES)  6.19 us
    ppermute x4, starting transfers between devices, to_sides(): lax.ppermute(to_right, axes, right)  5.92 us
    unnamed x30, local copies, waits for them, and re-layouts  5.65 us
    all_to_all x1, waiting for transfers between devices, sum_over_tiles(): return lax.all_to_all(copies, TILES, 0, 0).reshape(PAYLOAD_ROWS, LANES)  4.42 us
  transfers between devices with their start and end apart: 22, of which 4 were waited for; matrix products, arithmetic and copies ran while one was open for 0% of the time, Pallas kernels for 9%

profile of v7, /device:TPU:1, one launch (start us, length us, event | category | flops | bytes accessed | tf_op | source)
XLA Modules:
  0.0 189.6 jit_solution(12507141423149285692)
XLA Ops:
  3.7 3.9 %collective-permute-start = (f32[72,128]{1,0:T(8,128)}, f32[72,128]{1,0:T(8,128)S(1)}, u32[]{:S(2)}, u32[]{:S(2)}) collective-permute-start(f32[72,128]{1,0:T(8,128)} %get-tuple-element.66), channel_id=1, source_target_pairs={{0,1},{1,2},{2,3},{3,4},{4,5},{5,6},{6,7},{64,65},{65,66},{66,67},... | collective-permute-start | bytes 110600 | tf_op jit(solution)/shard_map/ppermute | solution.py:507
  14.2 1.6 collective-permute-start.2
  15.8 3.1 %collective-permute-start.3 = (f32[384,128]{1,0:T(8,128)S(1)}, f32[384,128]{1,0:T(8,128)S(1)}, u32[]{:S(2)}, u32[]{:S(2)}) collective-permute-start(f32[384,128]{1,0:T(8,128)S(1)} %get-tuple-element.72), channel_id=1, source_target_pairs={{8,16},{16,8},{24,32},{32,24},{40,48},{48,40},{72,80},{80,72},{88,... | collective-permute-start | bytes 589832 | tf_op jit(solution)/shard_map/ppermute | solution.py:498
  18.9 2.6 %shard_map.155.own_ref = f32[96,1024]{1,0:T(8,128)S(1)} custom-call(f32[96,1024]{1,0:T(8,128)S(1)} %get-tuple-element.68.field_ref.refs_0_, f32[96,128]{1,0:T(8,128)S(1)} %get-tuple-element.69.refs_1_.strip_ref, f32[4704,128]{1,0:T(8,128)S(1)} %get-tuple-element.70.refs_2_.taps_ref.refs_3_), custom_call_target="tpu_custom_call" | custom-call | flops 9633792 | tf_op jit(solution)/shard_map/pallas_call | solution.py:36
  22.8 7.9 %shard_map.156 = (f32[96,1024]{1,0:T(8,128)S(1)}, f32[1,1024]{1,0:T(1,128)S(1)}, f32[384,1024]{1,0:T(8,128)S(1)}, f32[384,1024]{1,0:T(8,128)S(1)}, f32[96,128]{1...) custom-call(f32[96,1024]{1,0:T(8,128)S(1)} %get-tuple-element.68.field_ref.refs_0_, ...), custom_call_target="tpu_custom_call" | custom-call | tf_op jit(solution)/shard_map/pallas_call | solution.py:36
  30.7 2.8 %shard_map.157 = (f32[96,1024]{1,0:T(8,128)S(1)}, f32[96,128]{1,0:T(8,128)S(1)}, f32[384,128]{1,0:T(8,128)S(1)}, f32[384,128]{1,0:T(8,128)S(1)}) custom-call(f32[96,1024]{1,0:T(8,128)S(1)} %broadcast_multiply_fusion.cotan_ref.refs_0_, f32[24,128]{1,0:T(8,128)S(1)} %slice_multiply_fusion.1.from_left.refs_4_, ...), custom_call_target="tpu_custom_call" | custom-call | tf_op jit(solution)/shard_map/pallas_call | solution.py:36
  34.9 2.6 %shard_map.158.own_ref = f32[96,1024]{1,0:T(8,128)S(1)} custom-call(f32[96,1024]{1,0:T(8,128)S(1)} %broadcast_multiply_fusion.cotan_ref.refs_0_, f32[96,1024]{1,0:T(8,128)S(1)} %get-tuple-element.85.refs_1_, f32[96,128]{1,0:T(8,128)S(1)} %get-tuple-element.86.refs_2_, f32[4704,128]{1,0:T(8,128)S(1)} %get-tuple-element.70.refs_2_.taps_ref.refs_3_), custom_call_target="tpu_custom_call" | custom-call | flops 9633792 | tf_op jit(solution)/shard_map/pallas_call | solution.py:36
  37.5 2.4 %shard_map.159 = (f32[96,1024]{1,0:T(8,128)S(1)}, f32[24,128]{1,0:T(8,128)S(1)}, f32[24,128]{1,0:T(8,128)S(1)}) custom-call(f32[96,1024]{1,0:T(8,128)S(1)} %shard_map.158.own_ref, f32[384,128]{1,0:T(8,128)S(1)} %collective-permute-done.4.a_ref, f32[384,128]{1,0:T(8,128)S(1)} %collective-permute-done.5.b_ref, s32[1]{0:T(128)} %bitcast.2.odd_ref.refs_12_, ...), custom_call_target="tpu_custom_call" | custom-call | tf_op jit(solution)/shard_map/pallas_call | solution.py:36
  42.0 2.8 %shard_map.160 = (f32[96,1024]{1,0:T(8,128)S(1)}, f32[96,128]{1,0:T(8,128)S(1)}, f32[384,128]{1,0:T(8,128)S(1)}, f32[384,128]{1,0:T(8,128)S(1)}) custom-call(f32[96,1024]{1,0:T(8,128)S(1)} %collective-permute-done.6.cotan_ref.refs_0_.refs_1_, f32[24,128]{1,0:T(8,128)S(1)} %collective-permute-done.7.from_left.refs_5_, ...), custom_call_target="tpu_custom_call" | custom-call | tf_op jit(solution)/shard_map/pallas_call | solution.py:36
  46.2 2.6 %shard_map.161.own_ref = f32[96,1024]{1,0:T(8,128)S(1)} custom-call(f32[96,1024]{1,0:T(8,128)S(1)} %collective-permute-done.6.cotan_ref.refs_0_.refs_1_, f32[96,1024]{1,0:T(8,128)S(1)} %get-tuple-element.92.refs_1_, f32[96,128]{1,0:T(8,128)S(1)} %get-tuple-element.93.refs_2_, f32[4704,128]{1,0:T(8,128)S(1)} %get-tuple-element.70.refs_2_.taps_ref.refs_3_), custom_call_target="tpu_custom_call" | custom-call | flops 9633792 | tf_op jit(solution)/shard_map/pallas_call | solution.py:36
  48.8 2.4 %shard_map.162 = (f32[96,1024]{1,0:T(8,128)S(1)}, f32[24,128]{1,0:T(8,128)S(1)}, f32[24,128]{1,0:T(8,128)S(1)}) custom-call(f32[96,1024]{1,0:T(8,128)S(1)} %shard_map.161.own_ref, f32[384,128]{1,0:T(8,128)S(1)} %collective-permute-done.9.a_ref, f32[384,128]{1,0:T(8,128)S(1)} %collective-permute-done.10.b_ref, s32[1]{0:T(128)} %bitcast.2.odd_ref.refs_12_, ...), custom_call_target="tpu_custom_call" | custom-call | tf_op jit(solution)/shard_map/pallas_call | solution.py:36
  53.3 2.8 %shard_map.163 = (f32[96,1024]{1,0:T(8,128)S(1)}, f32[96,128]{1,0:T(8,128)S(1)}, f32[384,128]{1,0:T(8,128)S(1)}, f32[384,128]{1,0:T(8,128)S(1)}) custom-call(f32[96,1024]{1,0:T(8,128)S(1)} %collective-permute-done.11.cotan_ref.refs_0_.refs_2_, f32[24,128]{1,0:T(8,128)S(1)} %collective-permute-done.12.from_left.refs_6_, ...), custom_call_target="tpu_custom_call" | custom-call | tf_op jit(solution)/shard_map/pallas_call | solution.py:36
  57.5 2.6 %shard_map.164.own_ref = f32[96,1024]{1,0:T(8,128)S(1)} custom-call(f32[96,1024]{1,0:T(8,128)S(1)} %collective-permute-done.11.cotan_ref.refs_0_.refs_2_, f32[96,1024]{1,0:T(8,128)S(1)} %get-tuple-element.99.refs_1_, f32[96,128]{1,0:T(8,128)S(1)} %get-tuple-element.100.refs_2_, f32[4704,128]{1,0:T(8,128)S(1)} %get-tuple-element.70.refs_2_.taps_ref.refs_3_), custom_call_target="tpu_custom_call" | custom-call | flops 9633792 | tf_op jit(solution)/shard_map/pallas_call | solution.py:36
  60.1 2.4 %shard_map.165 = (f32[96,1024]{1,0:T(8,128)S(1)}, f32[24,128]{1,0:T(8,128)S(1)}, f32[24,128]{1,0:T(8,128)S(1)}) custom-call(f32[96,1024]{1,0:T(8,128)S(1)} %shard_map.164.own_ref, f32[384,128]{1,0:T(8,128)S(1)} %collective-permute-done.14.a_ref, f32[384,128]{1,0:T(8,128)S(1)} %collective-permute-done.15.b_ref, s32[1]{0:T(128)} %bitcast.2.odd_ref.refs_12_, ...), custom_call_target="tpu_custom_call" | custom-call | tf_op jit(solution)/shard_map/pallas_call | solution.py:36
  66.0 55.2 %collective-permute-done.18.refs_11_ = f32[24,128]{1,0:T(8,128)S(1)} collective-permute-done((f32[24,128]{1,0:T(8,128)S(1)}, f32[24,128]{1,0:T(8,128)S(1)}, u32[]{:S(2)}, u32[]{:S(2)}) %collective-permute-start.18) | collective-permute-done | bytes 12320 | tf_op jit(solution)/shard_map/ppermute | solution.py:507
  121.2 2.9 %shard_map.166 = (f32[96,1024]{1,0:T(8,128)S(1)}, f32[96,128]{1,0:T(8,128)S(1)}, f32[384,128]{1,0:T(8,128)S(1)}, f32[384,128]{1,0:T(8,128)S(1)}, f32[96,1024]{1,0:T(8,128)S(1)}, /*index=5*/f32[384,1024]{1,0:T(8,128)S(1)}) custom-call(f32[96,1024]{1,0:T(8,128)S(1)} %broadcast_multiply_fusion.cotan_ref.refs_0_, ...), custom_call_target="tpu_custom_call" | custom-call | tf_op jit(solution)/shard_map/pallas_call | solution.py:36
  124.1 6.7 %shard_map.169 = f32[1024,128]{1,0:T(8,128)S(1)} custom-call(f32[96,1024]{1,0:T(8,128)S(1)} %get-tuple-element.68.field_ref.refs_0_, f32[96,128]{1,0:T(8,128)S(1)} %get-tuple-element.69.refs_1_.strip_ref, f32[384,128]{1,0:T(8,128)S(1)} %collective-permute-done.2.a_ref, f32[384,128]{1,0:T(8,128)S(1)} %collective-permute-done.3.b_ref, ...), custom_call_target="tpu_custom_call" | custom-call | flops 38535168 | tf_op jit(solution)/shard_map/pallas_call | solution.py:36
  130.8 34.7 %all_to_all.10.shares_ref = f32[64,16,128]{2,1,0:T(8,128)S(1)} all-to-all(f32[64,16,128]{2,1,0:T(8,128)S(1)} %bitcast.16), channel_id=1, replica_groups=mesh['section'=4,'ty'=8,'tx'=8] {'ty','tx'}, dimensions={0} | all-to-all | bytes 1048576 | tf_op jit(solution)/shard_map/all_to_all | solution.py:512
  166.4 6.2 %all-to-all-start.1 = ((f32[64,16,128]{2,1,0:T(8,128)}), f32[64,16,128]{2,1,0:T(8,128)S(1)}, u32[]{:S(2)}, u32[]{:S(2)}) async-start(f32[64,16,128]{2,1,0:T(8,128)} %shard_map.170), calls=%async_computation.1 | async-start | bytes 1048576 | tf_op jit(solution)/shard_map/all_to_all | solution.py:514
  173.1 3.2 %collective-permute-start.20 = (f32[384,128]{1,0:T(8,128)}, f32[384,128]{1,0:T(8,128)S(1)}, u32[]{:S(2)}, u32[]{:S(2)}) collective-permute-start(f32[384,128]{1,0:T(8,128)} %copy-done.13), channel_id=1, source_target_pairs={{8,16},{16,8},{24,32},{32,24},{40,48},{48,40},{72,80},{80,72},{88,... | collective-permute-start | bytes 589832 | tf_op jit(solution)/shard_map/ppermute | solution.py:498
  177.4 2.6 %shard_map.167.own_ref = f32[96,1024]{1,0:T(8,128)S(1)} custom-call(f32[96,1024]{1,0:T(8,128)S(1)} %copy-done.3, f32[96,1024]{1,0:T(8,128)S(1)} %copy-done.1, f32[96,128]{1,0:T(8,128)S(1)} %get-tuple-element.108.refs_2_, f32[4704,128]{1,0:T(8,128)S(1)} %get-tuple-element.70.refs_2_.taps_ref.refs_3_), custom_call_target="tpu_custom_call" | custom-call | flops 9633792 | tf_op jit(solution)/shard_map/pallas_call | solution.py:36
  180.0 1.6 collective-permute-done.20.b_ref
  181.6 2.9 %shard_map.168 = f32[768,128]{1,0:T(8,128)} custom-call(f32[96,1024]{1,0:T(8,128)S(1)} %shard_map.167.own_ref, f32[384,128]{1,0:T(8,128)S(1)} %collective-permute-done.19.a_ref, f32[384,128]{1,0:T(8,128)S(1)} %collective-permute-done.20.b_ref, s32[1]{0:T(128)} %bitcast.2.odd_ref.refs_12_, f32[4704,128]{1,0:T(8,128)S(1)} %get-tuple-element.70.refs_2_.taps_ref.refs_3_), custom_call_target="tpu_custom_call" | custom-call | tf_op jit(solution)/shard_map/pallas_call | solution.py:36
  184.5 4.4 %all-to-all-done.1 = f32[64,16,128]{2,1,0:T(8,128)S(1)} async-done(((f32[64,16,128]{2,1,0:T(8,128)}), f32[64,16,128]{2,1,0:T(8,128)S(1)}, u32[]{:S(2)}, u32[]{:S(2)}) %all-to-all-start.1) | async-done | bytes 524320 | tf_op jit(solution)/shard_map/all_to_all | solution.py:514
  (74 shorter events, 25.4 us)
Async XLA Ops:
  3.7 9.5 %collective-permute-start = (f32[72,128]{1,0:T(8,128)}, f32[72,128]{1,0:T(8,128)S(1)}, u32[]{:S(2)}, u32[]{:S(2)}) collective-permute-start(f32[72,128]{1,0:T(8,128)} %get-tuple-element.66), channel_id=1, source_target_pairs={{0,1},{1,2},{2,3},{3,4},{4,5},{5,6},{6,7},{64,65},{65,66},{66,67},... | collective-permute-start | bytes 110600 | tf_op jit(solution)/shard_map/ppermute | solution.py:507
  7.7 5.6 %collective-permute-start.1 = (f32[72,128]{1,0:T(8,128)}, f32[72,128]{1,0:T(8,128)}, u32[]{:S(2)}, u32[]{:S(2)}) collective-permute-start(f32[72,128]{1,0:T(8,128)} %get-tuple-element.67), channel_id=1, source_target_pairs={{1,0},{2,1},{3,2},{4,3},{5,4},{6,5},{7,6},{65,64},{66,65},{67,66},... | collective-permute-start | bytes 110600 | tf_op jit(solution)/shard_map/ppermute | solution.py:507
  14.2 8.1 %collective-permute-start.2 = (f32[384,128]{1,0:T(8,128)S(1)}, f32[384,128]{1,0:T(8,128)S(1)}, u32[]{:S(2)}, u32[]{:S(2)}) collective-permute-start(f32[384,128]{1,0:T(8,128)S(1)} %get-tuple-element.71), channel_id=1, source_target_pairs={{0,8},{8,0},{16,24},{24,16},{32,40},{40,32},{48,56},{56,48},{64,72... | collective-permute-start | bytes 589832 | tf_op jit(solution)/shard_map/ppermute | solution.py:497
  15.8 7.0 %collective-permute-start.3 = (f32[384,128]{1,0:T(8,128)S(1)}, f32[384,128]{1,0:T(8,128)S(1)}, u32[]{:S(2)}, u32[]{:S(2)}) collective-permute-start(f32[384,128]{1,0:T(8,128)S(1)} %get-tuple-element.72), channel_id=1, source_target_pairs={{8,16},{16,8},{24,32},{32,24},{40,48},{48,40},{72,80},{80,72},{88,... | collective-permute-start | bytes 589832 | tf_op jit(solution)/shard_map/ppermute | solution.py:498
  33.5 4.0 %collective-permute-start.4 = (f32[384,128]{1,0:T(8,128)S(1)}, f32[384,128]{1,0:T(8,128)S(1)}, u32[]{:S(2)}, u32[]{:S(2)}) collective-permute-start(f32[384,128]{1,0:T(8,128)S(1)} %get-tuple-element.87), channel_id=1, source_target_pairs={{192,200},{200,192},{208,216},{216,208},{224,232},{232,224},{240,2... | collective-permute-start | bytes 589832 | tf_op jit(solution)/shard_map/ppermute | solution.py:497
  34.2 3.3 %collective-permute-start.5 = (f32[384,128]{1,0:T(8,128)S(1)}, f32[384,128]{1,0:T(8,128)S(1)}, u32[]{:S(2)}, u32[]{:S(2)}) collective-permute-start(f32[384,128]{1,0:T(8,128)S(1)} %get-tuple-element.88), channel_id=1, source_target_pairs={{200,208},{208,200},{216,224},{224,216},{232,240},{240,232},{201,2... | collective-permute-start | bytes 589832 | tf_op jit(solution)/shard_map/ppermute | solution.py:498
  39.9 2.1 %collective-permute-start.6 = (f32[96,1024]{1,0:T(8,128)S(1)}, f32[96,1024]{1,0:T(8,128)S(1)}, u32[]{:S(2)}, u32[]{:S(2)}) collective-permute-start(f32[96,1024]{1,0:T(8,128)S(1)} %get-tuple-element.89), channel_id=1, source_target_pairs={{192,128},{193,129},{194,130},{195,131},{196,132},{197,133},{198,1... | collective-permute-start | bytes 1179656 | tf_op jit(solution)/shard_map/ppermute | solution.py:574
  40.6 1.3 collective-permute-start.7
  41.3 0.7 collective-permute-start.8
  44.8 4.0 %collective-permute-start.9 = (f32[384,128]{1,0:T(8,128)S(1)}, f32[384,128]{1,0:T(8,128)S(1)}, u32[]{:S(2)}, u32[]{:S(2)}) collective-permute-start(f32[384,128]{1,0:T(8,128)S(1)} %get-tuple-element.94), channel_id=1, source_target_pairs={{128,136},{136,128},{144,152},{152,144},{160,168},{168,160},{176,1... | collective-permute-start | bytes 589832 | tf_op jit(solution)/shard_map/ppermute | solution.py:497
  45.5 3.3 %collective-permute-start.10 = (f32[384,128]{1,0:T(8,128)S(1)}, f32[384,128]{1,0:T(8,128)S(1)}, u32[]{:S(2)}, u32[]{:S(2)}) collective-permute-start(f32[384,128]{1,0:T(8,128)S(1)} %get-tuple-element.95), channel_id=1, source_target_pairs={{136,144},{144,136},{152,160},{160,152},{168,176},{176,168},{137,1... | collective-permute-start | bytes 589832 | tf_op jit(solution)/shard_map/ppermute | solution.py:498
  51.2 2.1 %collective-permute-start.11 = (f32[96,1024]{1,0:T(8,128)S(1)}, f32[96,1024]{1,0:T(8,128)S(1)}, u32[]{:S(2)}, u32[]{:S(2)}) collective-permute-start(f32[96,1024]{1,0:T(8,128)S(1)} %get-tuple-element.96), channel_id=1, source_target_pairs={{128,64},{129,65},{130,66},{131,67},{132,68},{133,69},{134,70},{13... | collective-permute-start | bytes 1179656 | tf_op jit(solution)/shard_map/ppermute | solution.py:574
  51.9 1.3 collective-permute-start.12
  52.6 0.7 collective-permute-start.13
  56.1 4.0 %collective-permute-start.14 = (f32[384,128]{1,0:T(8,128)S(1)}, f32[384,128]{1,0:T(8,128)S(1)}, u32[]{:S(2)}, u32[]{:S(2)}) collective-permute-start(f32[384,128]{1,0:T(8,128)S(1)} %get-tuple-element.101), channel_id=1, source_target_pairs={{64,72},{72,64},{80,88},{88,80},{96,104},{104,96},{112,120},{120,1... | collective-permute-start | bytes 589832 | tf_op jit(solution)/shard_map/ppermute | solution.py:497
  56.8 3.3 %collective-permute-start.15 = (f32[384,128]{1,0:T(8,128)S(1)}, f32[384,128]{1,0:T(8,128)S(1)}, u32[]{:S(2)}, u32[]{:S(2)}) collective-permute-start(f32[384,128]{1,0:T(8,128)S(1)} %get-tuple-element.102), channel_id=1, source_target_pairs={{72,80},{80,72},{88,96},{96,88},{104,112},{112,104},{73,81},{81,73... | collective-permute-start | bytes 589832 | tf_op jit(solution)/shard_map/ppermute | solution.py:498
  62.5 58.7 %collective-permute-start.16 = (f32[96,1024]{1,0:T(8,128)S(1)}, f32[96,1024]{1,0:T(8,128)S(1)}, u32[]{:S(2)}, u32[]{:S(2)}) collective-permute-start(f32[96,1024]{1,0:T(8,128)S(1)} %get-tuple-element.103), channel_id=1, source_target_pairs={{64,0},{65,1},{66,2},{67,3},{68,4},{69,5},{70,6},{71,7},{72,8},{73... | collective-permute-start | bytes 1179656 | tf_op jit(solution)/shard_map/ppermute | solution.py:574
  63.8 2.2 %collective-permute-start.17 = (f32[24,128]{1,0:T(8,128)S(1)}, f32[24,128]{1,0:T(8,128)S(1)}, u32[]{:S(2)}, u32[]{:S(2)}) collective-permute-start(f32[24,128]{1,0:T(8,128)S(1)} %get-tuple-element.104), channel_id=1, source_target_pairs={{64,1},{65,2},{66,3},{67,4},{68,5},{69,6},{70,7},{72,9},{73,10},{7... | collective-permute-start | bytes 36872 | tf_op jit(solution)/shard_map/ppermute | solution.py:507
  64.5 56.7 %collective-permute-start.18 = (f32[24,128]{1,0:T(8,128)S(1)}, f32[24,128]{1,0:T(8,128)S(1)}, u32[]{:S(2)}, u32[]{:S(2)}) collective-permute-start(f32[24,128]{1,0:T(8,128)S(1)} %get-tuple-element.105), channel_id=1, source_target_pairs={{65,0},{66,1},{67,2},{68,3},{69,4},{70,5},{71,6},{73,8},{74,9},{75... | collective-permute-start | bytes 36872 | tf_op jit(solution)/shard_map/ppermute | solution.py:507
  124.1 41.5 %copy-start.13 = (f32[384,128]{1,0:T(8,128)}, f32[384,128]{1,0:T(8,128)S(1)}, u32[]{:S(2)}) copy-start(f32[384,128]{1,0:T(8,128)S(1)} %get-tuple-element.110) | copy-start | bytes 589828
  130.8 45.6 %copy-start.1 = (f32[96,1024]{1,0:T(8,128)S(1)}, f32[96,1024]{1,0:T(8,128)}, u32[]{:S(2)}) copy-start(f32[96,1024]{1,0:T(8,128)} %copy-done) | copy-start | bytes 1179652
  166.4 22.5 %all-to-all-start.1 = ((f32[64,16,128]{2,1,0:T(8,128)}), f32[64,16,128]{2,1,0:T(8,128)S(1)}, u32[]{:S(2)}, u32[]{:S(2)}) async-start(f32[64,16,128]{2,1,0:T(8,128)} %shard_map.170), calls=%async_computation.1 | async-start | bytes 1048576 | tf_op jit(solution)/shard_map/all_to_all | solution.py:514
  172.6 7.4 %collective-permute-start.19 = (f32[384,128]{1,0:T(8,128)}, f32[384,128]{1,0:T(8,128)S(1)}, u32[]{:S(2)}, u32[]{:S(2)}) collective-permute-start(f32[384,128]{1,0:T(8,128)} %copy-done.14), channel_id=1, source_target_pairs={{0,8},{8,0},{16,24},{24,16},{32,40},{40,32},{48,56},{56,48},{64,72... | collective-permute-start | bytes 589832 | tf_op jit(solution)/shard_map/ppermute | solution.py:497
  173.1 8.4 %collective-permute-start.20 = (f32[384,128]{1,0:T(8,128)}, f32[384,128]{1,0:T(8,128)S(1)}, u32[]{:S(2)}, u32[]{:S(2)}) collective-permute-start(f32[384,128]{1,0:T(8,128)} %copy-done.13), channel_id=1, source_target_pairs={{8,16},{16,8},{24,32},{32,24},{40,48},{48,40},{72,80},{80,72},{88,... | collective-permute-start | bytes 589832 | tf_op jit(solution)/shard_map/ppermute | solution.py:498
  (13 other events, 79.8 us)
